TPU v7x, 128 devices: a whole 4x4x4 slice. The times are simulated.
128 devices in a mesh: gx: 8 (over z, core), gy: 16 (over x, y).
Axes of the slice: x: 4, y: 4, z: 4, core: 2. Of those that a mesh axis runs over, the one named last changes fastest.
Arguments:
- ensemble: bfloat16 [10, 90, 128, 4096], P(None, None, 'gx', 'gy'), may hold values from -6 to 6
- vertical_weights: float32 [90, 90], replicated, may hold values from 0 to 1
- dual_vector: float32 [262144], P(('gx', 'gy')), may hold values from -48 to 48
- observed_column: int32 [262144], P(('gx', 'gy')), may hold values from 0 to 524287, as said below
- observed_level: int32 [262144], P(('gx', 'gy')), may hold values from 0 to 89
- active_count: int32 [128], P(('gx', 'gy')), may hold values from 1024 to 2048, as said below
Outputs:
- increment: float32 [90, 128, 4096], P(None, 'gx', 'gy')
- obs_product: float32 [262144], P(('gx', 'gy'))
Inputs may be any that keep to these rules, and one draw needn't show every extreme that they name: `active_count`: some device has all 2048 slots active. `observed_column`: over the active slots of one device, at most 48 columns lie in any one device's tile (16 rows by 256 columns); in every draw one tile receives exactly 48 from every device.
All inputs are finite; a program needn't handle non-finite values.
Results may differ from a plain program's by a relative error of at most 0.0003.
Values sent between devices are 32-bit elements; how exact they have to be, the bound alone decides.
No kernel may reach another device: no remote copies, remote signals or barrier semaphores. Data moves between devices by JAX's collectives and lax.ppermute only.
A program may use at most 640 MiB of HBM per device.

v0:
```python
import jax
import jax.numpy as jnp
from jax import lax
from jax.sharding import PartitionSpec as P

DIFF_STEPS = 3


diffusivity = 0.24


def extended(array, sides, width):
    for axis, dim in sides:
        size, length = (lax.axis_size(axis), array.shape[dim])
        up = [(i, (i + 1) % size) for i in range(size - 1)]
        down = [(j, i) for i, j in up]
        last = lax.slice_in_dim(array, length - width, length, axis=dim)
        first = lax.slice_in_dim(array, 0, width, axis=dim)
        before = lax.ppermute(last, axis, up)
        after = lax.ppermute(first, axis, down)
        array = jnp.concatenate([before, array, after], axis=dim)
    return array


def diffuse_once(padded):
    centre = padded[:, :, 1:-1, 1:-1]
    beside_all = (
        padded[:, :, 2:, 1:-1]
        + padded[:, :, :-2, 1:-1]
        + padded[:, :, 1:-1, 2:]
        + padded[:, :, 1:-1, :-2]
    )
    return centre + diffusivity * (beside_all - 4.0 * centre)


def vertical_mix(vertical_weights, spread):

    def one_member(field):
        return jnp.tensordot(
            vertical_weights, field, axes=((1,), (0,)), precision=lax.Precision.HIGHEST
        )

    return lax.map(one_member, spread)


def body(ensemble, vertical_weights, dual_vector, observed_column, observed_level, active_count):
    members, levels, tile_rows, tile_cols = ensemble.shape
    mesh_rows = lax.axis_size("gx")
    mesh_cols = lax.axis_size("gy")
    devices = mesh_rows * mesh_cols
    slot_count = dual_vector.shape[0]
    capacity = 3 * slot_count // devices
    total_cols = tile_cols * mesh_cols
    active = jnp.arange(slot_count, dtype=jnp.int32) < active_count[0]
    global_row = observed_column // total_cols
    global_col = observed_column % total_cols
    target = global_row // tile_rows * mesh_cols + global_col // tile_cols
    cell_index = (
        observed_level * (tile_rows * tile_cols)
        + global_row % tile_rows * tile_cols
        + global_col % tile_cols
    )
    one_hot = (
        (target[:, None] == jnp.arange(devices, dtype=jnp.int32)[None, :]) & active[:, None]
    ).astype(jnp.int32)
    seat_rank = jnp.sum(jnp.cumsum(one_hot, axis=0) * one_hot, axis=1) - 1
    position = jnp.where(active, target * capacity + seat_rank, devices * capacity)
    outgoing = jnp.zeros((2, devices * capacity), jnp.float32)
    outgoing = outgoing.at[0, position].set(dual_vector, mode="drop")
    outgoing = outgoing.at[1, position].set(cell_index.astype(jnp.float32), mode="drop")
    incoming = lax.all_to_all(outgoing, ("gx", "gy"), split_axis=1, concat_axis=1, tiled=True)
    amounts = incoming[0]
    cell_slots = incoming[1].astype(jnp.int32)
    level_slot = cell_slots // (tile_rows * tile_cols)
    row_slot = cell_slots // tile_cols % tile_rows
    col_slot = cell_slots % tile_cols
    adjoint = (
        jnp.zeros((levels, tile_rows, tile_cols), jnp.float32)
        .at[level_slot, row_slot, col_slot]
        .add(amounts)
    )
    spread = ensemble.astype(jnp.float32) * adjoint[None]
    vertical = vertical_mix(vertical_weights, spread)
    diffused = vertical
    for repeat in range(DIFF_STEPS):
        diffused = diffuse_once(extended(diffused, (("gx", 2), ("gy", 3)), 1))
    increment = jnp.sum(ensemble.astype(jnp.float32) * diffused, axis=0) / (members - 1)
    picked = increment[level_slot, row_slot, col_slot]
    returned = lax.all_to_all(picked, ("gx", "gy"), split_axis=0, concat_axis=0, tiled=True)
    obs_product = jnp.where(active, returned[jnp.minimum(position, devices * capacity - 1)], 0.0)
    return (increment, obs_product)


def solution(mesh):
    placed = (
        P(None, None, "gx", "gy"),
        P(),
        P(("gx", "gy")),
        P(("gx", "gy")),
        P(("gx", "gy")),
        P(("gx", "gy")),
    )
    return jax.shard_map(
        body,
        mesh=mesh,
        in_specs=placed,
        out_specs=(P(None, "gx", "gy"), P(("gx", "gy"))),
        check_vma=False,
    )
```

profile of v0, /device:TPU:1, one launch (start us, length us, event | category | flops | bytes accessed | tf_op | source)
XLA Modules:
  0.0 520.0 jit_solution(8077230773236381017)
XLA Ops:
  6.1 8.2 %scatter_custom_fusion = f32[12288]{0:T(1024)S(1)} fusion(s32[2048]{0:T(1024)S(1)} %get-tuple-element.61, f32[2048]{0:T(1024)} %param.10, f32[]{:T(128)} %constant.125.clone.1), kind=kCustom, calls=%fused_computation.104 | custom fusion | bytes 49664
  14.3 8.1 %scatter_fusion = f32[12288]{0:T(1024)S(1)} fusion(f32[12288]{0:T(1024)S(1)} %scatter_custom_fusion, s32[2048]{0:T(1024)S(1)} %get-tuple-element.62, f32[2048]{0:T(1024)S(1)} %get-tuple-element.59), kind=kCustom, calls=%fused_computation.3 | custom fusion | bytes 32768
  23.3 11.5 %all-to-all-start = ((f32[2,128,48]{2,0,1:T(2,128)}), f32[2,128,48]{2,0,1:T(2,128)S(1)}, u32[]{:S(2)}, u32[]{:S(2)}) async-start(f32[2,128,48]{2,0,1:T(2,128)} %copy.16), calls=%async_computation | async-start | bytes 262144 | tf_op jit(solution)/shard_map/all_to_all | solution.py:71
  34.8 14.7 %copy.13 = bf16[10,90,16,256]{1,3,2,0:T(8,128)(2,1)} copy(bf16[10,90,16,256]{3,2,1,0:T(8,128)(2,1)} %param.8) | data formatting | bytes 14745600 | tf_op args[0]
  51.0 38.8 %scatter_custom_fusion.2 = f32[368640]{0:T(1024)S(1)} fusion(s32[6144]{0:T(1024)S(1)} %broadcast_select_fusion, f32[6144]{0:T(1024)S(1)} %reshape.257, f32[]{:T(128)} %constant.125.clone.1), kind=kCustom, calls=%fused_computation.64 | custom fusion | flops 6144 | bytes 1474564
  93.2 12.1 %convert_multiply_fusion.1 = f32[10,90,16,256]{1,3,2,0:T(8,128)} fusion(bf16[10,90,16,256]{1,3,2,0:T(8,128)(2,1)} %copy.13, f32[90,16,256]{0,2,1:T(8,128)S(1)} %copy.17), kind=kLoop, calls=%fused_computation.12 | loop fusion | flops 7372800 | bytes 23592960 | tf_op jit(solution)/shard_map/mul | solution.py:82
  105.2 20.7 %copy.18 = f32[10,90,16,256]{3,1,2,0:T(8,128)} copy(f32[10,90,16,256]{1,3,2,0:T(8,128)} %convert_multiply_fusion.1) | data formatting | bytes 29491200 | tf_op jit(solution)/shard_map/while | solution.py:43
  126.0 40.8 %while.10 = (s32[]{:T(128)}, f32[10,90,16,256]{3,1,2,0:T(8,128)}, f32[10,90,16,256]{3,1,2,0:T(8,128)}, f32[90,90]{1,0:T(8,128)S(1)}, s32[]{:T(128)}) while((s32[]{:T(128)}, f32[10,90,16,256]{3,1,2,0:T(8,128)}, f32[10,90,16,256]{3,1,2,0:T(8,128)}, f32[90,90]{1,0:T(8,128)S(1)}, s32[]{:T(128)}) %tuple.40), condition=%wide.region_7.8_spmd, body=%wide.region_6.7_spmd.sunk | while | flops 398131200 | bytes 3179213 | solution.py:43
  126.0 4.1 bitcast_dynamic-update-slice_fusion.2
  138.2 4.1 bitcast_dynamic-update-slice_fusion.2
  142.3 4.1 bitcast_dynamic-update-slice_fusion.2
  158.7 4.1 bitcast_dynamic-update-slice_fusion.2
  176.0 19.0 %copy.29 = f32[10,90,16,256]{1,3,2,0:T(8,128)} copy(f32[10,90,16,256]{3,1,2,0:T(8,128)} %get-tuple-element.24) | data formatting | bytes 29491200 | tf_op jit(solution)/shard_map/while | solution.py:43
  207.2 46.4 %fusion.23 = f32[10,90,16,256]{1,3,2,0:T(8,128)} fusion(f32[10,90,16,256]{1,3,2,0:T(8,128)} %copy.29, f32[10,90,18,1]{1,3,2,0:T(1,128)S(1)} %collective-permute-done.3, f32[10,90,1,256]{1,3,2,0:T(8,128)S(1)} %copy.21, f32[10,90,1,256]{1,3,2,0:T(8,128)S(1)} %copy.23, f32[10,90,18,1]{1,3,2,0:T(1,128)S(1)} %collective-permute-done.2), kind=kLoop, calls=%fused_computation.46 | loop fusion | flops 55296000 | bytes 31464000 | tf_op jit(solution)/shard_map/add | solution.py:33
  264.9 8.2 %collective-permute-done.4 = f32[10,90,1,256]{3,2,1,0:T(1,128)S(1)} collective-permute-done((f32[10,90,1,256]{3,2,1,0:T(1,128)}, f32[10,90,1,256]{3,2,1,0:T(1,128)S(1)}, u32[]{:S(2)}, u32[]{:S(2)}) %collective-permute-start.4) | collective-permute-done | bytes 921632 | tf_op jit(solution)/shard_map/ppermute | solution.py:20
  280.6 5.0 collective-permute-start.7
  286.9 46.1 %fusion.17 = f32[10,90,16,256]{1,3,2,0:T(8,128)} fusion(f32[10,90,16,256]{1,3,2,0:T(8,128)} %fusion.23, f32[10,90,18,1]{1,3,2,0:T(1,128)S(1)} %collective-permute-done.7, f32[10,90,1,256]{1,3,2,0:T(8,128)S(1)} %copy.31, f32[10,90,1,256]{1,3,2,0:T(8,128)S(1)} %copy.33, f32[10,90,18,1]{1,3,2,0:T(1,128)S(1)} %collective-permute-done.6), kind=kLoop, calls=%fused_computation.32 | loop fusion | flops 55296000 | bytes 31464000 | tf_op jit(solution)/shard_map/add | solution.py:33
  339.9 5.3 %collective-permute-start.9 = (f32[10,90,1,256]{3,2,1,0:T(1,128)S(1)}, f32[10,90,1,256]{3,2,1,0:T(1,128)}, u32[]{:S(2)}, u32[]{:S(2)}) collective-permute-start(f32[10,90,1,256]{3,2,1,0:T(1,128)S(1)} %copy.38), channel_id=1, source_target_pairs={{0,16},{16,32},{32,48},{48,64},{64,80},{80,96},{96,112},{1,17},{17... | collective-permute-start | bytes 2764808 | tf_op jit(solution)/shard_map/ppermute | solution.py:19
  345.3 8.5 %collective-permute-done.8 = f32[10,90,1,256]{3,2,1,0:T(1,128)S(1)} collective-permute-done((f32[10,90,1,256]{3,2,1,0:T(1,128)}, f32[10,90,1,256]{3,2,1,0:T(1,128)S(1)}, u32[]{:S(2)}, u32[]{:S(2)}) %collective-permute-start.8) | collective-permute-done | bytes 921632 | tf_op jit(solution)/shard_map/ppermute | solution.py:20
  360.9 4.7 collective-permute-start.11
  367.1 47.8 %fusion.7 = f32[90,16,256]{0,2,1:T(8,128)} fusion(bf16[10,90,16,256]{1,3,2,0:T(8,128)(2,1)} %copy.13, f32[10,90,16,256]{1,3,2,0:T(8,128)} %fusion.17, f32[10,90,18,1]{1,3,2,0:T(1,128)S(1)} %collective-permute-done.11, f32[10,90,1,256]{1,3,2,0:T(8,128)S(1)} %copy.37, f32[10,90,1,256]{1,3,2,0:T(8,128)S(1)} %copy.39, ...), kind=kLoop, calls=%fused_computation.13 | loop fusion | flops 65986560 | bytes 25565760 | tf_op jit(solution)/shard_map/reduce_sum | solution.py:87
  417.3 60.7 %gather_fusion = f32[6144]{0:T(1024)S(1)} fusion(f32[90,16,256]{2,1,0:T(8,128)S(1)} %broadcast_multiply_fusion, s32[6144]{0:T(1024)S(1)} %bitcast.36), kind=kCustom, calls=%fused_computation | custom fusion | bytes 122880 | tf_op jit(solution)/shard_map/gather | solution.py:88
  478.1 28.1 %all_to_all.21 = f32[128,48,1]{1,2,0:T(1,128)S(1)} all-to-all(f32[128,48,1]{1,2,0:T(1,128)S(1)} %bitcast.37), channel_id=1, replica_groups=mesh['gx'=8,'gy'=16] {'gx','gy'}, dimensions={0} | all-to-all | bytes 49152 | tf_op jit(solution)/shard_map/all_to_all | solution.py:89
  507.6 11.8 %gather_fusion.1 = f32[2048]{0:T(1024)S(1)} fusion(f32[6144]{0:T(1024)S(1)} %all_to_all.18, s32[2048]{0:T(1024)S(1)} %get-tuple-element.57), kind=kCustom, calls=%fused_computation.1 | custom fusion | bytes 24576 | tf_op jit(solution)/shard_map/gather | solution.py:90
  (87 shorter events, 96.0 us)
Async XLA Ops:
  2.2 48.2 %copy-start.3 = (s32[3]{0:T(128)S(1)}, s32[3]{0:T(128)}, u32[]{:S(2)}) copy-start(s32[3]{0:T(128)} %constant.162) | copy-start | bytes 40
  2.2 48.3 %copy-start.2 = (s32[3]{0:T(128)S(1)}, s32[3]{0:T(128)}, u32[]{:S(2)}) copy-start(s32[3]{0:T(128)} %constant.165) | copy-start | bytes 40
  23.3 26.3 %all-to-all-start = ((f32[2,128,48]{2,0,1:T(2,128)}), f32[2,128,48]{2,0,1:T(2,128)S(1)}, u32[]{:S(2)}, u32[]{:S(2)}) async-start(f32[2,128,48]{2,0,1:T(2,128)} %copy.16), calls=%async_computation | async-start | bytes 262144 | tf_op jit(solution)/shard_map/all_to_all | solution.py:71
  105.2 20.7 %copy-start.1 = (f32[90,90]{1,0:T(8,128)S(1)}, f32[90,90]{1,0:T(8,128)}, u32[]{:S(2)}) copy-start(f32[90,90]{1,0:T(8,128)} %param.9) | copy-start | bytes 97204
  169.5 25.5 %collective-permute-start = (f32[10,90,1,256]{3,2,1,0:T(1,128)S(1)}, f32[10,90,1,256]{3,2,1,0:T(1,128)S(1)}, u32[]{:S(2)}, u32[]{:S(2)}) collective-permute-start(f32[10,90,1,256]{3,2,1,0:T(1,128)S(1)} %copy.19), channel_id=1, source_target_pairs={{16,0},{32,16},{48,32},{64,48},{80,64},{96,80},{112,96},{17,1},{33... | collective-permute-start | bytes 2764808 | tf_op jit(solution)/shard_map/ppermute | solution.py:20
  173.4 23.0 %collective-permute-start.1 = (f32[10,90,1,256]{3,2,1,0:T(1,128)S(1)}, f32[10,90,1,256]{3,2,1,0:T(1,128)}, u32[]{:S(2)}, u32[]{:S(2)}) collective-permute-start(f32[10,90,1,256]{3,2,1,0:T(1,128)S(1)} %copy.22), channel_id=1, source_target_pairs={{0,16},{16,32},{32,48},{48,64},{64,80},{80,96},{96,112},{1,17},{17... | collective-permute-start | bytes 2764808 | tf_op jit(solution)/shard_map/ppermute | solution.py:19
  200.4 5.3 %collective-permute-start.2 = (f32[10,90,18,1]{1,3,2,0:T(1,128)S(1)}, f32[10,90,18,1]{1,3,2,0:T(1,128)S(1)}, u32[]{:S(2)}, u32[]{:S(2)}) collective-permute-start(f32[10,90,18,1]{1,3,2,0:T(1,128)S(1)} %get-tuple-element.49), channel_id=1, source_target_pairs={{1,0},{2,1},{3,2},{4,3},{5,4},{6,5},{7,6},{8,7},{9,8},{10,9},{11,1... | collective-permute-start | bytes 194408 | tf_op jit(solution)/shard_map/ppermute | solution.py:20
  201.7 5.6 %collective-permute-start.3 = (f32[10,90,18,1]{1,3,2,0:T(1,128)S(1)}, f32[10,90,18,1]{1,3,2,0:T(1,128)S(1)}, u32[]{:S(2)}, u32[]{:S(2)}) collective-permute-start(f32[10,90,18,1]{1,3,2,0:T(1,128)S(1)} %get-tuple-element.50), channel_id=1, source_target_pairs={{0,1},{1,2},{2,3},{3,4},{4,5},{5,6},{6,7},{7,8},{8,9},{9,10},{10,1... | collective-permute-start | bytes 194408 | tf_op jit(solution)/shard_map/ppermute | solution.py:19
  257.6 15.6 %collective-permute-start.4 = (f32[10,90,1,256]{3,2,1,0:T(1,128)}, f32[10,90,1,256]{3,2,1,0:T(1,128)S(1)}, u32[]{:S(2)}, u32[]{:S(2)}) collective-permute-start(f32[10,90,1,256]{3,2,1,0:T(1,128)} %copy.30), channel_id=1, source_target_pairs={{16,0},{32,16},{48,32},{64,48},{80,64},{96,80},{112,96},{17,1},{33... | collective-permute-start | bytes 2764808 | tf_op jit(solution)/shard_map/ppermute | solution.py:20
  262.5 12.8 %collective-permute-start.5 = (f32[10,90,1,256]{3,2,1,0:T(1,128)S(1)}, f32[10,90,1,256]{3,2,1,0:T(1,128)}, u32[]{:S(2)}, u32[]{:S(2)}) collective-permute-start(f32[10,90,1,256]{3,2,1,0:T(1,128)S(1)} %copy.32), channel_id=1, source_target_pairs={{0,16},{16,32},{32,48},{48,64},{64,80},{80,96},{96,112},{1,17},{17... | collective-permute-start | bytes 2764808 | tf_op jit(solution)/shard_map/ppermute | solution.py:19
  279.3 6.3 %collective-permute-start.6 = (f32[10,90,18,1]{1,3,2,0:T(1,128)S(1)}, f32[10,90,18,1]{1,3,2,0:T(1,128)S(1)}, u32[]{:S(2)}, u32[]{:S(2)}) collective-permute-start(f32[10,90,18,1]{1,3,2,0:T(1,128)S(1)} %get-tuple-element.47), channel_id=1, source_target_pairs={{1,0},{2,1},{3,2},{4,3},{5,4},{6,5},{7,6},{8,7},{9,8},{10,9},{11,1... | collective-permute-start | bytes 194408 | tf_op jit(solution)/shard_map/ppermute | solution.py:20
  280.6 6.3 %collective-permute-start.7 = (f32[10,90,18,1]{1,3,2,0:T(1,128)S(1)}, f32[10,90,18,1]{1,3,2,0:T(1,128)S(1)}, u32[]{:S(2)}, u32[]{:S(2)}) collective-permute-start(f32[10,90,18,1]{1,3,2,0:T(1,128)S(1)} %get-tuple-element.48), channel_id=1, source_target_pairs={{0,1},{1,2},{2,3},{3,4},{4,5},{5,6},{6,7},{7,8},{8,9},{9,10},{10,1... | collective-permute-start | bytes 194408 | tf_op jit(solution)/shard_map/ppermute | solution.py:19
  336.9 17.0 %collective-permute-start.8 = (f32[10,90,1,256]{3,2,1,0:T(1,128)}, f32[10,90,1,256]{3,2,1,0:T(1,128)S(1)}, u32[]{:S(2)}, u32[]{:S(2)}) collective-permute-start(f32[10,90,1,256]{3,2,1,0:T(1,128)} %copy.36), channel_id=1, source_target_pairs={{16,0},{32,16},{48,32},{64,48},{80,64},{96,80},{112,96},{17,1},{33... | collective-permute-start | bytes 2764808 | tf_op jit(solution)/shard_map/ppermute | solution.py:20
  339.9 15.7 %collective-permute-start.9 = (f32[10,90,1,256]{3,2,1,0:T(1,128)S(1)}, f32[10,90,1,256]{3,2,1,0:T(1,128)}, u32[]{:S(2)}, u32[]{:S(2)}) collective-permute-start(f32[10,90,1,256]{3,2,1,0:T(1,128)S(1)} %copy.38), channel_id=1, source_target_pairs={{0,16},{16,32},{32,48},{48,64},{64,80},{80,96},{96,112},{1,17},{17... | collective-permute-start | bytes 2764808 | tf_op jit(solution)/shard_map/ppermute | solution.py:19
  359.6 6.0 %collective-permute-start.10 = (f32[10,90,18,1]{1,3,2,0:T(1,128)S(1)}, f32[10,90,18,1]{1,3,2,0:T(1,128)S(1)}, u32[]{:S(2)}, u32[]{:S(2)}) collective-permute-start(f32[10,90,18,1]{1,3,2,0:T(1,128)S(1)} %get-tuple-element.45), channel_id=1, source_target_pairs={{1,0},{2,1},{3,2},{4,3},{5,4},{6,5},{7,6},{8,7},{9,8},{10,9},{11,1... | collective-permute-start | bytes 194408 | tf_op jit(solution)/shard_map/ppermute | solution.py:20
  360.9 6.2 %collective-permute-start.11 = (f32[10,90,18,1]{1,3,2,0:T(1,128)S(1)}, f32[10,90,18,1]{1,3,2,0:T(1,128)S(1)}, u32[]{:S(2)}, u32[]{:S(2)}) collective-permute-start(f32[10,90,18,1]{1,3,2,0:T(1,128)S(1)} %get-tuple-element.46), channel_id=1, source_target_pairs={{0,1},{1,2},{2,3},{3,4},{4,5},{5,6},{6,7},{7,8},{8,9},{9,10},{10,1... | collective-permute-start | bytes 194408 | tf_op jit(solution)/shard_map/ppermute | solution.py:19
  417.3 102.8 %copy-start = (f32[90,16,256]{2,1,0:T(8,128)}, f32[90,16,256]{2,1,0:T(8,128)S(1)}, u32[]{:S(2)}) copy-start(f32[90,16,256]{2,1,0:T(8,128)S(1)} %broadcast_multiply_fusion) | copy-start | bytes 4423684
where the time goes:
time: 522 us; the launch traced here: 520 us
  other arithmetic  202 us (39%)
  local copies, waits for them, and re-layouts  176 us (34%)
  starting transfers between devices  48 us (9%)
  matrix products  40.8 us (8%)
  blocking collectives  28.1 us (5%)
  waiting for transfers between devices  22.4 us (4%)
    add x2, other arithmetic, diffuse_once(): return centre + diffusivity * (beside_all - 4.0 * centre)  92.5 us
    gather x1, local copies, waits for them, and re-layouts, body(): picked = increment[level_slot, row_slot, col_slot]  60.7 us
    reduce_sum x1, other arithmetic, body(): jnp.sum(ensemble.astype(jnp.float32) * diffused, axis=0) / (members - 1)  47.8 us
    dot_general x10, matrix products, one_member(): jnp.tensordot(vertical_weights, field, axes=((1,), (0,)), precision=lax.P...  40.8 us
    unnamed x7, other arithmetic  40.7 us
    while x2, local copies, waits for them, and re-layouts, vertical_mix(): return lax.map(one_member, spread)  39.7 us
    unnamed x11, local copies, waits for them, and re-layouts  31.1 us
    all_to_all x1, blocking collectives, body(): lax.all_to_all(picked, ('gx', 'gy'), split_axis=0, concat_axis=0, tiled=T...  28.1 us
  transfers between devices with their start and end apart: 13, of which 7 were waited for; matrix products, arithmetic and copies ran while one was open for 8% of the time, Pallas kernels for 0%

commit v1 on v0

v1 whole, which is shorter than its diff:
```python
import jax
import jax.numpy as jnp
import numpy as np
from jax import lax
from jax.experimental import pallas as pl
from jax.experimental.pallas import tpu as pltpu
from jax.sharding import PartitionSpec as P

F32 = jnp.float32
BF16 = jnp.bfloat16
I32 = jnp.int32

MEM, LEV, ROWS, COLS = 10, 90, 16, 256
PAD = 96
DEV = 128
CAP = 48
SLOTS = 2048
HALF = 128
EDGE = 3
STRIP = 18
PER_HALF = 5
SELF = 1.0 / 6.0
SCALE = 0.24**3 / (MEM - 1)
VMEM = 56 * 1024 * 1024


def split(value, count):
    parts = []
    for _ in range(count - 1):
        top = value.astype(BF16)
        parts.append(top)
        value = value - top.astype(F32)
    parts.append(value.astype(BF16))
    return parts


def dot(a, b):
    return lax.dot_general(a, b, (((1,), (0,)), ((), ())), preferred_element_type=F32)


def dot_nt(a, b):
    return lax.dot_general(a, b, (((1,), (1,)), ((), ())), preferred_element_type=F32)


def iota(shape, dim):
    return lax.broadcasted_iota(I32, shape, dim)


def one_hot(test):
    return jnp.where(test, 1.0, 0.0).astype(BF16)


def params(**kw):
    return pltpu.CompilerParams(vmem_limit_bytes=VMEM, **kw)


def cost(flops, moved):
    return pl.CostEstimate(flops=flops, bytes_accessed=moved, transcendentals=0)


def pack_kernel(count, dual, col, lev, upper, out, tgt_out, rank_out, left_v, left_c, right_v, right_c):
    number = count[0]
    rows = iota((DEV, HALF), 0)
    lane = iota((1, HALF), 1)
    carry = jnp.zeros((DEV, HALF), F32)
    for i in range(SLOTS // HALF):
        at = slice(i * HALF, (i + 1) * HALF)
        column = col[i : i + 1, :]
        row = column >> 12
        gcol = column & 4095
        y = gcol & 255
        y = ((y & 1) << 7) + (y >> 1)
        target = ((row >> 4) << 4) + (gcol >> 8)
        target = jnp.where(i * HALF + lane < number, target, -1)
        hit = rows == target
        both = dot(one_hot(hit), upper[...])
        rank = jnp.sum(jnp.where(hit, both[:, :HALF] + carry, 0.0), axis=0, keepdims=True)
        carry = carry + both[:, HALF:]
        tgt_out[i : i + 1, :] = target
        rank = rank.astype(I32)
        rank_out[i : i + 1, :] = rank
        right_v[:, at] = one_hot(rows == rank)
        right_c[:, at] = one_hot(rows == rank + CAP)
        values = dual[i : i + 1, :]
        for p, piece in enumerate(split(values, 3)):
            left_v[p * DEV : (p + 1) * DEV, at] = jnp.where(hit, piece.astype(F32), 0.0).astype(BF16)
        cells = (lev[i : i + 1, :] << 12, (row & 15) << 8, y)
        for p, piece in enumerate(cells):
            left_c[p * DEV : (p + 1) * DEV, at] = jnp.where(hit, piece.astype(F32), 0.0).astype(BF16)
    a = dot_nt(left_v[...], right_v[...])
    b = dot_nt(left_c[...], right_c[...])
    out[...] = ((a[:DEV] + a[DEV : 2 * DEV]) + a[2 * DEV :]) + ((b[:DEV] + b[DEV : 2 * DEV]) + b[2 * DEV :])


def pack(count, dual, col, lev):
    upper = np.concatenate([np.triu(np.ones((HALF, HALF)), 1), np.ones((HALF, HALF))], 1)
    spec = pl.BlockSpec(memory_space=pltpu.VMEM)
    return pl.pallas_call(
        pack_kernel,
        name="pack",
        out_shape=(
            jax.ShapeDtypeStruct((DEV, HALF), F32),
            jax.ShapeDtypeStruct((SLOTS // HALF, HALF), I32),
            jax.ShapeDtypeStruct((SLOTS // HALF, HALF), I32),
        ),
        in_specs=[pl.BlockSpec(memory_space=pltpu.SMEM)] + [spec] * 4,
        out_specs=(spec,) * 3,
        scratch_shapes=[pltpu.VMEM((3 * DEV, SLOTS), BF16)] * 2 + [pltpu.VMEM((DEV, SLOTS), BF16)] * 2,
        compiler_params=params(),
        cost_estimate=cost(10**9, 10**6),
    )(count, dual.reshape(-1, HALF), col.reshape(-1, HALF), lev.reshape(-1, HALF), jnp.asarray(upper, BF16))


def unpack_kernel(back, tgt, rank, out):
    rows = iota((DEV, HALF), 0)
    table = jnp.concatenate(split(back[...], 3), axis=0)
    for i in range(SLOTS // HALF):
        found = dot(table, one_hot(rows == rank[i : i + 1, :]))
        found = (found[:DEV] + found[DEV : 2 * DEV]) + found[2 * DEV :]
        out[i : i + 1, :] = jnp.sum(jnp.where(rows == tgt[i : i + 1, :], found, 0.0), axis=0, keepdims=True)


def unpack(back, tgt, rank):
    spec = pl.BlockSpec(memory_space=pltpu.VMEM)
    return pl.pallas_call(
        unpack_kernel,
        name="unpack",
        out_shape=jax.ShapeDtypeStruct((SLOTS // HALF, HALF), F32),
        in_specs=[spec] * 3,
        out_specs=spec,
        compiler_params=params(),
        cost_estimate=cost(10**8, 10**5),
    )(back, tgt, rank).reshape(SLOTS)


def strip_lane(member):
    return member // PER_HALF * HALF + member % PER_HALF * STRIP


def natural(permuted):
    return ((permuted & 127) << 1) + (permuted >> 7)


def arrange_kernel(ens, perm_y, perm_r, out, up, down, strip, side, strip_acc, side_acc):
    k = pl.program_id(0)

    @pl.when(k == 0)
    def _():
        strip_acc[...] = jnp.zeros_like(strip_acc)
        side_acc[...] = jnp.zeros_like(side_acc)

    base = k // PER_HALF * HALF + k % PER_HALF * STRIP
    y = natural(iota((COLS, COLS), 0))
    lane = iota((COLS, COLS), 1)
    want = jnp.where(y < 6, base + 3 + y, jnp.where(y >= 250, base + y - 241, -1))
    select = one_hot(lane == want)
    want = jnp.where(y < 3, 3 * k + y, jnp.where(y >= 253, HALF + 3 * k + y - 253, -1))
    select = jnp.concatenate([select, one_hot(lane == want)], axis=1)
    for b in range(6):
        if b < 5:
            block = ens[0, b * 256 : (b + 1) * 256, :]
        else:
            block = jnp.concatenate([ens[0, 1280:1440, :], jnp.zeros((96, COLS), BF16)], axis=0)
        block = dot(block, perm_y[...]).astype(BF16)
        turned = dot(perm_r[...], block)
        edges = dot(turned.astype(BF16), select)
        at = slice(b * 16, (b + 1) * 16)
        for x in range(ROWS):
            part = turned[x * 16 : (x + 1) * 16, :]
            out[0, x, at, :] = part.astype(BF16)
            if x < EDGE:
                up[0, x, at, :] = part
            if x >= ROWS - EDGE:
                down[0, x - (ROWS - EDGE), at, :] = part
            strip_acc[x, at, :] += edges[x * 16 : (x + 1) * 16, :COLS]
            side_acc[x, at, :] += edges[x * 16 : (x + 1) * 16, COLS:]

    @pl.when(k == MEM - 1)
    def _():
        strip[...] = strip_acc[...].astype(BF16)
        side[0] = side_acc[:, :, :HALF]
        side[1] = side_acc[:, :, HALF:]


def arrange(ensemble):
    y = np.arange(COLS)
    perm_y = np.zeros((COLS, COLS))
    perm_y[y, (y % 2) * HALF + y // 2] = 1
    perm_r = np.zeros((256, 256))
    i = np.arange(256)
    perm_r[i % 16 * 16 + i // 16, i] = 1
    whole = pl.BlockSpec((256, 256), lambda k: (0, 0))
    return pl.pallas_call(
        arrange_kernel,
        name="arrange",
        grid=(MEM,),
        out_shape=(
            jax.ShapeDtypeStruct((MEM, ROWS, PAD, COLS), BF16),
            jax.ShapeDtypeStruct((MEM, EDGE, PAD, COLS), F32),
            jax.ShapeDtypeStruct((MEM, EDGE, PAD, COLS), F32),
            jax.ShapeDtypeStruct((ROWS, PAD, COLS), BF16),
            jax.ShapeDtypeStruct((2, ROWS, PAD, HALF), F32),
        ),
        in_specs=[pl.BlockSpec((1, LEV * ROWS, COLS), lambda k: (k, 0, 0)), whole, whole],
        out_specs=(
            pl.BlockSpec((1, ROWS, PAD, COLS), lambda k: (k, 0, 0, 0)),
            pl.BlockSpec((1, EDGE, PAD, COLS), lambda k: (k, 0, 0, 0)),
            pl.BlockSpec((1, EDGE, PAD, COLS), lambda k: (k, 0, 0, 0)),
            pl.BlockSpec((ROWS, PAD, COLS), lambda k: (0, 0, 0)),
            pl.BlockSpec((2, ROWS, PAD, HALF), lambda k: (0, 0, 0, 0)),
        ),
        scratch_shapes=[pltpu.VMEM((ROWS, PAD, COLS), F32)] * 2,
        compiler_params=params(),
        cost_estimate=cost(10**10, 25 * 10**6),
    )(ensemble.reshape(MEM, LEV * ROWS, COLS), jnp.asarray(perm_y, BF16), jnp.asarray(perm_r, BF16))


def strip_kernel(strip, left, right, out, up, down):
    from_lane = iota((HALF, COLS), 0)
    k, c = from_lane // 3, from_lane % 3
    base = k // PER_HALF * HALF + k % PER_HALF * STRIP
    lane = iota((HALF, COLS), 1)
    good = from_lane < 3 * MEM
    place_l = one_hot((lane == base + c) & good)
    place_r = one_hot((lane == base + 15 + c) & good)
    for x in range(ROWS):
        value = strip[x].astype(F32) + dot(left[0, x].astype(BF16), place_l) + dot(right[0, x].astype(BF16), place_r)
        out[x] = value.astype(BF16)
        if x < EDGE:
            up[x] = value
        if x >= ROWS - EDGE:
            down[x - (ROWS - EDGE)] = value


def complete_strip(strip, left, right):
    spec = pl.BlockSpec(memory_space=pltpu.VMEM)
    return pl.pallas_call(
        strip_kernel,
        name="complete_strip",
        out_shape=(
            jax.ShapeDtypeStruct((ROWS, PAD, COLS), BF16),
            jax.ShapeDtypeStruct((EDGE, PAD, COLS), F32),
            jax.ShapeDtypeStruct((EDGE, PAD, COLS), F32),
        ),
        in_specs=[spec] * 3,
        out_specs=(spec,) * 3,
        compiler_params=params(),
        cost_estimate=cost(10**9, 4 * 10**6),
    )(strip, left, right)


KTILE = 1024


def scatter_kernel(incoming, out, sides, turned, hot1, hot2, acc):
    turned[...] = incoming[...].T
    acc[...] = jnp.zeros_like(acc)
    rows1 = iota((4 * PAD, HALF), 0)
    rows2 = iota((4 * COLS, HALF), 0)

    @pl.loop(0, CAP // 8)
    def _(j):
        first = pl.multiple_of(j * 8, 8)
        values = turned[pl.ds(first, 8), :]
        cells = turned[pl.ds(CAP + first, 8), :].astype(I32)
        for q in range(8):
            at = slice(q * HALF, (q + 1) * HALF)
            cell = cells[q : q + 1, :]
            key1 = ((cell >> 10) & 3) * PAD + (cell >> 12)
            hit = rows1 == key1
            for p, piece in enumerate(split(values[q : q + 1, :], 2)):
                hot1[p * 4 * PAD : (p + 1) * 4 * PAD, at] = jnp.where(hit, piece.astype(F32), 0.0).astype(BF16)
            hot2[:, at] = one_hot(rows2 == (cell & 1023))
        for n in range(4):
            cols = slice(n * COLS, (n + 1) * COLS)
            acc[:, cols] += dot_nt(hot1[...], hot2[cols, :])

    y = natural(iota((COLS, COLS), 0))
    lane = iota((COLS, COLS), 1)
    place = jnp.where(y < 3, y, jnp.where(y >= 253, HALF + y - 253, -1000))
    packed = jnp.zeros((PAD, COLS), F32)
    for x in range(ROWS):
        cols = slice(x % 4 * COLS, (x % 4 + 1) * COLS)
        level = x // 4 * PAD
        value = acc[level : level + PAD, cols] + acc[4 * PAD + level : 4 * PAD + level + PAD, cols]
        out[x] = value
        select = one_hot(lane == place + 3 * x)
        for piece in split(value, 2):
            packed = packed + dot(piece, select)
    sides[0] = packed[:, :HALF]
    sides[1] = packed[:, HALF:]


def scatter(incoming):
    spec = pl.BlockSpec(memory_space=pltpu.VMEM)
    return pl.pallas_call(
        scatter_kernel,
        name="scatter",
        out_shape=(
            jax.ShapeDtypeStruct((ROWS, PAD, COLS), F32),
            jax.ShapeDtypeStruct((2, PAD, HALF), F32),
        ),
        in_specs=[spec],
        out_specs=(spec,) * 2,
        scratch_shapes=[
            pltpu.VMEM((HALF, DEV), F32),
            pltpu.VMEM((8 * PAD, KTILE), BF16),
            pltpu.VMEM((4 * COLS, KTILE), BF16),
            pltpu.VMEM((8 * PAD, 4 * COLS), F32),
        ],
        compiler_params=params(),
        cost_estimate=cost(10**10, 2 * 10**6),
    )(incoming)


def adjoint_strip_kernel(adjoint, left, right, out, up, down):
    lane = iota((COLS, COLS), 1)
    member_c = jnp.where(lane % HALF < PER_HALF * STRIP, lane % HALF % STRIP, -1)
    y = natural(iota((COLS, COLS), 0))
    own = one_hot(member_c == jnp.where(y < 6, 3 + y, jnp.where(y >= 250, y - 241, -2)))
    from_lane = iota((HALF, COLS), 0)
    member_c = member_c[:HALF]
    for x in range(ROWS):
        c = from_lane - 3 * x
        good = (c >= 0) & (c < 3)
        place_l = one_hot(good & (member_c == c))
        place_r = one_hot(good & (member_c == c + 15))
        value = jnp.zeros((PAD, COLS), F32)
        for source, place in ((adjoint[x], own), (left[0], place_l), (right[0], place_r)):
            for piece in split(source, 2):
                value = value + dot(piece, place)
        out[x] = value
        if x < EDGE:
            up[x] = adjoint[x]
            up[EDGE + x] = value
        if x >= ROWS - EDGE:
            down[x - (ROWS - EDGE)] = adjoint[x]
            down[x - (ROWS - EDGE) + EDGE] = value


def adjoint_strip(adjoint, left, right):
    spec = pl.BlockSpec(memory_space=pltpu.VMEM)
    return pl.pallas_call(
        adjoint_strip_kernel,
        name="adjoint_strip",
        out_shape=(
            jax.ShapeDtypeStruct((ROWS, PAD, COLS), F32),
            jax.ShapeDtypeStruct((2 * EDGE, PAD, COLS), F32),
            jax.ShapeDtypeStruct((2 * EDGE, PAD, COLS), F32),
        ),
        in_specs=[spec] * 3,
        out_specs=(spec,) * 3,
        compiler_params=params(),
        cost_estimate=cost(10**9, 4 * 10**6),
    )(adjoint, left, right)


def beside_permuted(value):
    even, odd = value[:, :HALF], value[:, HALF:]
    return jnp.concatenate([odd + pltpu.roll(odd, 1, 1), even + pltpu.roll(even, HALF - 1, 1)], axis=1)


def beside_natural(value):
    halves = []
    for half in (value[:, :HALF], value[:, HALF:]):
        halves.append(pltpu.roll(half, 1, 1) + pltpu.roll(half, HALF - 1, 1))
    return jnp.concatenate(halves, axis=1)


def total(terms):
    result = None
    for term in terms:
        if term is not None:
            result = term if result is None else result + term
    return result


def diffuse(first, wanted, beside, mask=None):
    rows = first
    for step in range(1, EDGE + 1):
        reach = EDGE - step
        later = {}
        for x in range(min(wanted) - reach, max(wanted) + reach + 1):
            here = rows.get(x)
            terms = [rows.get(x - 1), rows.get(x + 1)]
            if here is not None:
                terms += [beside(here), here * SELF]
            value = total(terms)
            if value is not None:
                later[x] = value if mask is None or step == EDGE else mask(x, value)
        rows = later
    return {x: rows[x] for x in wanted}


def put_split(ref, index, at, value):
    top = value.astype(BF16)
    ref[index, at, :] = top
    ref[index, pl.ds(at.start + PAD, 16), :] = (value - top.astype(F32)).astype(BF16)


def mix(weights, field):
    both = dot(weights, field)
    return both[:PAD] + both[PAD:]


INNER = ROWS - 2 * EDGE


def inner_kernel(ens, adj, weights, ends, before, border, out, field):
    k = pl.program_id(0)

    @pl.when(k == 0)
    def _():
        out[...] = before[...]

    top_open, bottom_open = ends[0], ends[1]

    def mask(x, value):
        if x < 0:
            return value * top_open
        if x >= ROWS:
            return value * bottom_open
        return value

    @pl.loop(0, PAD // 16)
    def _(group):
        at = pl.ds(pl.multiple_of(group * 16, 16), 16)
        spread = {x: ens[0, x, at, :].astype(F32) * adj[x, at, :] for x in range(ROWS)}
        result = diffuse(spread, range(ROWS), beside_permuted, mask)
        for x in range(ROWS):
            if EDGE <= x < ROWS - EDGE:
                put_split(field, x - EDGE, at, result[x])
            else:
                border[0, x if x < EDGE else x - INNER, at, :] = result[x]

    @pl.loop(0, INNER)
    def _(x):
        out[x] += ens[0, x + EDGE].astype(F32) * mix(weights[...], field[x])


def inner(ens, adj, weights, ends, before, first, count):
    resident = lambda *shape: pl.BlockSpec(shape, lambda k: (0,) * len(shape))
    return pl.pallas_call(
        inner_kernel,
        name="inner",
        grid=(count,),
        out_shape=(
            jax.ShapeDtypeStruct((count, 2 * EDGE, PAD, COLS), F32),
            jax.ShapeDtypeStruct((INNER, PAD, COLS), F32),
        ),
        in_specs=[
            pl.BlockSpec((1, ROWS, PAD, COLS), lambda k: (k + first, 0, 0, 0)),
            resident(ROWS, PAD, COLS),
            resident(2 * PAD, 2 * PAD),
            pl.BlockSpec(memory_space=pltpu.SMEM),
            resident(INNER, PAD, COLS),
        ],
        out_specs=(
            pl.BlockSpec((1, 2 * EDGE, PAD, COLS), lambda k: (k, 0, 0, 0)),
            resident(INNER, PAD, COLS),
        ),
        scratch_shapes=[pltpu.VMEM((INNER, 2 * PAD, COLS), BF16)],
        compiler_params=params(),
        cost_estimate=cost(count * 2 * 10**9, count * 2 * 10**6),
    )(ens, adj, weights, ends, before)


def outer_kernel(ens_t, ens_b, halo_t, halo_b, adj_t, adj_b, border, weights, before, out, field):
    k = pl.program_id(0)

    @pl.when(k == 0)
    def _():
        out[...] = before[...]

    @pl.loop(0, PAD // 16)
    def _(group):
        at = pl.ds(pl.multiple_of(group * 16, 16), 16)
        above = {x - EDGE: halo_t[0, x, at, :] * adj_t[x, at, :] for x in range(EDGE)}
        result = diffuse(above, range(EDGE), beside_permuted)
        for x in range(EDGE):
            put_split(field, x, at, result[x] + border[0, x, at, :])
        below = {EDGE + x: halo_b[0, x, at, :] * adj_b[x, at, :] for x in range(EDGE)}
        result = diffuse(below, range(EDGE), beside_permuted)
        for x in range(EDGE):
            put_split(field, EDGE + x, at, result[x] + border[0, EDGE + x, at, :])

    for x in range(EDGE):
        out[x] += ens_t[0, x].astype(F32) * mix(weights[...], field[x])
    for x in range(EDGE):
        out[EDGE + x] += ens_b[0, x + 1].astype(F32) * mix(weights[...], field[EDGE + x])


def outer(ens, halo_t, halo_b, adj_t, adj_b, border, weights, before, first, count):
    resident = lambda *shape: pl.BlockSpec(shape, lambda k: (0,) * len(shape))
    member = lambda rows, at=0, off=0: pl.BlockSpec((1, rows, PAD, COLS), lambda k: (k + off, at, 0, 0))
    return pl.pallas_call(
        outer_kernel,
        name="outer",
        grid=(count,),
        out_shape=jax.ShapeDtypeStruct((2 * EDGE, PAD, COLS), F32),
        in_specs=[
            member(4, 0, first),
            member(4, 3, first),
            member(EDGE),
            member(EDGE),
            resident(EDGE, PAD, COLS),
            resident(EDGE, PAD, COLS),
            member(2 * EDGE),
            resident(2 * PAD, 2 * PAD),
            resident(2 * EDGE, PAD, COLS),
        ],
        out_specs=resident(2 * EDGE, PAD, COLS),
        scratch_shapes=[pltpu.VMEM((2 * EDGE, 2 * PAD, COLS), BF16)],
        compiler_params=params(),
        cost_estimate=cost(count * 10**9, count * 3 * 10**6),
    )(ens, ens, halo_t, halo_b, adj_t, adj_b, border, weights, before)


def edge_kernel(strip, halo_t, halo_b, adj, adj_t, adj_b, weights, ends, open_lanes, inside, border, out, field):
    top_open, bottom_open = ends[0], ends[1]

    @pl.loop(0, PAD // 16)
    def _(group):
        at = pl.ds(pl.multiple_of(group * 16, 16), 16)
        lanes = open_lanes[...]

        def mask(x, value):
            value = value * lanes
            if x < 0:
                return value * top_open
            if x >= ROWS:
                return value * bottom_open
            return value

        spread = {x: strip[x, at, :].astype(F32) * adj[x, at, :] for x in range(ROWS)}
        for x in range(EDGE):
            spread[x - EDGE] = halo_t[x, at, :] * adj_t[x, at, :]
            spread[ROWS + x] = halo_b[x, at, :] * adj_b[x, at, :]
        result = diffuse(spread, range(ROWS), beside_natural, mask)
        for x in range(ROWS):
            put_split(field, x, at, result[x])

    from_lane = iota((COLS, COLS), 0)
    c = jnp.where(from_lane % HALF < PER_HALF * STRIP, from_lane % HALF % STRIP, -1)
    place = jnp.where((c >= 3) & (c < 6), c - 3, jnp.where((c >= 12) & (c < 15), 241 + c, -1))
    y = natural(iota((COLS, COLS), 1))
    collect = one_hot(place == y)
    y = natural(iota((PAD, COLS), 1))
    middle = (y >= EDGE) & (y < COLS - EDGE)
    for x in range(ROWS):
        if EDGE <= x < ROWS - EDGE:
            value = inside[x - EDGE]
        else:
            value = border[x if x < EDGE else x - INNER]
        value = jnp.where(middle, value, 0.0)
        product = strip[x].astype(F32) * mix(weights[...], field[x])
        for piece in split(product, 2):
            value = value + dot(piece, collect)
        out[x] = value * SCALE


def edge(strip, halo_t, halo_b, adj, adj_t, adj_b, weights, ends, open_lanes, inside, border):
    spec = pl.BlockSpec(memory_space=pltpu.VMEM)
    return pl.pallas_call(
        edge_kernel,
        name="edge",
        out_shape=jax.ShapeDtypeStruct((ROWS, PAD, COLS), F32),
        in_specs=[spec] * 7 + [pl.BlockSpec(memory_space=pltpu.SMEM)] + [spec] * 3,
        out_specs=spec,
        scratch_shapes=[pltpu.VMEM((ROWS, 2 * PAD, COLS), BF16)],
        compiler_params=params(),
        cost_estimate=cost(4 * 10**9, 8 * 10**6),
    )(strip, halo_t, halo_b, adj, adj_t, adj_b, weights, ends, open_lanes, inside, border)


def gather_kernel(field, incoming, out, turned, table, hot, picked):
    turned[...] = incoming[...].T
    picked[...] = jnp.zeros_like(picked)
    for x in range(ROWS):
        cols = slice(x % 4 * COLS, (x % 4 + 1) * COLS)
        for p, piece in enumerate(split(field[x], 2)):
            first = (p * 4 + x // 4) * PAD
            table[first : first + PAD, cols] = piece
    rows1 = iota((4 * PAD, COLS), 0)
    rows2 = iota((4 * COLS, COLS), 0)

    @pl.loop(0, CAP // 8)
    def _(j):
        first = pl.multiple_of(j * 8, 8)
        cells = turned[pl.ds(CAP + first, 8), :].astype(I32)
        lines = []
        for q in range(0, 8, 2):
            cell = jnp.concatenate([cells[q : q + 1, :], cells[q + 1 : q + 2, :]], axis=1)
            hot[...] = one_hot(rows2 == (cell & 1023))
            found = dot(table[...], hot[...])
            key1 = ((cell >> 10) & 3) * PAD + (cell >> 12)
            found = jnp.where(rows1 == key1, found[: 4 * PAD] + found[4 * PAD :], 0.0)
            found = jnp.sum(found, axis=0, keepdims=True)
            lines += [found[:, :HALF], found[:, HALF:]]
        picked[pl.ds(first, 8), :] = jnp.concatenate(lines, axis=0)

    out[...] = picked[...].T


def gather(field, incoming):
    spec = pl.BlockSpec(memory_space=pltpu.VMEM)
    return pl.pallas_call(
        gather_kernel,
        name="gather",
        out_shape=jax.ShapeDtypeStruct((DEV, HALF), F32),
        in_specs=[spec] * 2,
        out_specs=spec,
        scratch_shapes=[
            pltpu.VMEM((HALF, DEV), F32),
            pltpu.VMEM((8 * PAD, 4 * COLS), BF16),
            pltpu.VMEM((4 * COLS, COLS), BF16),
            pltpu.VMEM((HALF, DEV), F32),
        ],
        compiler_params=params(),
        cost_estimate=cost(10**10, 2 * 10**6),
    )(field, incoming)


def restore_kernel(field, perm_y, perm_r, out, rows):
    for x in range(ROWS):
        value = field[x]
        high, low = split(value, 2)
        rows[x] = dot(high, perm_y[...]) + dot(low, perm_y[...])
    for b in range(6):
        block = jnp.concatenate([rows[x, b * 16 : (b + 1) * 16, :] for x in range(ROWS)], axis=0)
        high, low = split(block, 2)
        value = dot(perm_r[...], high) + dot(perm_r[...], low)
        if b < 5:
            out[b * 256 : (b + 1) * 256, :] = value
        else:
            out[1280:1440, :] = value[:160]


def restore(field):
    y = np.arange(COLS)
    perm_y = np.zeros((COLS, COLS))
    perm_y[(y % 2) * HALF + y // 2, y] = 1
    i = np.arange(256)
    perm_r = np.zeros((256, 256))
    perm_r[i, i % 16 * 16 + i // 16] = 1
    spec = pl.BlockSpec(memory_space=pltpu.VMEM)
    return pl.pallas_call(
        restore_kernel,
        name="restore",
        out_shape=jax.ShapeDtypeStruct((LEV * ROWS, COLS), F32),
        in_specs=[spec] * 3,
        out_specs=spec,
        scratch_shapes=[pltpu.VMEM((ROWS, PAD, COLS), F32)],
        compiler_params=params(),
        cost_estimate=cost(10**9, 3 * 10**6),
    )(field, jnp.asarray(perm_y, BF16), jnp.asarray(perm_r, BF16)).reshape(LEV, ROWS, COLS)


def forward(value, axis):
    size = lax.axis_size(axis)
    return lax.ppermute(value, axis, [(i, i + 1) for i in range(size - 1)])


def backward(value, axis):
    size = lax.axis_size(axis)
    return lax.ppermute(value, axis, [(i + 1, i) for i in range(size - 1)])


FIRST = 5


def body(ensemble, vertical_weights, dual_vector, observed_column, observed_level, active_count):
    gx, gy = lax.axis_index("gx"), lax.axis_index("gy")
    last_x, last_y = lax.axis_size("gx") - 1, lax.axis_size("gy") - 1
    ends = jnp.stack([gx != 0, gx != last_x]).astype(F32)
    lane = jnp.arange(COLS) % HALF % STRIP
    closed = ((lane < 3) & (gy == 0)) | ((lane >= 15) & (gy == last_y))
    open_lanes = jnp.where(closed, 0.0, 1.0).astype(F32)[None, :]
    wide = jnp.pad(vertical_weights, ((0, PAD - LEV), (0, PAD - LEV)))
    high = lax.reduce_precision(wide, 8, 7)
    low = (wide - high).astype(BF16)
    high = high.astype(BF16)
    weights = jnp.concatenate(
        [jnp.concatenate([high, high], 1), jnp.concatenate([low, jnp.zeros_like(low)], 1)], 0
    )

    outgoing, target, rank = pack(active_count, dual_vector, observed_column, observed_level)
    incoming = lax.all_to_all(outgoing, ("gx", "gy"), split_axis=0, concat_axis=0, tiled=True)

    ens, ens_up, ens_down, strip, side = arrange(ensemble)
    halo_t = forward(ens_down, "gx")
    halo_b = backward(ens_up, "gx")
    from_left = forward(side[1:], "gy")
    from_right = backward(side[:1], "gy")
    strip, strip_up, strip_down = complete_strip(strip, from_left, from_right)
    strip_t = forward(strip_down, "gx")
    strip_b = backward(strip_up, "gx")

    adj, sides = scatter(incoming)
    adj_left = forward(sides[1:], "gy")
    adj_right = backward(sides[:1], "gy")
    zero = jnp.zeros((INNER, PAD, COLS), F32)
    border0, inside = inner(ens, adj, weights, ends, zero, 0, FIRST)
    adj_strip, adj_up, adj_down = adjoint_strip(adj, adj_left, adj_right)
    adj_t = forward(adj_down, "gx")
    adj_b = backward(adj_up, "gx")
    border1, inside = inner(ens, adj, weights, ends, inside, FIRST, MEM - FIRST)

    zero = jnp.zeros((2 * EDGE, PAD, COLS), F32)
    border = jnp.concatenate([border0, border1], axis=0)
    outside = outer(ens, halo_t, halo_b, adj_t[:EDGE], adj_b[:EDGE], border, weights, zero, 0, MEM)
    field = edge(
        strip, strip_t, strip_b, adj_strip, adj_t[EDGE:], adj_b[EDGE:], weights, ends, open_lanes, inside, outside
    )
    picked = gather(field, incoming)
    back = lax.all_to_all(picked, ("gx", "gy"), split_axis=0, concat_axis=0, tiled=True)
    increment = restore(field)
    obs_product = unpack(back, target, rank)
    return (increment, obs_product)


def solution(mesh):
    placed = (
        P(None, None, "gx", "gy"),
        P(),
        P(("gx", "gy")),
        P(("gx", "gy")),
        P(("gx", "gy")),
        P(("gx", "gy")),
    )
    return jax.shard_map(
        body,
        mesh=mesh,
        in_specs=placed,
        out_specs=(P(None, "gx", "gy"), P(("gx", "gy"))),
        check_vma=False,
    )
```

time: 522 us -> 218 us (0.42)
  other arithmetic: 202 us -> 7.06 us
  local copies, waits for them, and re-layouts: 176 us -> 9.78 us
  Pallas kernels: 0 us -> 143 us
  matrix products: 40.8 us -> 0 us
  blocking collectives: 28.1 us -> 0 us
  waiting for transfers between devices: 22.4 us -> 7.75 us
    pallas_call x0 -> x12, Pallas kernels: none -> 143 us  [the longest x2 42 us: inner(): pl.pallas_call(inner_kernel, name='inner', grid=(count,), out_shape=(jax....]
    add x2 -> x0, other arithmetic: 92.5 us -> none  [diffuse_once(): return centre + diffusivity * (beside_all - 4.0 * centre)]
    gather x2 -> x0, local copies, waits for them, and re-layouts: 72.5 us -> none  [the longest x1 60.7 us: body(): picked = increment[level_slot, row_slot, col_slot]]
    reduce_sum x2 -> x0, other arithmetic: 48.9 us -> none  [the longest x1 47.8 us: body(): jnp.sum(ensemble.astype(jnp.float32) * diffused, axis=0) / (members - 1)]
    dot_general x10 -> x0, matrix products: 40.8 us -> none  [one_member(): jnp.tensordot(vertical_weights, field, axes=((1,), (0,)), precision=lax.P...]
    unnamed x7 -> x0, other arithmetic: 40.7 us -> none
    while x2 -> x0, local copies, waits for them, and re-layouts: 39.7 us -> none  [vertical_mix(): return lax.map(one_member, spread)]
    all_to_all x1 -> x0, blocking collectives: 28.1 us -> none  [body(): lax.all_to_all(picked, ('gx', 'gy'), split_axis=0, concat_axis=0, tiled=T...]
  transfers between devices with their start and end apart: 13 -> 12, of which waited for: 7 -> 2; matrix products, arithmetic and copies ran while one was open for 8% -> 6% of each run, Pallas kernels for 0% -> 53%
where the time goes in v1:
time: 218 us; the launch traced here: 217 us
  Pallas kernels  143 us (66%)
  starting transfers between devices  48.4 us (22%)
  local copies, waits for them, and re-layouts  9.78 us (4%)
  waiting for transfers between devices  7.75 us (4%)
  other arithmetic  7.06 us (3%)
    pallas_call x2, Pallas kernels, inner(): pl.pallas_call(inner_kernel, name='inner', grid=(count,), out_shape=(jax....  42 us
    pallas_call x1, Pallas kernels, arrange(): pl.pallas_call(arrange_kernel, name='arrange', grid=(MEM,), out_shape=(ja...  28.9 us
    pallas_call x1, Pallas kernels, outer(): pl.pallas_call(outer_kernel, name='outer', grid=(count,), out_shape=jax.S...  16.6 us
    ppermute x5, starting transfers between devices, forward(): return lax.ppermute(value, axis, [(i, i + 1) for i in range(size - 1)])  16.5 us
    pallas_call x1, Pallas kernels, scatter(): pl.pallas_call(scatter_kernel, name='scatter', out_shape=(jax.ShapeDtypeS...  16.2 us
    pallas_call x1, Pallas kernels, gather(): pl.pallas_call(gather_kernel, name='gather', out_shape=jax.ShapeDtypeStru...  13.3 us
    all_to_all x1, starting transfers between devices, body(): lax.all_to_all(outgoing, ('gx', 'gy'), split_axis=0, concat_axis=0, tiled...  11.5 us
    all_to_all x1, starting transfers between devices, body(): lax.all_to_all(picked, ('gx', 'gy'), split_axis=0, concat_axis=0, tiled=T...  11.1 us
  transfers between devices with their start and end apart: 12, of which 2 were waited for; matrix products, arithmetic and copies ran while one was open for 6% of the time, Pallas kernels for 53%

profile of v1, /device:TPU:1, one launch (start us, length us, event | category | flops | bytes accessed | tf_op | source)
XLA Modules:
  0.0 217.5 jit_solution(29738268602127904)
XLA Ops:
  1.3 3.5 %pack.1 = (f32[128,128]{1,0:T(8,128)}, s32[16,128]{1,0:T(8,128)}, s32[16,128]{1,0:T(8,128)}) custom-call(s32[1]{0:T(128)S(6)} %copy.15.count, f32[16,128]{1,0:T(8,128)} %bitcast.22, s32[16,128]{1,0:T(8,128)} %bitcast.23, s32[16,128]{1,0:T(8,128)} %bitcast.24, bf16[128,256]{1,0:T(8,128)(2,1)} %constant.58.clone.upper), custom_call_target="tpu_custom_call" | custom-call | flops 1000000000 | bytes 1000000 | tf_op jit(solution)/shard_map/pack/pallas_call | solution.py:98
  4.8 11.5 %all-to-all-start = ((f32[128,1,128]{2,1,0:T(1,128)}), f32[128,1,128]{2,1,0:T(1,128)S(1)}, u32[]{:S(2)}, u32[]{:S(2)}) async-start(f32[128,1,128]{2,1,0:T(1,128)} %bitcast.18), calls=%async_computation | async-start | bytes 131072 | tf_op jit(solution)/shard_map/all_to_all | solution.py:688
  16.3 28.9 %arrange.1 = (bf16[10,16,96,256]{3,2,1,0:T(8,128)(2,1)}, f32[10,3,96,256]{3,2,1,0:T(8,128)}, f32[10,3,96,256]{3,2,1,0:T(8,128)}, bf16[16,96,256]{2,1,0:T(8,128)(2,1)}, f32[2,16,96,128]{3,2,1,0:T(8,128)}) custom-call(bf16[10,1440,256]{2,1,0:T(8,128)(2,1)} %bitcast.21, bf16[256,256]{1,0:T(8,128)(2,1)} %constant.59.clone.perm_y, ...), custom_call_target="tpu_custom_call" | custom-call | flops 10000000000 | bytes 25000000 | tf_op jit(solution)/shard_map/arrange/pallas_call | solution.py:193
  45.2 3.8 %collective-permute-start.8 = (f32[10,3,96,256]{3,2,1,0:T(8,128)}, f32[10,3,96,256]{3,2,1,0:T(8,128)}, u32[]{:S(2)}, u32[]{:S(2)}) collective-permute-start(f32[10,3,96,256]{3,2,1,0:T(8,128)} %get-tuple-element.36), channel_id=1, source_target_pairs={{0,16},{16,32},{32,48},{48,64},{64,80},{80,96},{96,112},{1,17},{17... | collective-permute-start | bytes 8847368 | tf_op jit(solution)/shard_map/ppermute | solution.py:661
  49.0 2.2 %collective-permute-start.9 = (f32[10,3,96,256]{3,2,1,0:T(8,128)}, f32[10,3,96,256]{3,2,1,0:T(8,128)}, u32[]{:S(2)}, u32[]{:S(2)}) collective-permute-start(f32[10,3,96,256]{3,2,1,0:T(8,128)} %get-tuple-element.37), channel_id=1, source_target_pairs={{16,0},{32,16},{48,32},{64,48},{80,64},{96,80},{112,96},{17,1},{33... | collective-permute-start | bytes 8847368 | tf_op jit(solution)/shard_map/ppermute | solution.py:666
  52.7 3.3 %collective-permute-start = (f32[1,16,96,128]{3,2,1,0:T(8,128)S(1)}, f32[1,16,96,128]{3,2,1,0:T(8,128)S(1)}, u32[]{:S(2)}, u32[]{:S(2)}) collective-permute-start(f32[1,16,96,128]{3,2,1,0:T(8,128)S(1)} %get-tuple-element.43), channel_id=1, source_target_pairs={{0,1},{1,2},{2,3},{3,4},{4,5},{5,6},{6,7},{7,8},{8,9},{9,10},{10,1... | collective-permute-start | bytes 2359304 | tf_op jit(solution)/shard_map/ppermute | solution.py:661
  58.0 16.2 %scatter.1 = (f32[16,96,256]{2,1,0:T(8,128)}, f32[2,96,128]{2,1,0:T(8,128)}) custom-call(f32[128,128]{1,0:T(8,128)} %bitcast.16), custom_call_target="tpu_custom_call" | custom-call | flops 10000000000 | bytes 2000000 | tf_op jit(solution)/shard_map/scatter/pallas_call | solution.py:296
  75.0 3.0 %collective-permute-start.4 = (f32[1,96,128]{2,1,0:T(8,128)S(1)}, f32[1,96,128]{2,1,0:T(8,128)S(1)}, u32[]{:S(2)}, u32[]{:S(2)}) collective-permute-start(f32[1,96,128]{2,1,0:T(8,128)S(1)} %get-tuple-element.49), channel_id=1, source_target_pairs={{0,1},{1,2},{2,3},{3,4},{4,5},{5,6},{6,7},{7,8},{8,9},{9,10},{10,1... | collective-permute-start | bytes 147464 | tf_op jit(solution)/shard_map/ppermute | solution.py:661
  81.3 2.1 collective-permute-done.5.right
  84.0 4.5 %adjoint_strip.1 = (f32[16,96,256]{2,1,0:T(8,128)}, f32[6,96,256]{2,1,0:T(8,128)}, f32[6,96,256]{2,1,0:T(8,128)}) custom-call(f32[16,96,256]{2,1,0:T(8,128)} %get-tuple-element.28.adjoint.adj, f32[1,96,128]{2,1,0:T(8,128)} %copy-done.9, f32[1,96,128]{2,1,0:T(8,128)} %copy-done.10), custom_call_target="tpu_custom_call" | custom-call | flops 1000000000 | bytes 4000000 | tf_op jit(solution)/shard_map/adjoint_strip/pallas_call | solution.py:343
  88.6 2.6 %collective-permute-start.7 = (f32[6,96,256]{2,1,0:T(8,128)}, f32[6,96,256]{2,1,0:T(8,128)S(1)}, u32[]{:S(2)}, u32[]{:S(2)}) collective-permute-start(f32[6,96,256]{2,1,0:T(8,128)} %get-tuple-element.32), channel_id=1, source_target_pairs={{16,0},{32,16},{48,32},{64,48},{80,64},{96,80},{112,96},{17,1},{33... | collective-permute-start | bytes 1769480 | tf_op jit(solution)/shard_map/ppermute | solution.py:666
  92.2 20.9 %inner.2 = (f32[5,6,96,256]{3,2,1,0:T(8,128)}, f32[10,96,256]{2,1,0:T(8,128)}) custom-call(bf16[10,16,96,256]{3,2,1,0:T(8,128)(2,1)} %get-tuple-element.33.ens.ens_t.ens_b, f32[16,96,256]{2,1,0:T(8,128)} %get-tuple-element.28.adjoint.adj, bf16[192,192]{1,0:T(8,128)(2,1)} %fusion.1.weights, f32[2]{0:T(128)} %add_convert_fusion.ends, ...), custom_call_target="tpu_custom_call" | custom-call | flops 10000000000 | bytes 10000000 | tf_op jit(solution)/shard_map/inner/pallas_call | solution.py:443
  113.2 3.9 %collective-permute-start.6 = (f32[6,96,256]{2,1,0:T(8,128)S(1)}, f32[6,96,256]{2,1,0:T(8,128)S(1)}, u32[]{:S(2)}, u32[]{:S(2)}) collective-permute-start(f32[6,96,256]{2,1,0:T(8,128)S(1)} %copy-done.6), channel_id=1, source_target_pairs={{0,16},{16,32},{32,48},{48,64},{64,80},{80,96},{96,112},{1,17},{17... | collective-permute-start | bytes 1769480 | tf_op jit(solution)/shard_map/ppermute | solution.py:661
  117.1 21.1 %inner.3 = (f32[5,6,96,256]{3,2,1,0:T(8,128)}, f32[10,96,256]{2,1,0:T(8,128)}) custom-call(bf16[10,16,96,256]{3,2,1,0:T(8,128)(2,1)} %get-tuple-element.33.ens.ens_t.ens_b, f32[16,96,256]{2,1,0:T(8,128)} %get-tuple-element.28.adjoint.adj, bf16[192,192]{1,0:T(8,128)(2,1)} %fusion.1.weights, f32[2]{0:T(128)} %add_convert_fusion.ends, ...), custom_call_target="tpu_custom_call" | custom-call | flops 10000000000 | bytes 10000000 | tf_op jit(solution)/shard_map/inner/pallas_call | solution.py:443
  138.2 5.1 %pad_maximum_fusion.border = f32[10,6,96,256]{3,2,1,0:T(8,128)} fusion(f32[5,6,96,256]{3,2,1,0:T(8,128)} %get-tuple-element.39, f32[5,6,96,256]{3,2,1,0:T(8,128)S(1)} %copy-done), kind=kLoop, calls=%fused_computation | loop fusion | flops 1474560 | bytes 11796480 | tf_op jit(solution)/shard_map/concatenate | solution.py:710
  146.2 3.2 %complete_strip.1 = (bf16[16,96,256]{2,1,0:T(8,128)(2,1)}, f32[3,96,256]{2,1,0:T(8,128)}, f32[3,96,256]{2,1,0:T(8,128)}) custom-call(bf16[16,96,256]{2,1,0:T(8,128)(2,1)} %get-tuple-element.22.strip, f32[1,16,96,128]{3,2,1,0:T(8,128)} %copy-done.4, f32[1,16,96,128]{3,2,1,0:T(8,128)} %copy-done.5), custom_call_target="tpu_custom_call" | custom-call | flops 1000000000 | bytes 4000000 | tf_op jit(solution)/shard_map/complete_strip/pallas_call | solution.py:237
  149.4 2.4 %collective-permute-start.2 = (f32[3,96,256]{2,1,0:T(8,128)}, f32[3,96,256]{2,1,0:T(8,128)S(1)}, u32[]{:S(2)}, u32[]{:S(2)}) collective-permute-start(f32[3,96,256]{2,1,0:T(8,128)} %get-tuple-element.25), channel_id=1, source_target_pairs={{0,16},{16,32},{32,48},{48,64},{64,80},{80,96},{96,112},{1,17},{17... | collective-permute-start | bytes 884744 | tf_op jit(solution)/shard_map/ppermute | solution.py:661
  154.6 16.6 %outer.1.border = f32[6,96,256]{2,1,0:T(8,128)} custom-call(bf16[10,16,96,256]{3,2,1,0:T(8,128)(2,1)} %get-tuple-element.33.ens.ens_t.ens_b, bf16[10,16,96,256]{3,2,1,0:T(8,128)(2,1)} %get-tuple-element.33.ens.ens_t.ens_b, f32[10,3,96,256]{3,2,1,0:T(8,128)} %collective-permute-done.8.halo_t, f32[10,3,96,256]{3,2,1,0:T(8,128)} %collective-permute-done.9.halo_b, ...), custom_call_target="tpu_custom_call" | custom-call | flops 10000000000 | bytes 30000000 | tf_op jit(solution)/shard_map/outer/pallas_call | solution.py:496
  172.1 8.7 %edge.1.field = f32[16,96,256]{2,1,0:T(8,128)} custom-call(bf16[16,96,256]{2,1,0:T(8,128)(2,1)} %get-tuple-element.24.strip, f32[3,96,256]{2,1,0:T(8,128)} %copy-done.7, f32[3,96,256]{2,1,0:T(8,128)} %copy-done.8, f32[16,96,256]{2,1,0:T(8,128)} %get-tuple-element.30.adj, f32[3,96,256]{2,1,0:T(8,128)} %get-tuple-element.47.adj_t, ...), custom_call_target="tpu_custom_call" | custom-call | flops 4000000000 | bytes 8000000 | tf_op jit(solution)/shard_map/edge/pallas_call | solution.py:564
  180.8 13.3 %gather.1 = f32[128,128]{1,0:T(8,128)} custom-call(f32[16,96,256]{2,1,0:T(8,128)} %edge.1.field, f32[128,128]{1,0:T(8,128)} %bitcast.17), custom_call_target="tpu_custom_call" | custom-call | flops 10000000000 | bytes 2000000 | tf_op jit(solution)/shard_map/gather/pallas_call | solution.py:607
  194.2 11.1 %all-to-all-start.1 = ((f32[128,1,128]{2,1,0:T(1,128)}), f32[128,1,128]{2,1,0:T(1,128)S(1)}, u32[]{:S(2)}, u32[]{:S(2)}) async-start(f32[128,1,128]{2,1,0:T(1,128)} %bitcast.20), calls=%async_computation.1 | async-start | bytes 131072 | tf_op jit(solution)/shard_map/all_to_all | solution.py:716
  205.2 3.9 %restore.1 = f32[1440,256]{1,0:T(8,128)} custom-call(f32[16,96,256]{2,1,0:T(8,128)} %edge.1.field, bf16[256,256]{1,0:T(8,128)(2,1)} %constant.61.clone.perm_y, bf16[256,256]{1,0:T(8,128)(2,1)} %constant.60.clone.perm_r), custom_call_target="tpu_custom_call" | custom-call | flops 1000000000 | bytes 3000000 | tf_op jit(solution)/shard_map/restore/pallas_call | solution.py:647
  209.2 5.6 %all-to-all-done.1 = f32[128,1,128]{2,1,0:T(1,128)S(1)} async-done(((f32[128,1,128]{2,1,0:T(1,128)}), f32[128,1,128]{2,1,0:T(1,128)S(1)}, u32[]{:S(2)}, u32[]{:S(2)}) %all-to-all-start.1) | async-done | bytes 65568 | tf_op jit(solution)/shard_map/all_to_all | solution.py:716
  215.4 2.0 unpack.1
  (45 shorter events, 16.3 us)
Async XLA Ops:
  4.8 52.6 %all-to-all-start = ((f32[128,1,128]{2,1,0:T(1,128)}), f32[128,1,128]{2,1,0:T(1,128)S(1)}, u32[]{:S(2)}, u32[]{:S(2)}) async-start(f32[128,1,128]{2,1,0:T(1,128)} %bitcast.18), calls=%async_computation | async-start | bytes 131072 | tf_op jit(solution)/shard_map/all_to_all | solution.py:688
  45.2 10.9 %copy-start.3 = (f32[90,90]{1,0:T(8,128)S(1)}, f32[90,90]{1,0:T(8,128)}, u32[]{:S(2)}) copy-start(f32[90,90]{1,0:T(8,128)} %param.12) | copy-start | bytes 97204
  45.2 108.6 %collective-permute-start.8 = (f32[10,3,96,256]{3,2,1,0:T(8,128)}, f32[10,3,96,256]{3,2,1,0:T(8,128)}, u32[]{:S(2)}, u32[]{:S(2)}) collective-permute-start(f32[10,3,96,256]{3,2,1,0:T(8,128)} %get-tuple-element.36), channel_id=1, source_target_pairs={{0,16},{16,32},{32,48},{48,64},{64,80},{80,96},{96,112},{1,17},{17... | collective-permute-start | bytes 8847368 | tf_op jit(solution)/shard_map/ppermute | solution.py:661
  49.0 104.8 %collective-permute-start.9 = (f32[10,3,96,256]{3,2,1,0:T(8,128)}, f32[10,3,96,256]{3,2,1,0:T(8,128)}, u32[]{:S(2)}, u32[]{:S(2)}) collective-permute-start(f32[10,3,96,256]{3,2,1,0:T(8,128)} %get-tuple-element.37), channel_id=1, source_target_pairs={{16,0},{32,16},{48,32},{64,48},{80,64},{96,80},{112,96},{17,1},{33... | collective-permute-start | bytes 8847368 | tf_op jit(solution)/shard_map/ppermute | solution.py:666
  52.7 92.4 %collective-permute-start = (f32[1,16,96,128]{3,2,1,0:T(8,128)S(1)}, f32[1,16,96,128]{3,2,1,0:T(8,128)S(1)}, u32[]{:S(2)}, u32[]{:S(2)}) collective-permute-start(f32[1,16,96,128]{3,2,1,0:T(8,128)S(1)} %get-tuple-element.43), channel_id=1, source_target_pairs={{0,1},{1,2},{2,3},{3,4},{4,5},{5,6},{6,7},{7,8},{8,9},{9,10},{10,1... | collective-permute-start | bytes 2359304 | tf_op jit(solution)/shard_map/ppermute | solution.py:661
  57.4 0.6 copy-start.1
  75.0 5.0 %collective-permute-start.4 = (f32[1,96,128]{2,1,0:T(8,128)S(1)}, f32[1,96,128]{2,1,0:T(8,128)S(1)}, u32[]{:S(2)}, u32[]{:S(2)}) collective-permute-start(f32[1,96,128]{2,1,0:T(8,128)S(1)} %get-tuple-element.49), channel_id=1, source_target_pairs={{0,1},{1,2},{2,3},{3,4},{4,5},{5,6},{6,7},{7,8},{8,9},{9,10},{10,1... | collective-permute-start | bytes 147464 | tf_op jit(solution)/shard_map/ppermute | solution.py:661
  78.1 5.3 %collective-permute-start.5 = (f32[1,96,128]{2,1,0:T(8,128)S(1)}, f32[1,96,128]{2,1,0:T(8,128)S(1)}, u32[]{:S(2)}, u32[]{:S(2)}) collective-permute-start(f32[1,96,128]{2,1,0:T(8,128)S(1)} %get-tuple-element.48), channel_id=1, source_target_pairs={{1,0},{2,1},{3,2},{4,3},{5,4},{6,5},{7,6},{8,7},{9,8},{10,9},{11,1... | collective-permute-start | bytes 147464 | tf_op jit(solution)/shard_map/ppermute | solution.py:666
  80.0 3.4 %copy-start.9 = (f32[1,96,128]{2,1,0:T(8,128)}, f32[1,96,128]{2,1,0:T(8,128)S(1)}, u32[]{:S(2)}) copy-start(f32[1,96,128]{2,1,0:T(8,128)S(1)} %collective-permute-done.4.left) | copy-start | bytes 147460
  80.0 65.0 %collective-permute-start.1 = (f32[1,16,96,128]{3,2,1,0:T(8,128)S(1)}, f32[1,16,96,128]{3,2,1,0:T(8,128)S(1)}, u32[]{:S(2)}, u32[]{:S(2)}) collective-permute-start(f32[1,16,96,128]{3,2,1,0:T(8,128)S(1)} %get-tuple-element.42), channel_id=1, source_target_pairs={{1,0},{2,1},{3,2},{4,3},{5,4},{6,5},{7,6},{8,7},{9,8},{10,9},{11,1... | collective-permute-start | bytes 2359304 | tf_op jit(solution)/shard_map/ppermute | solution.py:666
  83.4 0.6 copy-start.10
  88.6 24.6 %collective-permute-start.7 = (f32[6,96,256]{2,1,0:T(8,128)}, f32[6,96,256]{2,1,0:T(8,128)S(1)}, u32[]{:S(2)}, u32[]{:S(2)}) collective-permute-start(f32[6,96,256]{2,1,0:T(8,128)} %get-tuple-element.32), channel_id=1, source_target_pairs={{16,0},{32,16},{48,32},{64,48},{80,64},{96,80},{112,96},{17,1},{33... | collective-permute-start | bytes 1769480 | tf_op jit(solution)/shard_map/ppermute | solution.py:666
  92.2 21.0 %copy-start.6 = (f32[6,96,256]{2,1,0:T(8,128)S(1)}, f32[6,96,256]{2,1,0:T(8,128)}, u32[]{:S(2)}) copy-start(f32[6,96,256]{2,1,0:T(8,128)} %get-tuple-element.31) | copy-start | bytes 1769476
  113.2 31.0 %collective-permute-start.6 = (f32[6,96,256]{2,1,0:T(8,128)S(1)}, f32[6,96,256]{2,1,0:T(8,128)S(1)}, u32[]{:S(2)}, u32[]{:S(2)}) collective-permute-start(f32[6,96,256]{2,1,0:T(8,128)S(1)} %copy-done.6), channel_id=1, source_target_pairs={{0,16},{16,32},{32,48},{48,64},{64,80},{80,96},{96,112},{1,17},{17... | collective-permute-start | bytes 1769480 | tf_op jit(solution)/shard_map/ppermute | solution.py:661
  117.1 21.1 %copy-start = (f32[5,6,96,256]{3,2,1,0:T(8,128)S(1)}, f32[5,6,96,256]{3,2,1,0:T(8,128)}, u32[]{:S(2)}) copy-start(f32[5,6,96,256]{3,2,1,0:T(8,128)} %get-tuple-element.38) | copy-start | bytes 8847364
  145.1 0.9 copy-start.4
  145.1 1.1 copy-start.5
  149.4 21.9 %collective-permute-start.2 = (f32[3,96,256]{2,1,0:T(8,128)}, f32[3,96,256]{2,1,0:T(8,128)S(1)}, u32[]{:S(2)}, u32[]{:S(2)}) collective-permute-start(f32[3,96,256]{2,1,0:T(8,128)} %get-tuple-element.25), channel_id=1, source_target_pairs={{0,16},{16,32},{32,48},{48,64},{64,80},{80,96},{96,112},{1,17},{17... | collective-permute-start | bytes 884744 | tf_op jit(solution)/shard_map/ppermute | solution.py:661
  151.8 19.5 %collective-permute-start.3 = (f32[3,96,256]{2,1,0:T(8,128)}, f32[3,96,256]{2,1,0:T(8,128)S(1)}, u32[]{:S(2)}, u32[]{:S(2)}) collective-permute-start(f32[3,96,256]{2,1,0:T(8,128)} %get-tuple-element.26), channel_id=1, source_target_pairs={{16,0},{32,16},{48,32},{64,48},{80,64},{96,80},{112,96},{17,1},{33... | collective-permute-start | bytes 884744 | tf_op jit(solution)/shard_map/ppermute | solution.py:666
  171.3 0.7 copy-start.7
  171.3 0.8 copy-start.8
  194.2 20.6 %all-to-all-start.1 = ((f32[128,1,128]{2,1,0:T(1,128)}), f32[128,1,128]{2,1,0:T(1,128)S(1)}, u32[]{:S(2)}, u32[]{:S(2)}) async-start(f32[128,1,128]{2,1,0:T(1,128)} %bitcast.20), calls=%async_computation.1 | async-start | bytes 131072 | tf_op jit(solution)/shard_map/all_to_all | solution.py:716
  214.8 0.6 copy-start.2

commit v2 on v1

v2 whole, which is shorter than its diff:
```python
import jax
import jax.numpy as jnp
import numpy as np
from jax import lax
from jax.experimental import pallas as pl
from jax.experimental.pallas import tpu as pltpu
from jax.sharding import PartitionSpec as P

F32 = jnp.float32
BF16 = jnp.bfloat16
I32 = jnp.int32

MEM, LEV, ROWS, COLS = 10, 90, 16, 256
PAD = 96
DEV = 128
CAP = 48
SLOTS = 2048
HALF = 128
QUARTER = 64
DUO = 2 * COLS
DUOS = MEM // 2
EDGE = 3
STRIP = 18
PAIRS = STRIP // 2
SELF = 1.0 / 6.0
SCALE = 0.24**3 / (MEM - 1)
VMEM = 20 * 1024 * 1024


def split(value, count):
    parts = []
    for _ in range(count - 1):
        top = value.astype(BF16)
        parts.append(top)
        value = value - top.astype(F32)
    parts.append(value.astype(BF16))
    return parts


def dot(a, b):
    return lax.dot_general(a, b, (((1,), (0,)), ((), ())), preferred_element_type=F32)


def dot_nt(a, b):
    return lax.dot_general(a, b, (((1,), (1,)), ((), ())), preferred_element_type=F32)


def iota(shape, dim):
    return lax.broadcasted_iota(I32, shape, dim)


def one_hot(test):
    return jnp.where(test, 1.0, 0.0).astype(BF16)


def params(**kw):
    return pltpu.CompilerParams(vmem_limit_bytes=VMEM, **kw)


def cost(flops, moved):
    return pl.CostEstimate(flops=flops, bytes_accessed=moved, transcendentals=0)


def pack_kernel(count, dual, col, lev, upper, vertical, out, tgt_out, rank_out, weights, left_v, left_c, right_v, right_c):
    wide = jnp.concatenate([vertical[...], jnp.zeros((LEV, PAD - LEV), F32)], axis=1)
    high, low = split(jnp.concatenate([wide, jnp.zeros((PAD - LEV, PAD), F32)], axis=0), 2)
    both = jnp.concatenate([low, jnp.zeros_like(low)], axis=1)
    weights[...] = jnp.concatenate([jnp.concatenate([high, high], axis=1), both], axis=0)
    number = count[0]
    rows = iota((DEV, HALF), 0)
    lane = iota((1, HALF), 1)
    carry = jnp.zeros((DEV, HALF), F32)
    for i in range(SLOTS // HALF):
        at = slice(i * HALF, (i + 1) * HALF)
        column = col[i : i + 1, :]
        row = column >> 12
        gcol = column & 4095
        y = gcol & 255
        y = ((y & 3) << 6) + (y >> 2)
        target = ((row >> 4) << 4) + (gcol >> 8)
        target = jnp.where(i * HALF + lane < number, target, -1)
        hit = rows == target
        both = dot(one_hot(hit), upper[...])
        rank = jnp.sum(jnp.where(hit, both[:, :HALF] + carry, 0.0), axis=0, keepdims=True)
        carry = carry + both[:, HALF:]
        tgt_out[i : i + 1, :] = target
        rank = rank.astype(I32)
        rank_out[i : i + 1, :] = rank
        right_v[:, at] = one_hot(rows == rank)
        right_c[:, at] = one_hot(rows == rank + CAP)
        values = dual[i : i + 1, :]
        for p, piece in enumerate(split(values, 3)):
            left_v[p * DEV : (p + 1) * DEV, at] = jnp.where(hit, piece.astype(F32), 0.0).astype(BF16)
        cells = (lev[i : i + 1, :] << 12, (row & 15) << 8, y)
        for p, piece in enumerate(cells):
            left_c[p * DEV : (p + 1) * DEV, at] = jnp.where(hit, piece.astype(F32), 0.0).astype(BF16)
    a = dot_nt(left_v[...], right_v[...])
    b = dot_nt(left_c[...], right_c[...])
    out[...] = ((a[:DEV] + a[DEV : 2 * DEV]) + a[2 * DEV :]) + ((b[:DEV] + b[DEV : 2 * DEV]) + b[2 * DEV :])


def pack(count, dual, col, lev, vertical):
    upper = np.concatenate([np.triu(np.ones((HALF, HALF)), 1), np.ones((HALF, HALF))], 1)
    spec = pl.BlockSpec(memory_space=pltpu.VMEM)
    return pl.pallas_call(
        pack_kernel,
        name="pack",
        out_shape=(
            jax.ShapeDtypeStruct((DEV, HALF), F32),
            jax.ShapeDtypeStruct((SLOTS // HALF, HALF), I32),
            jax.ShapeDtypeStruct((SLOTS // HALF, HALF), I32),
            jax.ShapeDtypeStruct((2 * PAD, 2 * PAD), BF16),
        ),
        in_specs=[pl.BlockSpec(memory_space=pltpu.SMEM)] + [spec] * 5,
        out_specs=(spec,) * 4,
        scratch_shapes=[pltpu.VMEM((3 * DEV, SLOTS), BF16)] * 2 + [pltpu.VMEM((DEV, SLOTS), BF16)] * 2,
        compiler_params=params(),
        cost_estimate=cost(10**9, 10**6),
    )(count, dual.reshape(-1, HALF), col.reshape(-1, HALF), lev.reshape(-1, HALF), jnp.asarray(upper, BF16), vertical)


def unpack_kernel(back, tgt, rank, out):
    rows = iota((DEV, HALF), 0)
    table = jnp.concatenate(split(back[...], 3), axis=0)
    for i in range(SLOTS // HALF):
        found = dot(table, one_hot(rows == rank[i : i + 1, :]))
        found = (found[:DEV] + found[DEV : 2 * DEV]) + found[2 * DEV :]
        out[i : i + 1, :] = jnp.sum(jnp.where(rows == tgt[i : i + 1, :], found, 0.0), axis=0, keepdims=True)


def unpack(back, tgt, rank):
    spec = pl.BlockSpec(memory_space=pltpu.VMEM)
    return pl.pallas_call(
        unpack_kernel,
        name="unpack",
        out_shape=jax.ShapeDtypeStruct((SLOTS // HALF, HALF), F32),
        in_specs=[spec] * 3,
        out_specs=spec,
        compiler_params=params(),
        cost_estimate=cost(10**8, 10**5),
    )(back, tgt, rank).reshape(SLOTS)


def strip_place(lane):
    j = lane % HALF
    return j // PAIRS, jnp.where(j < MEM * PAIRS, j % PAIRS * 2 + lane // HALF, -1)


def natural(place):
    return ((place & 63) << 2) + (place >> 6)


def duo_place(place):
    return ((place & 63) << 2) + (place >> 7), (place >> 6) & 1


def widen(value):
    low = iota((value.shape[0], HALF), 1) < QUARTER
    phases = []
    for half in (value[:, :HALF], value[:, HALF:]):
        turned = pltpu.roll(half, QUARTER, 1)
        phases += [jnp.where(low, half, turned), jnp.where(low, turned, half)]
    return jnp.concatenate(phases, axis=1)


def fold(value):
    low = iota((value.shape[0], HALF), 1) < QUARTER
    p = [value[:, i * HALF : (i + 1) * HALF] for i in range(4)]
    return jnp.concatenate(
        [jnp.where(low, p[i], p[i + 1]) + pltpu.roll(jnp.where(low, p[i + 1], p[i]), QUARTER, 1) for i in (0, 2)],
        axis=1,
    )


def arrange_kernel(ens, perm_y, perm_r, out, up, down, strip, side_l, side_r, buffer, rows, select, sem):
    def fetch(k):
        return pltpu.make_async_copy(ens.at[k], buffer.at[k % 4], sem.at[k % 4])

    fetch(0).start()
    fetch(1).start()
    rows[LEV * ROWS :, :] = jnp.zeros((rows.shape[0] - LEV * ROWS, DUO), BF16)

    @pl.loop(0, DUOS)
    def _(duo):
        @pl.when(duo < DUOS - 1)
        def _():
            fetch(2 * duo + 2).start()
            fetch(2 * duo + 3).start()

        fetch(2 * duo).wait()
        fetch(2 * duo + 1).wait()
        here, there = 2 * duo % 4, (2 * duo + 1) % 4
        y, which = duo_place(iota((DUO, COLS), 0))
        member, c = strip_place(iota((DUO, COLS), 1))
        want = jnp.where(y < 6, 3 + y, jnp.where(y >= 250, y - 241, -2))
        select[pl.ds(pl.multiple_of(duo * DUO, DUO), DUO), :] = one_hot((member == 2 * duo + which) & (c == want))
        for b in range(6):
            at = slice(b * 240, (b + 1) * 240)
            block = jnp.concatenate([buffer[here, at, :], buffer[there, at, :]], axis=1)
            rows[at, :] = dot(block, perm_y[...]).astype(BF16)
        for b in range(6):
            turned = dot(perm_r[...], rows[b * 256 : (b + 1) * 256, :])
            at = slice(b * 16, (b + 1) * 16)
            for x in range(ROWS):
                part = turned[x * 16 : (x + 1) * 16, :]
                out[duo, x, at, :] = part.astype(BF16)
                if x < EDGE:
                    up[duo, x, at, :] = part
                if x >= ROWS - EDGE:
                    down[duo, x - (ROWS - EDGE), at, :] = part

    @pl.loop(0, ROWS)
    def _(x):
        every = jnp.concatenate([out[duo, x] for duo in range(DUOS)], axis=1)
        strip[x] = dot(every, select[...]).astype(BF16)

    member, c = strip_place(iota((COLS, COLS), 0))
    left, right = (c >= 3) & (c < 6), (c >= 12) & (c < 15)
    spot = jnp.where(left, 3 * member + c - 3, jnp.where(right, HALF + 3 * member + c - 12, -1000))
    for group in range(4):
        sides = jnp.zeros((PAD, COLS), F32)
        for j in range(4):
            sides = sides + dot(strip[group * 4 + j], one_hot(iota((COLS, COLS), 1) == spot + 30 * j))
        side_l[group] = sides[:, :HALF]
        side_r[group] = sides[:, HALF:]


def arrange(ensemble):
    y = np.arange(COLS)
    perm_y = np.zeros((DUO, DUO))
    for which in range(2):
        perm_y[which * COLS + y, y % 4 * HALF + which * QUARTER + y // 4] = 1
    i = np.arange(256)
    perm_r = np.zeros((256, 256))
    perm_r[i % 16 * 16 + i // 16, i] = 1
    spec = pl.BlockSpec(memory_space=pltpu.VMEM)
    return pl.pallas_call(
        arrange_kernel,
        name="arrange",
        out_shape=(
            jax.ShapeDtypeStruct((DUOS, ROWS, PAD, DUO), BF16),
            jax.ShapeDtypeStruct((DUOS, EDGE, PAD, DUO), F32),
            jax.ShapeDtypeStruct((DUOS, EDGE, PAD, DUO), F32),
            jax.ShapeDtypeStruct((ROWS, PAD, COLS), BF16),
            jax.ShapeDtypeStruct((4, PAD, HALF), F32),
            jax.ShapeDtypeStruct((4, PAD, HALF), F32),
        ),
        in_specs=[pl.BlockSpec(memory_space=pl.ANY), spec, spec],
        out_specs=(spec,) * 6,
        scratch_shapes=[
            pltpu.VMEM((4, LEV * ROWS, COLS), BF16),
            pltpu.VMEM((PAD * ROWS, DUO), BF16),
            pltpu.VMEM((DUOS * DUO, COLS), BF16),
            pltpu.SemaphoreType.DMA((4,)),
        ],
        compiler_params=params(),
        cost_estimate=cost(10**10, 25 * 10**6),
    )(ensemble.reshape(MEM, LEV * ROWS, COLS), jnp.asarray(perm_y, BF16), jnp.asarray(perm_r, BF16))


KTILE = 1024


def scatter_kernel(incoming, ens_l, ens_r, out, wide, side_l, side_r, turned, hot1, hot2, acc):
    turned[...] = incoming[...].T
    acc[...] = jnp.zeros_like(acc)
    rows1 = iota((4 * PAD, HALF), 0)
    rows2 = iota((4 * COLS, HALF), 0)

    @pl.loop(0, CAP // 8)
    def _(j):
        first = pl.multiple_of(j * 8, 8)
        values = turned[pl.ds(first, 8), :]
        cells = turned[pl.ds(CAP + first, 8), :].astype(I32)
        for q in range(8):
            at = slice(q * HALF, (q + 1) * HALF)
            cell = cells[q : q + 1, :]
            key1 = ((cell >> 10) & 3) * PAD + (cell >> 12)
            hit = rows1 == key1
            for p, piece in enumerate(split(values[q : q + 1, :], 2)):
                hot1[p * 4 * PAD : (p + 1) * 4 * PAD, at] = jnp.where(hit, piece.astype(F32), 0.0).astype(BF16)
            hot2[:, at] = one_hot(rows2 == (cell & 1023))
        for n in range(4):
            cols = slice(n * COLS, (n + 1) * COLS)
            acc[:, cols] += dot_nt(hot1[...], hot2[cols, :])

    y = natural(iota((COLS, COLS), 0))
    lane = iota((COLS, COLS), 1)
    place = jnp.where(y < 3, y, jnp.where(y >= 253, HALF + y - 253, -1000))
    packed = jnp.zeros((PAD, COLS), F32)
    for x in range(ROWS):
        cols = slice(x % 4 * COLS, (x % 4 + 1) * COLS)
        level = x // 4 * PAD
        value = acc[level : level + PAD, cols] + acc[4 * PAD + level : 4 * PAD + level + PAD, cols]
        out[x] = value
        wide[x] = widen(value)
        select = one_hot(lane == place + 3 * x)
        for piece in split(value, 2):
            packed = packed + dot(piece, select)
    side_l[:4] = ens_l[...]
    side_r[:4] = ens_r[...]
    side_l[4] = packed[:, :HALF]
    side_r[4] = packed[:, HALF:]


def scatter(incoming, ens_l, ens_r):
    spec = pl.BlockSpec(memory_space=pltpu.VMEM)
    return pl.pallas_call(
        scatter_kernel,
        name="scatter",
        out_shape=(
            jax.ShapeDtypeStruct((ROWS, PAD, COLS), F32),
            jax.ShapeDtypeStruct((ROWS, PAD, DUO), F32),
            jax.ShapeDtypeStruct((5, PAD, HALF), F32),
            jax.ShapeDtypeStruct((5, PAD, HALF), F32),
        ),
        in_specs=[spec] * 3,
        out_specs=(spec,) * 4,
        scratch_shapes=[
            pltpu.VMEM((HALF, DEV), F32),
            pltpu.VMEM((8 * PAD, KTILE), BF16),
            pltpu.VMEM((4 * COLS, KTILE), BF16),
            pltpu.VMEM((8 * PAD, 4 * COLS), F32),
        ],
        compiler_params=params(),
        cost_estimate=cost(10**10, 2 * 10**6),
    )(incoming, ens_l, ens_r)


def strips_kernel(strip, adjoint, left, right, ens_out, out, up, down):
    member, member_c = strip_place(iota((COLS, COLS), 1))
    y = natural(iota((COLS, COLS), 0))
    own = one_hot(member_c == jnp.where(y < 6, 3 + y, jnp.where(y >= 250, y - 241, -2)))
    from_lane = iota((HALF, COLS), 0)
    member_c, member = member_c[:HALF], member[:HALF]
    pieces = [split(side[4], 2) for side in (left, right)]
    for x in range(ROWS):
        value = strip[x].astype(F32)
        first = x % 4 * 30 + 3 * member
        for side, shift in ((left, 0), (right, 15)):
            inside = (member_c >= shift) & (member_c < shift + 3)
            spot = one_hot(inside & (from_lane == first + member_c - shift))
            value = value + dot(side[x // 4].astype(BF16), spot)
        ens_out[x] = value.astype(BF16)
        if x < EDGE:
            up[2, x] = value
        if x >= ROWS - EDGE:
            down[2, x - (ROWS - EDGE)] = value
        value = jnp.zeros((PAD, COLS), F32)
        for piece in split(adjoint[x], 2):
            value = value + dot(piece, own)
        for side, shift in ((pieces[0], 0), (pieces[1], 15)):
            inside = (member_c >= shift) & (member_c < shift + 3)
            spot = one_hot(inside & (from_lane == 3 * x + member_c - shift))
            for piece in side:
                value = value + dot(piece, spot)
        out[x] = value
        if x < EDGE:
            up[0, x] = adjoint[x]
            up[1, x] = value
        if x >= ROWS - EDGE:
            down[0, x - (ROWS - EDGE)] = adjoint[x]
            down[1, x - (ROWS - EDGE)] = value


def strips(strip, adjoint, left, right):
    spec = pl.BlockSpec(memory_space=pltpu.VMEM)
    return pl.pallas_call(
        strips_kernel,
        name="strips",
        out_shape=(
            jax.ShapeDtypeStruct((ROWS, PAD, COLS), BF16),
            jax.ShapeDtypeStruct((ROWS, PAD, COLS), F32),
            jax.ShapeDtypeStruct((3, EDGE, PAD, COLS), F32),
            jax.ShapeDtypeStruct((3, EDGE, PAD, COLS), F32),
        ),
        in_specs=[spec] * 4,
        out_specs=(spec,) * 4,
        compiler_params=params(),
        cost_estimate=cost(10**9, 4 * 10**6),
    )(strip, adjoint, left, right)


def beside_permuted(value):
    even, odd = value[:, :HALF], value[:, HALF:]
    return jnp.concatenate([odd + pltpu.roll(odd, 1, 1), even + pltpu.roll(even, HALF - 1, 1)], axis=1)


def beside_duo(value):
    p = [value[:, i * HALF : (i + 1) * HALF] for i in range(4)]
    return jnp.concatenate(
        [pltpu.roll(p[3], 1, 1) + p[1], p[0] + p[2], p[1] + p[3], p[2] + pltpu.roll(p[0], HALF - 1, 1)], axis=1
    )


def total(terms):
    result = None
    for term in terms:
        if term is not None:
            result = term if result is None else result + term
    return result


def diffuse(get, given, wanted, beside, emit, mask=None):
    rows = [{} for _ in range(EDGE + 1)]
    for x in range(min(wanted) - EDGE, max(wanted) + EDGE + 1):
        if x in given:
            rows[0][x] = get(x)
        for step in range(1, EDGE + 1):
            at, reach, older = x - step, EDGE - step, rows[step - 1]
            if not min(wanted) - reach <= at <= max(wanted) + reach:
                continue
            terms = [older.get(at - 1), older.get(at + 1)]
            if at in older:
                terms += [beside(older[at]), older[at] * SELF]
            value = total(terms)
            if value is None:
                continue
            if step == EDGE:
                emit(at, value)
            else:
                rows[step][at] = value if mask is None else mask(at, value)


def put_split(ref, index, at, value):
    top = value.astype(BF16)
    ref[index, at, :] = top
    ref[index, pl.ds(at.start + PAD, 16), :] = (value - top.astype(F32)).astype(BF16)


def mix(weights, field):
    both = dot(weights, field)
    return both[:PAD] + both[PAD:]


INNER = ROWS - 2 * EDGE


def inner_kernel(start, count, ens, adj, weights, place, *refs):
    border, out, field, first = refs[-4:]
    out[...] = refs[0][...] if start else jnp.zeros_like(out)
    top_open = jnp.where(place[0] == 0, 0.0, 1.0)
    bottom_open = jnp.where(place[0] == place[2], 0.0, 1.0)

    def mask(x, value):
        if x < 0:
            return value * top_open
        if x >= ROWS:
            return value * bottom_open
        return value

    @pl.loop(0, count)
    def _(step):
        k = start + step

        @pl.loop(0, PAD // 16)
        def _(group):
            at = pl.ds(pl.multiple_of(group * 16, 16), 16)

            for part in range(2):
                eight = pl.ds(pl.multiple_of(group * 16 + part * 8, 8), 8)

                def get(x):
                    return ens[k, x, at, :].astype(F32)[part * 8 : part * 8 + 8, :] * adj[x, eight, :]

                def emit(x, value):
                    if not EDGE <= x < ROWS - EDGE:
                        border[step, x if x < EDGE else x - INNER, eight, :] = value
                    elif part == 0:
                        first[x - EDGE] = value
                    else:
                        put_split(field, x - EDGE, at, jnp.concatenate([first[x - EDGE], value], axis=0))

                diffuse(get, range(ROWS), range(ROWS), beside_duo, emit, mask)

        for x in range(INNER):
            out[x] += ens[k, x + EDGE].astype(F32) * mix(weights[...], field[x])


def inner(ens, adj, weights, place, start, count, before=()):
    spec = pl.BlockSpec(memory_space=pltpu.VMEM)
    return pl.pallas_call(
        lambda *refs: inner_kernel(start, count, *refs),
        name="inner",
        out_shape=(
            jax.ShapeDtypeStruct((count, 2 * EDGE, PAD, DUO), F32),
            jax.ShapeDtypeStruct((INNER, PAD, DUO), F32),
        ),
        in_specs=[spec] * 3 + [pl.BlockSpec(memory_space=pltpu.SMEM)] + [spec] * len(before),
        out_specs=(spec,) * 2,
        scratch_shapes=[pltpu.VMEM((INNER, 2 * PAD, DUO), BF16), pltpu.VMEM((INNER, 8, DUO), F32)],
        compiler_params=params(),
        cost_estimate=cost(count * 2 * 10**9, count * 2 * 10**6),
    )(ens, adj, weights, place, *before)


def outer_kernel(ens, halo_t, halo_b, adj_t, adj_b, border0, border1, weights, out, field, first, wide):
    out[...] = jnp.zeros_like(out)
    for x in range(EDGE):
        wide[x] = widen(adj_t[0, x])
        wide[EDGE + x] = widen(adj_b[0, x])

    for border, start in ((border0, 0), (border1, FIRST)):

        @pl.loop(0, border.shape[0])
        def _(step):
            k = start + step

            @pl.loop(0, PAD // 16)
            def _(group):
                at = pl.ds(pl.multiple_of(group * 16, 16), 16)

                for part in range(2):
                    eight = pl.ds(pl.multiple_of(group * 16 + part * 8, 8), 8)

                    def emit(x, value):
                        value = value + border[step, x, eight, :]
                        if part == 0:
                            first[x] = value
                        else:
                            put_split(field, x, at, jnp.concatenate([first[x], value], axis=0))

                    def get_t(x):
                        return halo_t[k, x + EDGE, eight, :] * wide[x + EDGE, eight, :]

                    def get_b(x):
                        return halo_b[k, x - 2 * EDGE, eight, :] * wide[x - EDGE, eight, :]

                    diffuse(get_t, range(-EDGE, 0), range(EDGE), beside_duo, emit)
                    diffuse(get_b, range(2 * EDGE, 3 * EDGE), range(EDGE, 2 * EDGE), beside_duo, emit)

            for x in range(2 * EDGE):
                row = x if x < EDGE else x + INNER
                out[x] += ens[k, row].astype(F32) * mix(weights[...], field[x])


def outer(ens, halo_t, halo_b, adj_t, adj_b, border0, border1, weights):
    spec = pl.BlockSpec(memory_space=pltpu.VMEM)
    return pl.pallas_call(
        outer_kernel,
        name="outer",
        out_shape=jax.ShapeDtypeStruct((2 * EDGE, PAD, DUO), F32),
        in_specs=[spec] * 8,
        out_specs=spec,
        scratch_shapes=[
            pltpu.VMEM((2 * EDGE, 2 * PAD, DUO), BF16),
            pltpu.VMEM((2 * EDGE, 8, DUO), F32),
            pltpu.VMEM((2 * EDGE, PAD, DUO), F32),
        ],
        compiler_params=params(),
        cost_estimate=cost(MEM * 10**9, MEM * 3 * 10**6),
    )(ens, halo_t, halo_b, adj_t, adj_b, border0, border1, weights)


def edge_kernel(strip, adj, halo_t, halo_b, weights, place, inside, border, out, field):
    top_open = jnp.where(place[0] == 0, 0.0, 1.0)
    bottom_open = jnp.where(place[0] == place[2], 0.0, 1.0)
    left_open = jnp.where(place[1] == 0, 0.0, 1.0)
    right_open = jnp.where(place[1] == place[3], 0.0, 1.0)

    @pl.loop(0, PAD // 16)
    def _(group):
        at = pl.ds(pl.multiple_of(group * 16, 16), 16)
        c = strip_place(iota((16, COLS), 1))[1]
        lanes = jnp.where(c < 3, left_open, jnp.where(c >= 15, right_open, 1.0))

        def mask(x, value):
            value = value * lanes
            if x < 0:
                return value * top_open
            if x >= ROWS:
                return value * bottom_open
            return value

        def get(x):
            if x < 0:
                return halo_t[2, x + EDGE, at, :] * halo_t[1, x + EDGE, at, :]
            if x >= ROWS:
                return halo_b[2, x - ROWS, at, :] * halo_b[1, x - ROWS, at, :]
            return strip[x, at, :].astype(F32) * adj[x, at, :]

        def emit(x, value):
            put_split(field, x, at, value)

        diffuse(get, range(-EDGE, ROWS + EDGE), range(ROWS), beside_permuted, emit, mask)

    c = strip_place(iota((COLS, COLS), 0))[1]
    spot = jnp.where((c >= 3) & (c < 6), c - 3, jnp.where((c >= 12) & (c < 15), 241 + c, -1))
    collect = one_hot(spot == natural(iota((COLS, COLS), 1)))
    y = natural(iota((PAD, COLS), 1))
    middle = (y >= EDGE) & (y < COLS - EDGE)
    for x in range(ROWS):
        if EDGE <= x < ROWS - EDGE:
            value = inside[x - EDGE]
        else:
            value = border[x if x < EDGE else x - INNER]
        value = jnp.where(middle, fold(value), 0.0)
        product = strip[x].astype(F32) * mix(weights[...], field[x])
        for piece in split(product, 2):
            value = value + dot(piece, collect)
        out[x] = value * SCALE


def edge(strip, adj, halo_t, halo_b, weights, place, inside, border):
    spec = pl.BlockSpec(memory_space=pltpu.VMEM)
    return pl.pallas_call(
        edge_kernel,
        name="edge",
        out_shape=jax.ShapeDtypeStruct((ROWS, PAD, COLS), F32),
        in_specs=[spec] * 5 + [pl.BlockSpec(memory_space=pltpu.SMEM)] + [spec] * 2,
        out_specs=spec,
        scratch_shapes=[pltpu.VMEM((ROWS, 2 * PAD, COLS), BF16)],
        compiler_params=params(),
        cost_estimate=cost(4 * 10**9, 8 * 10**6),
    )(strip, adj, halo_t, halo_b, weights, place, inside, border)


def gather_kernel(field, incoming, out, turned, table, hot, picked):
    turned[...] = incoming[...].T
    picked[...] = jnp.zeros_like(picked)
    for x in range(ROWS):
        cols = slice(x % 4 * COLS, (x % 4 + 1) * COLS)
        for p, piece in enumerate(split(field[x], 2)):
            first = (p * 4 + x // 4) * PAD
            table[first : first + PAD, cols] = piece
    rows1 = iota((4 * PAD, COLS), 0)
    rows2 = iota((4 * COLS, COLS), 0)

    @pl.loop(0, CAP // 8)
    def _(j):
        first = pl.multiple_of(j * 8, 8)
        cells = turned[pl.ds(CAP + first, 8), :].astype(I32)
        lines = []
        for q in range(0, 8, 2):
            cell = jnp.concatenate([cells[q : q + 1, :], cells[q + 1 : q + 2, :]], axis=1)
            hot[...] = one_hot(rows2 == (cell & 1023))
            found = dot(table[...], hot[...])
            key1 = ((cell >> 10) & 3) * PAD + (cell >> 12)
            found = jnp.where(rows1 == key1, found[: 4 * PAD] + found[4 * PAD :], 0.0)
            found = jnp.sum(found, axis=0, keepdims=True)
            lines += [found[:, :HALF], found[:, HALF:]]
        picked[pl.ds(first, 8), :] = jnp.concatenate(lines, axis=0)

    out[...] = picked[...].T


def gather(field, incoming):
    spec = pl.BlockSpec(memory_space=pltpu.VMEM)
    return pl.pallas_call(
        gather_kernel,
        name="gather",
        out_shape=jax.ShapeDtypeStruct((DEV, HALF), F32),
        in_specs=[spec] * 2,
        out_specs=spec,
        scratch_shapes=[
            pltpu.VMEM((HALF, DEV), F32),
            pltpu.VMEM((8 * PAD, 4 * COLS), BF16),
            pltpu.VMEM((4 * COLS, COLS), BF16),
            pltpu.VMEM((HALF, DEV), F32),
        ],
        compiler_params=params(),
        cost_estimate=cost(10**10, 2 * 10**6),
    )(field, incoming)


def restore_kernel(field, perm_y, perm_r, out, rows):
    for x in range(ROWS):
        value = field[x]
        high, low = split(value, 2)
        rows[x] = dot(high, perm_y[...]) + dot(low, perm_y[...])
    for b in range(6):
        block = jnp.concatenate([rows[x, b * 16 : (b + 1) * 16, :] for x in range(ROWS)], axis=0)
        high, low = split(block, 2)
        value = dot(perm_r[...], high) + dot(perm_r[...], low)
        if b < 5:
            out[b * 256 : (b + 1) * 256, :] = value
        else:
            out[1280:1440, :] = value[:160]


def restore(field):
    y = np.arange(COLS)
    perm_y = np.zeros((COLS, COLS))
    perm_y[y % 4 * QUARTER + y // 4, y] = 1
    i = np.arange(256)
    perm_r = np.zeros((256, 256))
    perm_r[i, i % 16 * 16 + i // 16] = 1
    spec = pl.BlockSpec(memory_space=pltpu.VMEM)
    return pl.pallas_call(
        restore_kernel,
        name="restore",
        out_shape=jax.ShapeDtypeStruct((LEV * ROWS, COLS), F32),
        in_specs=[spec] * 3,
        out_specs=spec,
        scratch_shapes=[pltpu.VMEM((ROWS, PAD, COLS), F32)],
        compiler_params=params(),
        cost_estimate=cost(10**9, 3 * 10**6),
    )(field, jnp.asarray(perm_y, BF16), jnp.asarray(perm_r, BF16)).reshape(LEV, ROWS, COLS)


def forward(value, axis):
    size = lax.axis_size(axis)
    return lax.ppermute(value, axis, [(i, i + 1) for i in range(size - 1)])


def backward(value, axis):
    size = lax.axis_size(axis)
    return lax.ppermute(value, axis, [(i + 1, i) for i in range(size - 1)])


FIRST = 2


def body(ensemble, vertical_weights, dual_vector, observed_column, observed_level, active_count):
    place = jnp.stack(
        [lax.axis_index("gx"), lax.axis_index("gy"), lax.axis_size("gx") - 1, lax.axis_size("gy") - 1]
    ).astype(I32)
    outgoing, target, rank, weights = pack(
        active_count, dual_vector, observed_column, observed_level, vertical_weights
    )
    incoming = lax.all_to_all(outgoing, ("gx", "gy"), split_axis=0, concat_axis=0, tiled=True)

    ens, ens_up, ens_down, strip, ens_l, ens_r = arrange(ensemble)
    halo_t = forward(ens_down, "gx")
    halo_b = backward(ens_up, "gx")

    adj, wide, side_l, side_r = scatter(incoming, ens_l, ens_r)
    from_left = forward(side_r, "gy")
    from_right = backward(side_l, "gy")
    border0, inside = inner(ens, wide, weights, place, 0, FIRST)
    strip, adj_strip, up, down = strips(strip, adj, from_left, from_right)
    top = forward(down, "gx")
    bottom = backward(up, "gx")
    border1, inside = inner(ens, wide, weights, place, FIRST, DUOS - FIRST, (inside,))

    outside = outer(ens, halo_t, halo_b, top, bottom, border0, border1, weights)
    field = edge(strip, adj_strip, top, bottom, weights, place, inside, outside)
    picked = gather(field, incoming)
    back = lax.all_to_all(picked, ("gx", "gy"), split_axis=0, concat_axis=0, tiled=True)
    increment = restore(field)
    obs_product = unpack(back, target, rank)
    return (increment, obs_product)


def solution(mesh):
    placed = (
        P(None, None, "gx", "gy"),
        P(),
        P(("gx", "gy")),
        P(("gx", "gy")),
        P(("gx", "gy")),
        P(("gx", "gy")),
    )
    return jax.shard_map(
        body,
        mesh=mesh,
        in_specs=placed,
        out_specs=(P(None, "gx", "gy"), P(("gx", "gy"))),
        check_vma=False,
    )
```

time: 218 us -> 179 us (0.82)
  Pallas kernels: 143 us -> 86.3 us
  blocking collectives: 0 us -> 32.2 us
  starting transfers between devices: 48.4 us -> 29.6 us
  other arithmetic: 7.06 us -> 0.08 us
  waiting for transfers between devices: 7.75 us -> 14.4 us
  local copies, waits for them, and re-layouts: 9.78 us -> 14.4 us
    pallas_call x6 -> x5, Pallas kernels: 95.3 us -> 48.5 us  [the longest x1 18.9 us: arrange(): pl.pallas_call(arrange_kernel, name='arrange', out_shape=(jax.ShapeDtypeS...]
    all_to_all x0 -> x1, blocking collectives: none -> 32.2 us  [body(): lax.all_to_all(outgoing, ('gx', 'gy'), split_axis=0, concat_axis=0, tiled...]
    all_to_all x1 -> x0, starting transfers between devices: 11.5 us -> none  [body(): lax.all_to_all(outgoing, ('gx', 'gy'), split_axis=0, concat_axis=0, tiled...]
    unnamed x22 -> x40, local copies, waits for them, and re-layouts: 3.82 us -> 14.4 us
    concatenate x2 -> x0, other arithmetic: 5.82 us -> none  [the longest x1 5.1 us: body(): border = jnp.concatenate([border0, border1], axis=0)]
    slice x4 -> x0, local copies, waits for them, and re-layouts: 4.06 us -> none  [the longest x1 1.47 us: body(): from_right = backward(side[:1], 'gy')]
    ppermute x5 -> x3, starting transfers between devices: 9.32 us -> 5.31 us  [backward(): return lax.ppermute(value, axis, [(i + 1, i) for i in range(size - 1)])]
    pallas_call x1, Pallas kernels: 8.73 us -> 4.96 us  [edge(): pl.pallas_call(edge_kernel, name='edge', out_shape=jax.ShapeDtypeStruct((...]
  transfers between devices with their start and end apart: 12 -> 7, of which waited for: 2 -> 3; matrix products, arithmetic and copies ran while one was open for 6% -> 0% of each run, Pallas kernels for 53% -> 22%
where the time goes in v2:
time: 179 us
  Pallas kernels  86.3 us (48%)
  blocking collectives  32.2 us (18%)
  starting transfers between devices  29.6 us (17%)
  local copies, waits for them, and re-layouts  14.4 us (8%)
  waiting for transfers between devices  14.4 us (8%)
    all_to_all x1, blocking collectives, body(): lax.all_to_all(outgoing, ('gx', 'gy'), split_axis=0, concat_axis=0, tiled...  32.2 us
    pallas_call x1, Pallas kernels, arrange(): pl.pallas_call(arrange_kernel, name='arrange', out_shape=(jax.ShapeDtypeS...  18.9 us
    pallas_call x2, Pallas kernels, inner(): pl.pallas_call(lambda *refs: inner_kernel(start, count, *refs), name='inn...  16.7 us
    pallas_call x1, Pallas kernels, scatter(): pl.pallas_call(scatter_kernel, name='scatter', out_shape=(jax.ShapeDtypeS...  15.3 us
    unnamed x40, local copies, waits for them, and re-layouts  14.4 us
    ppermute x3, starting transfers between devices, forward(): return lax.ppermute(value, axis, [(i, i + 1) for i in range(size - 1)])  14.2 us
    pallas_call x1, Pallas kernels, gather(): pl.pallas_call(gather_kernel, name='gather', out_shape=jax.ShapeDtypeStru...  11.9 us
    all_to_all x1, starting transfers between devices, body(): lax.all_to_all(picked, ('gx', 'gy'), split_axis=0, concat_axis=0, tiled=T...  10 us
  transfers between devices with their start and end apart: 7, of which 3 were waited for; matrix products, arithmetic and copies ran while one was open for 0% of the time, Pallas kernels for 22%

profile of v2, /device:TPU:1, one launch (start us, length us, event | category | flops | bytes accessed | tf_op | source)
XLA Modules:
  0.0 178.5 jit_solution(1759269764830844564)
XLA Ops:
  0.6 3.1 %copy-done = bf16[10,90,16,256]{3,2,1,0:T(8,128)(2,1)S(1)} copy-done((bf16[10,90,16,256]{3,2,1,0:T(8,128)(2,1)S(1)}, bf16[10,90,16,256]{3,2,1,0:T(8,128)(2,1)}, u32[]{:S(2)}) %copy-start) | copy-done | bytes 7372824
  5.7 18.9 %arrange.1 = (bf16[5,16,96,512]{3,2,1,0:T(8,128)(2,1)S(1)}, f32[5,3,96,512]{3,2,1,0:T(8,128)}, f32[5,3,96,512]{3,2,1,0:T(8,128)}, bf16[16,96,256]{2,1,0:T(8,128)...) custom-call(bf16[10,1440,256]{2,1,0:T(8,128)(2,1)S(1)} %bitcast.20, bf16[512,512]{1,0:T(8,128)(2,1)S(1)} %copy-done.5, ...), custom_call_target="tpu_custom_call" | custom-call | flops 10000000000 | bytes 25000000 | tf_op jit(solution)/shard_map/arrange/pallas_call | solution.py:237
  24.6 4.9 %collective-permute-start.4 = (f32[5,3,96,512]{3,2,1,0:T(8,128)}, f32[5,3,96,512]{3,2,1,0:T(8,128)S(1)}, u32[]{:S(2)}, u32[]{:S(2)}) collective-permute-start(f32[5,3,96,512]{3,2,1,0:T(8,128)} %get-tuple-element.40), channel_id=1, source_target_pairs={{0,16},{16,32},{32,48},{48,64},{64,80},{80,96},{96,112},{1,17},{17... | collective-permute-start | bytes 8847368 | tf_op jit(solution)/shard_map/ppermute | solution.py:703
  29.5 1.9 %collective-permute-start.5 = (f32[5,3,96,512]{3,2,1,0:T(8,128)}, f32[5,3,96,512]{3,2,1,0:T(8,128)}, u32[]{:S(2)}, u32[]{:S(2)}) collective-permute-start(f32[5,3,96,512]{3,2,1,0:T(8,128)} %get-tuple-element.41), channel_id=1, source_target_pairs={{16,0},{32,16},{48,32},{64,48},{80,64},{96,80},{112,96},{17,1},{33... | collective-permute-start | bytes 8847368 | tf_op jit(solution)/shard_map/ppermute | solution.py:708
  32.1 2.0 %pack.1 = (f32[128,128]{1,0:T(8,128)S(1)}, s32[16,128]{1,0:T(8,128)S(1)}, s32[16,128]{1,0:T(8,128)S(1)}, bf16[192,192]{1,0:T(8,128)(2,1)S(1)}) custom-call(s32[1]{0:T(128)S(6)} %copy.15.count, f32[16,128]{1,0:T(8,128)S(1)} %bitcast.21, s32[16,128]{1,0:T(8,128)S(1)} %bitcast.22, s32[16,128]{1,0:T(8,128)S(1)} %bitcast.23, bf16[128,256]{1,0:T(8,128)(2,1)S(1)} %copy-done.9, ...), custom_call_target="tpu_custom_call" | custom-call | flops 1000000000 | bytes 1000000 | tf_op jit(solution)/shard_map/pack/pallas_call | solution.py:105
  34.8 32.2 %all_to_all.22 = f32[128,1,128]{2,1,0:T(1,128)S(1)} all-to-all(f32[128,1,128]{2,1,0:T(1,128)S(1)} %bitcast.19), channel_id=1, replica_groups=mesh['gx'=8,'gy'=16] {'gx','gy'}, dimensions={0} | all-to-all | bytes 131072 | tf_op jit(solution)/shard_map/all_to_all | solution.py:721
  67.0 15.3 %scatter.1 = (f32[16,96,256]{2,1,0:T(8,128)S(1)}, f32[16,96,512]{2,1,0:T(8,128)S(1)}, f32[5,96,128]{2,1,0:T(8,128)S(1)}, f32[5,96,128]{2,1,0:T(8,128)}) custom-call(f32[128,128]{1,0:T(8,128)S(1)} %bitcast.16, f32[4,96,128]{2,1,0:T(8,128)S(1)} %get-tuple-element.26.ens_l, f32[4,96,128]{2,1,0:T(8,128)S(1)} %get-tuple-element.27.ens_r), custom_call_target="tpu_custom_call" | custom-call | flops 10000000000 | bytes 2000000 | tf_op jit(solution)/shard_map/scatter/pallas_call | solution.py:308
  83.5 1.8 copy-done.16
  85.3 3.2 %collective-permute-start = (f32[5,96,128]{2,1,0:T(8,128)}, f32[5,96,128]{2,1,0:T(8,128)S(1)}, u32[]{:S(2)}, u32[]{:S(2)}) collective-permute-start(f32[5,96,128]{2,1,0:T(8,128)} %get-tuple-element.29), channel_id=1, source_target_pairs={{0,1},{1,2},{2,3},{3,4},{4,5},{5,6},{6,7},{7,8},{8,9},{9,10},{10,1... | collective-permute-start | bytes 737288 | tf_op jit(solution)/shard_map/ppermute | solution.py:703
  89.9 3.7 %collective-permute-done.left = f32[5,96,128]{2,1,0:T(8,128)S(1)} collective-permute-done((f32[5,96,128]{2,1,0:T(8,128)}, f32[5,96,128]{2,1,0:T(8,128)S(1)}, u32[]{:S(2)}, u32[]{:S(2)}) %collective-permute-start) | collective-permute-done | bytes 245792 | tf_op jit(solution)/shard_map/ppermute | solution.py:703
  93.5 3.6 %collective-permute-done.1.right = f32[5,96,128]{2,1,0:T(8,128)} collective-permute-done((f32[5,96,128]{2,1,0:T(8,128)S(1)}, f32[5,96,128]{2,1,0:T(8,128)}, u32[]{:S(2)}, u32[]{:S(2)}) %collective-permute-start.1) | collective-permute-done | bytes 245792 | tf_op jit(solution)/shard_map/ppermute | solution.py:708
  97.1 1.4 copy-done.11
  99.7 3.2 %strips.1 = (bf16[16,96,256]{2,1,0:T(8,128)(2,1)S(1)}, f32[16,96,256]{2,1,0:T(8,128)S(1)}, f32[3,3,96,256]{3,2,1,0:T(8,128)S(1)}, f32[3,3,96,256]{3,2,1,0:T(8,128)S(1)}) custom-call(bf16[16,96,256]{2,1,0:T(8,128)(2,1)S(1)} %copy-done.13, f32[16,96,256]{2,1,0:T(8,128)S(1)} %copy-done.11, f32[5,96,128]{2,1,0:T(8,128)S(1)} %collective-permute-done.left, ...), custom_call_target="tpu_custom_call" | custom-call | flops 1000000000 | bytes 4000000 | tf_op jit(solution)/shard_map/strips/pallas_call | solution.py:368
  102.8 6.1 %collective-permute-start.2 = (f32[3,3,96,256]{3,2,1,0:T(8,128)S(1)}, f32[3,3,96,256]{3,2,1,0:T(8,128)S(1)}, u32[]{:S(2)}, u32[]{:S(2)}) collective-permute-start(f32[3,3,96,256]{3,2,1,0:T(8,128)S(1)} %get-tuple-element.33), channel_id=1, source_target_pairs={{0,16},{16,32},{32,48},{48,64},{64,80},{80,96},{96,112},{1,17},{17... | collective-permute-start | bytes 2654216 | tf_op jit(solution)/shard_map/ppermute | solution.py:703
  109.0 2.1 %collective-permute-start.3 = (f32[3,3,96,256]{3,2,1,0:T(8,128)S(1)}, f32[3,3,96,256]{3,2,1,0:T(8,128)S(1)}, u32[]{:S(2)}, u32[]{:S(2)}) collective-permute-start(f32[3,3,96,256]{3,2,1,0:T(8,128)S(1)} %get-tuple-element.34), channel_id=1, source_target_pairs={{16,0},{32,16},{48,32},{64,48},{80,64},{96,80},{112,96},{17,1},{33... | collective-permute-start | bytes 2654216 | tf_op jit(solution)/shard_map/ppermute | solution.py:708
  111.1 3.2 %copy-done.15 = bf16[5,16,96,512]{3,2,1,0:T(8,128)(2,1)S(1)} copy-done((bf16[5,16,96,512]{3,2,1,0:T(8,128)(2,1)S(1)}, bf16[5,16,96,512]{3,2,1,0:T(8,128)(2,1)}, u32[]{:S(2)}) %copy-start.15) | copy-done | bytes 7864344
  114.3 6.8 %inner.2 = (f32[2,6,96,512]{3,2,1,0:T(8,128)S(1)}, f32[10,96,512]{2,1,0:T(8,128)S(1)}) custom-call(bf16[5,16,96,512]{3,2,1,0:T(8,128)(2,1)S(1)} %copy-done.15, f32[16,96,512]{2,1,0:T(8,128)S(1)} %copy-done.17, bf16[192,192]{1,0:T(8,128)(2,1)S(1)} %copy-done.19, s32[4]{0:T(128)S(1)} %pad_add_fusion.refs_3_.place), custom_call_target="tpu_custom_call" | custom-call | flops 4000000000 | bytes 4000000 | tf_op jit(solution)/shard_map/inner/pallas_call | solution.py:482
  121.1 10.0 %inner.3 = (f32[3,6,96,512]{3,2,1,0:T(8,128)S(1)}, f32[10,96,512]{2,1,0:T(8,128)S(1)}) custom-call(bf16[5,16,96,512]{3,2,1,0:T(8,128)(2,1)S(1)} %copy-done.15, f32[16,96,512]{2,1,0:T(8,128)S(1)} %copy-done.17, bf16[192,192]{1,0:T(8,128)(2,1)S(1)} %copy-done.19, s32[4]{0:T(128)S(1)} %pad_add_fusion.refs_3_.place, f32[10,96,512]{2,1,0:T(8,128)S(1)} %get-tuple-element.38.refs_4_), custom_call_target="tpu_custom_call" | custom-call | flops 6000000000 | bytes 6000000 | tf_op jit(solution)/shard_map/inner/pallas_call | solution.py:482
  131.1 9.7 %outer.1.border = f32[6,96,512]{2,1,0:T(8,128)S(1)} custom-call(bf16[5,16,96,512]{3,2,1,0:T(8,128)(2,1)S(1)} %copy-done.15, f32[5,3,96,512]{3,2,1,0:T(8,128)S(1)} %collective-permute-done.4.halo_t, f32[5,3,96,512]{3,2,1,0:T(8,128)} %collective-permute-done.5.halo_b, f32[3,3,96,256]{3,2,1,0:T(8,128)S(1)} %collective-permute-done.2.adj_t.halo_t, ...), custom_call_target="tpu_custom_call" | custom-call | flops 10000000000 | bytes 30000000 | tf_op jit(solution)/shard_map/outer/pallas_call | solution.py:539
  140.9 5.0 %edge.1.field = f32[16,96,256]{2,1,0:T(8,128)S(1)} custom-call(bf16[16,96,256]{2,1,0:T(8,128)(2,1)S(1)} %get-tuple-element.31.strip, f32[16,96,256]{2,1,0:T(8,128)S(1)} %get-tuple-element.32.adj, f32[3,3,96,256]{3,2,1,0:T(8,128)S(1)} %collective-permute-done.2.adj_t.halo_t, f32[3,3,96,256]{3,2,1,0:T(8,128)S(1)} %collective-permute-done.3.adj_b.halo_b, ...), custom_call_target="tpu_custom_call" | custom-call | flops 4000000000 | bytes 8000000 | tf_op jit(solution)/shard_map/edge/pallas_call | solution.py:606
  145.8 11.9 %gather.1 = f32[128,128]{1,0:T(8,128)} custom-call(f32[16,96,256]{2,1,0:T(8,128)S(1)} %edge.1.field, f32[128,128]{1,0:T(8,128)S(1)} %bitcast.17), custom_call_target="tpu_custom_call" | custom-call | flops 10000000000 | bytes 2000000 | tf_op jit(solution)/shard_map/gather/pallas_call | solution.py:649
  157.8 10.0 %all-to-all-start.1 = ((f32[128,1,128]{2,1,0:T(1,128)}), f32[128,1,128]{2,1,0:T(1,128)S(1)}, u32[]{:S(2)}, u32[]{:S(2)}) async-start(f32[128,1,128]{2,1,0:T(1,128)} %bitcast.11), calls=%async_computation.1 | async-start | bytes 131072 | tf_op jit(solution)/shard_map/all_to_all | solution.py:739
  167.8 2.4 %restore.1 = f32[1440,256]{1,0:T(8,128)} custom-call(f32[16,96,256]{2,1,0:T(8,128)S(1)} %edge.1.field, bf16[256,256]{1,0:T(8,128)(2,1)S(1)} %copy-done.8, bf16[256,256]{1,0:T(8,128)(2,1)S(1)} %copy-done.7), custom_call_target="tpu_custom_call" | custom-call | flops 1000000000 | bytes 3000000 | tf_op jit(solution)/shard_map/restore/pallas_call | solution.py:689
  170.2 7.1 %all-to-all-done.1 = f32[128,1,128]{2,1,0:T(1,128)S(1)} async-done(((f32[128,1,128]{2,1,0:T(1,128)}), f32[128,1,128]{2,1,0:T(1,128)S(1)}, u32[]{:S(2)}, u32[]{:S(2)}) %all-to-all-start.1) | async-done | bytes 65568 | tf_op jit(solution)/shard_map/all_to_all | solution.py:739
  (43 shorter events, 7.5 us)
Async XLA Ops:
  0.6 3.1 %copy-start = (bf16[10,90,16,256]{3,2,1,0:T(8,128)(2,1)S(1)}, bf16[10,90,16,256]{3,2,1,0:T(8,128)(2,1)}, u32[]{:S(2)}) copy-start(bf16[10,90,16,256]{3,2,1,0:T(8,128)(2,1)} %param.11) | copy-start | bytes 22118404
  5.7 26.4 %copy-start.1 = (f32[90,90]{1,0:T(8,128)S(1)}, f32[90,90]{1,0:T(8,128)}, u32[]{:S(2)}) copy-start(f32[90,90]{1,0:T(8,128)} %vertical.1) | copy-start | bytes 97204
  5.7 26.4 %copy-start.2 = (f32[2048]{0:T(1024)S(1)}, f32[2048]{0:T(1024)}, u32[]{:S(2)}) copy-start(f32[2048]{0:T(1024)} %param.13) | copy-start | bytes 24580
  5.7 26.4 %copy-start.3 = (s32[2048]{0:T(1024)S(1)}, s32[2048]{0:T(1024)}, u32[]{:S(2)}) copy-start(s32[2048]{0:T(1024)} %param.14) | copy-start | bytes 24580
  5.7 26.4 %copy-start.4 = (s32[2048]{0:T(1024)S(1)}, s32[2048]{0:T(1024)}, u32[]{:S(2)}) copy-start(s32[2048]{0:T(1024)} %param.15) | copy-start | bytes 24580
  5.7 26.4 %copy-start.9 = (bf16[128,256]{1,0:T(8,128)(2,1)S(1)}, bf16[128,256]{1,0:T(8,128)(2,1)}, u32[]{:S(2)}) copy-start(bf16[128,256]{1,0:T(8,128)(2,1)} %constant.21.clone.upper) | copy-start | bytes 196612
  24.6 57.8 %copy-start.12 = (bf16[16,96,256]{2,1,0:T(8,128)(2,1)}, bf16[16,96,256]{2,1,0:T(8,128)(2,1)S(1)}, u32[]{:S(2)}) copy-start(bf16[16,96,256]{2,1,0:T(8,128)(2,1)S(1)} %get-tuple-element.24.strip) | copy-start | bytes 2359300
  24.6 57.8 %copy-start.14 = (bf16[5,16,96,512]{3,2,1,0:T(8,128)(2,1)}, bf16[5,16,96,512]{3,2,1,0:T(8,128)(2,1)S(1)}, u32[]{:S(2)}) copy-start(bf16[5,16,96,512]{3,2,1,0:T(8,128)(2,1)S(1)} %get-tuple-element.36.refs_0_.ens) | copy-start | bytes 23592964
  24.6 106.5 %collective-permute-start.4 = (f32[5,3,96,512]{3,2,1,0:T(8,128)}, f32[5,3,96,512]{3,2,1,0:T(8,128)S(1)}, u32[]{:S(2)}, u32[]{:S(2)}) collective-permute-start(f32[5,3,96,512]{3,2,1,0:T(8,128)} %get-tuple-element.40), channel_id=1, source_target_pairs={{0,16},{16,32},{32,48},{48,64},{64,80},{80,96},{96,112},{1,17},{17... | collective-permute-start | bytes 8847368 | tf_op jit(solution)/shard_map/ppermute | solution.py:703
  29.5 101.6 %collective-permute-start.5 = (f32[5,3,96,512]{3,2,1,0:T(8,128)}, f32[5,3,96,512]{3,2,1,0:T(8,128)}, u32[]{:S(2)}, u32[]{:S(2)}) collective-permute-start(f32[5,3,96,512]{3,2,1,0:T(8,128)} %get-tuple-element.41), channel_id=1, source_target_pairs={{16,0},{32,16},{48,32},{64,48},{80,64},{96,80},{112,96},{17,1},{33... | collective-permute-start | bytes 8847368 | tf_op jit(solution)/shard_map/ppermute | solution.py:708
  82.3 1.2 copy-start.10
  83.5 1.8 copy-start.16
  85.3 8.2 %collective-permute-start = (f32[5,96,128]{2,1,0:T(8,128)}, f32[5,96,128]{2,1,0:T(8,128)S(1)}, u32[]{:S(2)}, u32[]{:S(2)}) collective-permute-start(f32[5,96,128]{2,1,0:T(8,128)} %get-tuple-element.29), channel_id=1, source_target_pairs={{0,1},{1,2},{2,3},{3,4},{4,5},{5,6},{6,7},{7,8},{8,9},{9,10},{10,1... | collective-permute-start | bytes 737288 | tf_op jit(solution)/shard_map/ppermute | solution.py:703
  88.5 8.6 %collective-permute-start.1 = (f32[5,96,128]{2,1,0:T(8,128)S(1)}, f32[5,96,128]{2,1,0:T(8,128)}, u32[]{:S(2)}, u32[]{:S(2)}) collective-permute-start(f32[5,96,128]{2,1,0:T(8,128)S(1)} %get-tuple-element.30), channel_id=1, source_target_pairs={{1,0},{2,1},{3,2},{4,3},{5,4},{6,5},{7,6},{8,7},{9,8},{10,9},{11,1... | collective-permute-start | bytes 737288 | tf_op jit(solution)/shard_map/ppermute | solution.py:708
  97.1 1.4 copy-start.11
  98.5 1.1 copy-start.13
  99.7 11.4 %copy-start.17 = (f32[16,96,512]{2,1,0:T(8,128)S(1)}, f32[16,96,512]{2,1,0:T(8,128)}, u32[]{:S(2)}) copy-start(f32[16,96,512]{2,1,0:T(8,128)} %copy-done.16) | copy-start | bytes 9437188
  99.7 11.4 %copy-start.19 = (bf16[192,192]{1,0:T(8,128)(2,1)S(1)}, bf16[192,192]{1,0:T(8,128)(2,1)}, u32[]{:S(2)}) copy-start(bf16[192,192]{1,0:T(8,128)(2,1)} %copy-done.18) | copy-start | bytes 221188
  102.8 28.2 %collective-permute-start.2 = (f32[3,3,96,256]{3,2,1,0:T(8,128)S(1)}, f32[3,3,96,256]{3,2,1,0:T(8,128)S(1)}, u32[]{:S(2)}, u32[]{:S(2)}) collective-permute-start(f32[3,3,96,256]{3,2,1,0:T(8,128)S(1)} %get-tuple-element.33), channel_id=1, source_target_pairs={{0,16},{16,32},{32,48},{48,64},{64,80},{80,96},{96,112},{1,17},{17... | collective-permute-start | bytes 2654216 | tf_op jit(solution)/shard_map/ppermute | solution.py:703
  109.0 22.1 %collective-permute-start.3 = (f32[3,3,96,256]{3,2,1,0:T(8,128)S(1)}, f32[3,3,96,256]{3,2,1,0:T(8,128)S(1)}, u32[]{:S(2)}, u32[]{:S(2)}) collective-permute-start(f32[3,3,96,256]{3,2,1,0:T(8,128)S(1)} %get-tuple-element.34), channel_id=1, source_target_pairs={{16,0},{32,16},{48,32},{64,48},{80,64},{96,80},{112,96},{17,1},{33... | collective-permute-start | bytes 2654216 | tf_op jit(solution)/shard_map/ppermute | solution.py:708
  111.1 3.2 %copy-start.15 = (bf16[5,16,96,512]{3,2,1,0:T(8,128)(2,1)S(1)}, bf16[5,16,96,512]{3,2,1,0:T(8,128)(2,1)}, u32[]{:S(2)}) copy-start(bf16[5,16,96,512]{3,2,1,0:T(8,128)(2,1)} %copy-done.14) | copy-start | bytes 23592964
  145.8 22.0 %copy-start.7 = (bf16[256,256]{1,0:T(8,128)(2,1)S(1)}, bf16[256,256]{1,0:T(8,128)(2,1)}, u32[]{:S(2)}) copy-start(bf16[256,256]{1,0:T(8,128)(2,1)} %constant.23.clone.perm_r) | copy-start | bytes 393220
  145.8 22.0 %copy-start.8 = (bf16[256,256]{1,0:T(8,128)(2,1)S(1)}, bf16[256,256]{1,0:T(8,128)(2,1)}, u32[]{:S(2)}) copy-start(bf16[256,256]{1,0:T(8,128)(2,1)} %constant.24.clone.perm_y) | copy-start | bytes 393220
  157.8 19.6 %all-to-all-start.1 = ((f32[128,1,128]{2,1,0:T(1,128)}), f32[128,1,128]{2,1,0:T(1,128)S(1)}, u32[]{:S(2)}, u32[]{:S(2)}) async-start(f32[128,1,128]{2,1,0:T(1,128)} %bitcast.11), calls=%async_computation.1 | async-start | bytes 131072 | tf_op jit(solution)/shard_map/all_to_all | solution.py:739
  (3 other events, 2.6 us)

commit v3 on v2

--- a/solution.py
+++ b/solution.py
@@ -1,6 +1,5 @@
 import jax
 import jax.numpy as jnp
-import numpy as np
 from jax import lax
 from jax.experimental import pallas as pl
 from jax.experimental.pallas import tpu as pltpu
@@ -25,6 +24,7 @@
 SELF = 1.0 / 6.0
 SCALE = 0.24**3 / (MEM - 1)
 VMEM = 20 * 1024 * 1024
+MOST = 58 * 1024 * 1024
 
 
 def split(value, count):
@@ -53,20 +53,22 @@
     return jnp.where(test, 1.0, 0.0).astype(BF16)
 
 
-def params(**kw):
-    return pltpu.CompilerParams(vmem_limit_bytes=VMEM, **kw)
+def params(limit=VMEM):
+    return pltpu.CompilerParams(vmem_limit_bytes=limit)
 
 
 def cost(flops, moved):
     return pl.CostEstimate(flops=flops, bytes_accessed=moved, transcendentals=0)
 
 
-def pack_kernel(count, dual, col, lev, upper, vertical, out, tgt_out, rank_out, weights, left_v, left_c, right_v, right_c):
+def pack_kernel(count, dual, col, lev, vertical, out, tgt_out, rank_out, weights, left_v, left_c, right_v, right_c):
     wide = jnp.concatenate([vertical[...], jnp.zeros((LEV, PAD - LEV), F32)], axis=1)
     high, low = split(jnp.concatenate([wide, jnp.zeros((PAD - LEV, PAD), F32)], axis=0), 2)
     both = jnp.concatenate([low, jnp.zeros_like(low)], axis=1)
     weights[...] = jnp.concatenate([jnp.concatenate([high, high], axis=1), both], axis=0)
     number = count[0]
+    lane = iota((DEV, COLS), 1)
+    upper = one_hot((lane > iota((DEV, COLS), 0)) | (lane >= HALF))
     rows = iota((DEV, HALF), 0)
     lane = iota((1, HALF), 1)
     carry = jnp.zeros((DEV, HALF), F32)
@@ -80,7 +82,7 @@
         target = ((row >> 4) << 4) + (gcol >> 8)
         target = jnp.where(i * HALF + lane < number, target, -1)
         hit = rows == target
-        both = dot(one_hot(hit), upper[...])
+        both = dot(one_hot(hit), upper)
         rank = jnp.sum(jnp.where(hit, both[:, :HALF] + carry, 0.0), axis=0, keepdims=True)
         carry = carry + both[:, HALF:]
         tgt_out[i : i + 1, :] = target
@@ -100,7 +102,6 @@
 
 
 def pack(count, dual, col, lev, vertical):
-    upper = np.concatenate([np.triu(np.ones((HALF, HALF)), 1), np.ones((HALF, HALF))], 1)
     spec = pl.BlockSpec(memory_space=pltpu.VMEM)
     return pl.pallas_call(
         pack_kernel,
@@ -111,12 +112,12 @@
             jax.ShapeDtypeStruct((SLOTS // HALF, HALF), I32),
             jax.ShapeDtypeStruct((2 * PAD, 2 * PAD), BF16),
         ),
-        in_specs=[pl.BlockSpec(memory_space=pltpu.SMEM)] + [spec] * 5,
+        in_specs=[pl.BlockSpec(memory_space=pltpu.SMEM)] + [spec] * 4,
         out_specs=(spec,) * 4,
         scratch_shapes=[pltpu.VMEM((3 * DEV, SLOTS), BF16)] * 2 + [pltpu.VMEM((DEV, SLOTS), BF16)] * 2,
         compiler_params=params(),
         cost_estimate=cost(10**9, 10**6),
-    )(count, dual.reshape(-1, HALF), col.reshape(-1, HALF), lev.reshape(-1, HALF), jnp.asarray(upper, BF16), vertical)
+    )(count, dual.reshape(-1, HALF), col.reshape(-1, HALF), lev.reshape(-1, HALF), vertical)
 
 
 def unpack_kernel(back, tgt, rank, out):
@@ -172,68 +173,79 @@
     )
 
 
-def arrange_kernel(ens, perm_y, perm_r, out, up, down, strip, side_l, side_r, buffer, rows, select, sem):
+def arrange_kernel(
+    ens, out, up, down, strip, side_l, side_r, taken, rows, turned_out, up_out, down_out, strip_acc, perm_y, perm_r, sem, sem_out
+):
     def fetch(k):
-        return pltpu.make_async_copy(ens.at[k], buffer.at[k % 4], sem.at[k % 4])
-
-    fetch(0).start()
-    fetch(1).start()
+        return pltpu.make_async_copy(ens.at[k], taken.at[k], sem.at[k])
+
+    def send(duo):
+        slot = duo % 2
+        return (
+            pltpu.make_async_copy(turned_out.at[slot], out.at[duo], sem_out.at[0, slot]),
+            pltpu.make_async_copy(up_out.at[slot], up.at[duo], sem_out.at[1, slot]),
+            pltpu.make_async_copy(down_out.at[slot], down.at[duo], sem_out.at[2, slot]),
+        )
+
+    for k in range(MEM):
+        fetch(k).start()
     rows[LEV * ROWS :, :] = jnp.zeros((rows.shape[0] - LEV * ROWS, DUO), BF16)
+    strip_acc[...] = jnp.zeros_like(strip_acc)
+    y, which = duo_place(iota((1, DUO), 1))
+    perm_y[...] = one_hot(iota((DUO, DUO), 0) == which * COLS + y)
+    i = iota((256, 1), 0)
+    perm_r[...] = one_hot(iota((256, 256), 1) == (i & 15) * 16 + (i >> 4))
 
     @pl.loop(0, DUOS)
     def _(duo):
-        @pl.when(duo < DUOS - 1)
+        @pl.when(duo >= 2)
         def _():
-            fetch(2 * duo + 2).start()
-            fetch(2 * duo + 3).start()
+            for copy in send(duo - 2):
+                copy.wait()
 
         fetch(2 * duo).wait()
         fetch(2 * duo + 1).wait()
-        here, there = 2 * duo % 4, (2 * duo + 1) % 4
+        here, there, slot = 2 * duo, 2 * duo + 1, duo % 2
         y, which = duo_place(iota((DUO, COLS), 0))
-        member, c = strip_place(iota((DUO, COLS), 1))
+        member, c = strip_place(iota((1, COLS), 1))
         want = jnp.where(y < 6, 3 + y, jnp.where(y >= 250, y - 241, -2))
-        select[pl.ds(pl.multiple_of(duo * DUO, DUO), DUO), :] = one_hot((member == 2 * duo + which) & (c == want))
-        for b in range(6):
-            at = slice(b * 240, (b + 1) * 240)
-            block = jnp.concatenate([buffer[here, at, :], buffer[there, at, :]], axis=1)
-            rows[at, :] = dot(block, perm_y[...]).astype(BF16)
+        select = one_hot((member == 2 * duo + which) & (c == want))
+        block = jnp.concatenate([taken[here], taken[there]], axis=1)
+        rows[: LEV * ROWS, :] = dot(block, perm_y[...]).astype(BF16)
         for b in range(6):
             turned = dot(perm_r[...], rows[b * 256 : (b + 1) * 256, :])
             at = slice(b * 16, (b + 1) * 16)
             for x in range(ROWS):
                 part = turned[x * 16 : (x + 1) * 16, :]
-                out[duo, x, at, :] = part.astype(BF16)
+                turned_out[slot, x, at, :] = part.astype(BF16)
                 if x < EDGE:
-                    up[duo, x, at, :] = part
+                    up_out[slot, x, at, :] = part
                 if x >= ROWS - EDGE:
-                    down[duo, x - (ROWS - EDGE), at, :] = part
-
-    @pl.loop(0, ROWS)
-    def _(x):
-        every = jnp.concatenate([out[duo, x] for duo in range(DUOS)], axis=1)
-        strip[x] = dot(every, select[...]).astype(BF16)
-
+                    down_out[slot, x - (ROWS - EDGE), at, :] = part
+        for copy in send(duo):
+            copy.start()
+        for x in range(ROWS):
+            strip_acc[x] += dot(turned_out[slot, x], select)
+
+    for duo in (DUOS - 2, DUOS - 1):
+        for copy in send(duo):
+            copy.wait()
     member, c = strip_place(iota((COLS, COLS), 0))
     left, right = (c >= 3) & (c < 6), (c >= 12) & (c < 15)
     spot = jnp.where(left, 3 * member + c - 3, jnp.where(right, HALF + 3 * member + c - 12, -1000))
+    places = [one_hot(iota((COLS, COLS), 1) == spot + 30 * j) for j in range(4)]
     for group in range(4):
         sides = jnp.zeros((PAD, COLS), F32)
         for j in range(4):
-            sides = sides + dot(strip[group * 4 + j], one_hot(iota((COLS, COLS), 1) == spot + 30 * j))
+            low = strip_acc[group * 4 + j].astype(BF16)
+            strip[group * 4 + j] = low
+            sides = sides + dot(low, places[j])
         side_l[group] = sides[:, :HALF]
         side_r[group] = sides[:, HALF:]
 
 
 def arrange(ensemble):
-    y = np.arange(COLS)
-    perm_y = np.zeros((DUO, DUO))
-    for which in range(2):
-        perm_y[which * COLS + y, y % 4 * HALF + which * QUARTER + y // 4] = 1
-    i = np.arange(256)
-    perm_r = np.zeros((256, 256))
-    perm_r[i % 16 * 16 + i // 16, i] = 1
-    spec = pl.BlockSpec(memory_space=pltpu.VMEM)
+    spec, far = pl.BlockSpec(memory_space=pltpu.VMEM), pl.BlockSpec(memory_space=pltpu.HBM)
     return pl.pallas_call(
         arrange_kernel,
         name="arrange",
@@ -245,17 +257,23 @@
             jax.ShapeDtypeStruct((4, PAD, HALF), F32),
             jax.ShapeDtypeStruct((4, PAD, HALF), F32),
         ),
-        in_specs=[pl.BlockSpec(memory_space=pl.ANY), spec, spec],
-        out_specs=(spec,) * 6,
+        in_specs=[far],
+        out_specs=(far,) * 3 + (spec,) * 3,
         scratch_shapes=[
-            pltpu.VMEM((4, LEV * ROWS, COLS), BF16),
+            pltpu.VMEM((MEM, LEV * ROWS, COLS), BF16),
             pltpu.VMEM((PAD * ROWS, DUO), BF16),
-            pltpu.VMEM((DUOS * DUO, COLS), BF16),
-            pltpu.SemaphoreType.DMA((4,)),
+            pltpu.VMEM((2, ROWS, PAD, DUO), BF16),
+            pltpu.VMEM((2, EDGE, PAD, DUO), F32),
+            pltpu.VMEM((2, EDGE, PAD, DUO), F32),
+            pltpu.VMEM((ROWS, PAD, COLS), F32),
+            pltpu.VMEM((DUO, DUO), BF16),
+            pltpu.VMEM((256, 256), BF16),
+            pltpu.SemaphoreType.DMA((MEM,)),
+            pltpu.SemaphoreType.DMA((3, 2)),
         ],
-        compiler_params=params(),
+        compiler_params=params(MOST),
         cost_estimate=cost(10**10, 25 * 10**6),
-    )(ensemble.reshape(MEM, LEV * ROWS, COLS), jnp.asarray(perm_y, BF16), jnp.asarray(perm_r, BF16))
+    )(ensemble.reshape(MEM, LEV * ROWS, COLS))
 
 
 KTILE = 1024
@@ -437,7 +455,12 @@
 
 
 def inner_kernel(start, count, ens, adj, weights, place, *refs):
-    border, out, field, first = refs[-4:]
+    border, out, field, first, taken, sem = refs[-6:]
+
+    def fetch(step):
+        return pltpu.make_async_copy(ens.at[start + step], taken.at[step % 2], sem.at[step % 2])
+
+    fetch(0).start()
     out[...] = refs[0][...] if start else jnp.zeros_like(out)
     top_open = jnp.where(place[0] == 0, 0.0, 1.0)
     bottom_open = jnp.where(place[0] == place[2], 0.0, 1.0)
@@ -451,7 +474,12 @@
 
     @pl.loop(0, count)
     def _(step):
-        k = start + step
+        @pl.when(step < count - 1)
+        def _():
+            fetch(step + 1).start()
+
+        fetch(step).wait()
+        slot = step % 2
 
         @pl.loop(0, PAD // 16)
         def _(group):
@@ -461,7 +489,7 @@
                 eight = pl.ds(pl.multiple_of(group * 16 + part * 8, 8), 8)
 
                 def get(x):
-                    return ens[k, x, at, :].astype(F32)[part * 8 : part * 8 + 8, :] * adj[x, eight, :]
+                    return taken[slot, x, at, :].astype(F32)[part * 8 : part * 8 + 8, :] * adj[x, eight, :]
 
                 def emit(x, value):
                     if not EDGE <= x < ROWS - EDGE:
@@ -474,11 +502,11 @@
                 diffuse(get, range(ROWS), range(ROWS), beside_duo, emit, mask)
 
         for x in range(INNER):
-            out[x] += ens[k, x + EDGE].astype(F32) * mix(weights[...], field[x])
+            out[x] += taken[slot, x + EDGE].astype(F32) * mix(weights[...], field[x])
 
 
 def inner(ens, adj, weights, place, start, count, before=()):
-    spec = pl.BlockSpec(memory_space=pltpu.VMEM)
+    spec, far = pl.BlockSpec(memory_space=pltpu.VMEM), pl.BlockSpec(memory_space=pltpu.HBM)
     return pl.pallas_call(
         lambda *refs: inner_kernel(start, count, *refs),
         name="inner",
@@ -486,15 +514,34 @@
             jax.ShapeDtypeStruct((count, 2 * EDGE, PAD, DUO), F32),
             jax.ShapeDtypeStruct((INNER, PAD, DUO), F32),
         ),
-        in_specs=[spec] * 3 + [pl.BlockSpec(memory_space=pltpu.SMEM)] + [spec] * len(before),
+        in_specs=[far, spec, spec, pl.BlockSpec(memory_space=pltpu.SMEM)] + [spec] * len(before),
         out_specs=(spec,) * 2,
-        scratch_shapes=[pltpu.VMEM((INNER, 2 * PAD, DUO), BF16), pltpu.VMEM((INNER, 8, DUO), F32)],
+        scratch_shapes=[
+            pltpu.VMEM((INNER, 2 * PAD, DUO), BF16),
+            pltpu.VMEM((INNER, 8, DUO), F32),
+            pltpu.VMEM((2, ROWS, PAD, DUO), BF16),
+            pltpu.SemaphoreType.DMA((2,)),
+        ],
         compiler_params=params(),
         cost_estimate=cost(count * 2 * 10**9, count * 2 * 10**6),
     )(ens, adj, weights, place, *before)
 
 
-def outer_kernel(ens, halo_t, halo_b, adj_t, adj_b, border0, border1, weights, out, field, first, wide):
+def outer_kernel(
+    ens, halo_t, halo_b, adj_t, adj_b, border0, border1, weights, out, field, first, wide, taken_e, taken_h, sem
+):
+    def fetch(duo):
+        slot = duo % 2
+        copies = (
+            (ens.at[duo, pl.ds(0, EDGE)], taken_e.at[slot, pl.ds(0, EDGE)]),
+            (ens.at[duo, pl.ds(ROWS - EDGE, EDGE)], taken_e.at[slot, pl.ds(EDGE, EDGE)]),
+            (halo_t.at[duo], taken_h.at[slot, pl.ds(0, EDGE)]),
+            (halo_b.at[duo], taken_h.at[slot, pl.ds(EDGE, EDGE)]),
+        )
+        return [pltpu.make_async_copy(a, b, sem.at[i, slot]) for i, (a, b) in enumerate(copies)]
+
+    for copy in fetch(0):
+        copy.start()
     out[...] = jnp.zeros_like(out)
     for x in range(EDGE):
         wide[x] = widen(adj_t[0, x])
@@ -504,7 +551,16 @@
 
         @pl.loop(0, border.shape[0])
         def _(step):
-            k = start + step
+            duo = start + step
+            slot = duo % 2
+
+            @pl.when(duo < DUOS - 1)
+            def _():
+                for copy in fetch(duo + 1):
+                    copy.start()
+
+            for copy in fetch(duo):
+                copy.wait()
 
             @pl.loop(0, PAD // 16)
             def _(group):
@@ -521,31 +577,33 @@
                             put_split(field, x, at, jnp.concatenate([first[x], value], axis=0))
 
                     def get_t(x):
-                        return halo_t[k, x + EDGE, eight, :] * wide[x + EDGE, eight, :]
+                        return taken_h[slot, x + EDGE, eight, :] * wide[x + EDGE, eight, :]
 
                     def get_b(x):
-                        return halo_b[k, x - 2 * EDGE, eight, :] * wide[x - EDGE, eight, :]
+                        return taken_h[slot, x - EDGE, eight, :] * wide[x - EDGE, eight, :]
 
                     diffuse(get_t, range(-EDGE, 0), range(EDGE), beside_duo, emit)
                     diffuse(get_b, range(2 * EDGE, 3 * EDGE), range(EDGE, 2 * EDGE), beside_duo, emit)
 
             for x in range(2 * EDGE):
-                row = x if x < EDGE else x + INNER
-                out[x] += ens[k, row].astype(F32) * mix(weights[...], field[x])
+                out[x] += taken_e[slot, x].astype(F32) * mix(weights[...], field[x])
 
 
 def outer(ens, halo_t, halo_b, adj_t, adj_b, border0, border1, weights):
-    spec = pl.BlockSpec(memory_space=pltpu.VMEM)
+    spec, far = pl.BlockSpec(memory_space=pltpu.VMEM), pl.BlockSpec(memory_space=pltpu.HBM)
     return pl.pallas_call(
         outer_kernel,
         name="outer",
         out_shape=jax.ShapeDtypeStruct((2 * EDGE, PAD, DUO), F32),
-        in_specs=[spec] * 8,
+        in_specs=[far] * 3 + [spec] * 5,
         out_specs=spec,
         scratch_shapes=[
             pltpu.VMEM((2 * EDGE, 2 * PAD, DUO), BF16),
             pltpu.VMEM((2 * EDGE, 8, DUO), F32),
             pltpu.VMEM((2 * EDGE, PAD, DUO), F32),
+            pltpu.VMEM((2, 2 * EDGE, PAD, DUO), BF16),
+            pltpu.VMEM((2, 2 * EDGE, PAD, DUO), F32),
+            pltpu.SemaphoreType.DMA((4, 2)),
         ],
         compiler_params=params(),
         cost_estimate=cost(MEM * 10**9, MEM * 3 * 10**6),
@@ -663,15 +721,18 @@
     )(field, incoming)
 
 
-def restore_kernel(field, perm_y, perm_r, out, rows):
+def restore_kernel(field, out, rows):
+    perm_y = one_hot(natural(iota((COLS, COLS), 0)) == iota((COLS, COLS), 1))
+    i = iota((256, 1), 0)
+    perm_r = one_hot(iota((256, 256), 1) == (i & 15) * 16 + (i >> 4))
     for x in range(ROWS):
         value = field[x]
         high, low = split(value, 2)
-        rows[x] = dot(high, perm_y[...]) + dot(low, perm_y[...])
+        rows[x] = dot(high, perm_y) + dot(low, perm_y)
     for b in range(6):
         block = jnp.concatenate([rows[x, b * 16 : (b + 1) * 16, :] for x in range(ROWS)], axis=0)
         high, low = split(block, 2)
-        value = dot(perm_r[...], high) + dot(perm_r[...], low)
+        value = dot(perm_r, high) + dot(perm_r, low)
         if b < 5:
             out[b * 256 : (b + 1) * 256, :] = value
         else:
@@ -679,23 +740,17 @@
 
 
 def restore(field):
-    y = np.arange(COLS)
-    perm_y = np.zeros((COLS, COLS))
-    perm_y[y % 4 * QUARTER + y // 4, y] = 1
-    i = np.arange(256)
-    perm_r = np.zeros((256, 256))
-    perm_r[i, i % 16 * 16 + i // 16] = 1
     spec = pl.BlockSpec(memory_space=pltpu.VMEM)
     return pl.pallas_call(
         restore_kernel,
         name="restore",
         out_shape=jax.ShapeDtypeStruct((LEV * ROWS, COLS), F32),
-        in_specs=[spec] * 3,
+        in_specs=[spec],
         out_specs=spec,
         scratch_shapes=[pltpu.VMEM((ROWS, PAD, COLS), F32)],
         compiler_params=params(),
         cost_estimate=cost(10**9, 3 * 10**6),
-    )(field, jnp.asarray(perm_y, BF16), jnp.asarray(perm_r, BF16)).reshape(LEV, ROWS, COLS)
+    )(field).reshape(LEV, ROWS, COLS)
 
 
 def forward(value, axis):
@@ -718,9 +773,10 @@
     outgoing, target, rank, weights = pack(
         active_count, dual_vector, observed_column, observed_level, vertical_weights
     )
+    ensemble, outgoing = lax.optimization_barrier((ensemble, outgoing))
     incoming = lax.all_to_all(outgoing, ("gx", "gy"), split_axis=0, concat_axis=0, tiled=True)
-
     ens, ens_up, ens_down, strip, ens_l, ens_r = arrange(ensemble)
+    incoming, ens_up, ens_down = lax.optimization_barrier((incoming, ens_up, ens_down))
     halo_t = forward(ens_down, "gx")
     halo_b = backward(ens_up, "gx")
 
@@ -728,6 +784,7 @@
     from_left = forward(side_r, "gy")
     from_right = backward(side_l, "gy")
     border0, inside = inner(ens, wide, weights, place, 0, FIRST)
+    from_left, from_right, inside = lax.optimization_barrier((from_left, from_right, inside))
     strip, adj_strip, up, down = strips(strip, adj, from_left, from_right)
     top = forward(down, "gx")
     bottom = backward(up, "gx")

time: 179 us -> 137 us (0.77)
  blocking collectives: 32.2 us -> 0 us
  local copies, waits for them, and re-layouts: 14.4 us -> 4.75 us
  starting transfers between devices: 29.6 us -> 39.2 us
  waiting for transfers between devices: 14.4 us -> 9.22 us
  Pallas kernels: 86.3 us -> 81.6 us
    all_to_all x1 -> x0, blocking collectives: 32.2 us -> none  [body(): lax.all_to_all(outgoing, ('gx', 'gy'), split_axis=0, concat_axis=0, tiled...]
    all_to_all x0 -> x1, starting transfers between devices: none -> 11.5 us  [body(): lax.all_to_all(outgoing, ('gx', 'gy'), split_axis=0, concat_axis=0, tiled...]
    unnamed x40 -> x16, local copies, waits for them, and re-layouts: 14.4 us -> 4.75 us
    pallas_call x1, Pallas kernels: 18.9 us -> 14.1 us  [arrange(): pl.pallas_call(arrange_kernel, name='arrange', out_shape=(jax.ShapeDtypeS...]
    ppermute x3, waiting for transfers between devices: 3.66 us -> 0.01 us  [forward(): return lax.ppermute(value, axis, [(i, i + 1) for i in range(size - 1)])]
    ppermute x3, starting transfers between devices: 14.2 us -> 11.6 us  [forward(): return lax.ppermute(value, axis, [(i, i + 1) for i in range(size - 1)])]
  transfers between devices with their start and end apart: 7 -> 8, of which waited for: 3 -> 3; matrix products, arithmetic and copies ran while one was open for 0% -> 0% of each run, Pallas kernels for 22% -> 37%
where the time goes in v3:
time: 137 us; the launch traced here: 136 us
  Pallas kernels  81.6 us (60%)
  starting transfers between devices  39.2 us (29%)
  waiting for transfers between devices  9.22 us (7%)
  local copies, waits for them, and re-layouts  4.75 us (3%)
  between operations  1.46 us (1%)
    pallas_call x2, Pallas kernels, inner(): pl.pallas_call(lambda *refs: inner_kernel(start, count, *refs), name='inn...  17.6 us
    pallas_call x1, Pallas kernels, scatter(): pl.pallas_call(scatter_kernel, name='scatter', out_shape=(jax.ShapeDtypeS...  14.7 us
    pallas_call x1, Pallas kernels, arrange(): pl.pallas_call(arrange_kernel, name='arrange', out_shape=(jax.ShapeDtypeS...  14.1 us
    pallas_call x1, Pallas kernels, gather(): pl.pallas_call(gather_kernel, name='gather', out_shape=jax.ShapeDtypeStru...  11.9 us
    ppermute x3, starting transfers between devices, forward(): return lax.ppermute(value, axis, [(i, i + 1) for i in range(size - 1)])  11.6 us
    all_to_all x1, starting transfers between devices, body(): lax.all_to_all(outgoing, ('gx', 'gy'), split_axis=0, concat_axis=0, tiled...  11.5 us
    all_to_all x1, starting transfers between devices, body(): lax.all_to_all(picked, ('gx', 'gy'), split_axis=0, concat_axis=0, tiled=T...  10.8 us
    pallas_call x1, Pallas kernels, outer(): pl.pallas_call(outer_kernel, name='outer', out_shape=jax.ShapeDtypeStruct...  9.99 us
  transfers between devices with their start and end apart: 8, of which 3 were waited for; matrix products, arithmetic and copies ran while one was open for 0% of the time, Pallas kernels for 37%

profile of v3, /device:TPU:1, one launch (start us, length us, event | category | flops | bytes accessed | tf_op | source)
XLA Modules:
  0.0 136.3 jit_solution(15392231286276687052)
XLA Ops:
  1.3 0.8 copy-done
  4.2 2.6 %pack.1 = (f32[128,128]{1,0:T(8,128)}, s32[16,128]{1,0:T(8,128)S(1)}, s32[16,128]{1,0:T(8,128)S(1)}, bf16[192,192]{1,0:T(8,128)(2,1)S(1)}) custom-call(s32[1]{0:T(128)S(6)} %copy.10.count, f32[16,128]{1,0:T(8,128)S(1)} %bitcast.19, s32[16,128]{1,0:T(8,128)S(1)} %bitcast.20, s32[16,128]{1,0:T(8,128)S(1)} %bitcast.21, f32[90,90]{1,0:T(8,128)S(1)} %copy-done), custom_call_target="tpu_custom_call" | custom-call | flops 1000000000 | bytes 1000000 | tf_op jit(solution)/shard_map/pack/pallas_call | solution.py:106
  6.8 11.5 %all-to-all-start = ((f32[128,1,128]{2,1,0:T(1,128)}), f32[128,1,128]{2,1,0:T(1,128)S(1)}, u32[]{:S(2)}, u32[]{:S(2)}) async-start(f32[128,1,128]{2,1,0:T(1,128)} %bitcast.5), calls=%async_computation | async-start | bytes 131072 | tf_op jit(solution)/shard_map/all_to_all | solution.py:777
  18.3 14.1 %arrange.1 = (bf16[5,16,96,512]{3,2,1,0:T(8,128)(2,1)}, f32[5,3,96,512]{3,2,1,0:T(8,128)}, f32[5,3,96,512]{3,2,1,0:T(8,128)}, bf16[16,96,256]{2,1,0:T(8,128)(2,1...) custom-call(bf16[10,1440,256]{2,1,0:T(8,128)(2,1)} %bitcast.22), custom_call_target="tpu_custom_call" | custom-call | flops 10000000000 | bytes 25000000 | tf_op jit(solution)/shard_map/arrange/pallas_call | solution.py:249
  32.4 3.6 %collective-permute-start.4 = (f32[5,3,96,512]{3,2,1,0:T(8,128)}, f32[5,3,96,512]{3,2,1,0:T(8,128)S(1)}, u32[]{:S(2)}, u32[]{:S(2)}) collective-permute-start(f32[5,3,96,512]{3,2,1,0:T(8,128)} %get-tuple-element.56), channel_id=1, source_target_pairs={{0,16},{16,32},{32,48},{48,64},{64,80},{80,96},{96,112},{1,17},{17... | collective-permute-start | bytes 8847368 | tf_op jit(solution)/shard_map/ppermute | solution.py:758
  36.1 1.9 %collective-permute-start.5 = (f32[5,3,96,512]{3,2,1,0:T(8,128)}, f32[5,3,96,512]{3,2,1,0:T(8,128)}, u32[]{:S(2)}, u32[]{:S(2)}) collective-permute-start(f32[5,3,96,512]{3,2,1,0:T(8,128)} %get-tuple-element.57), channel_id=1, source_target_pairs={{16,0},{32,16},{48,32},{64,48},{80,64},{96,80},{112,96},{17,1},{33... | collective-permute-start | bytes 8847368 | tf_op jit(solution)/shard_map/ppermute | solution.py:763
  38.1 0.9 copy-done.6
  39.0 0.9 copy-done.7
  39.9 14.7 %scatter.1 = (f32[16,96,256]{2,1,0:T(8,128)S(1)}, f32[16,96,512]{2,1,0:T(8,128)S(1)}, f32[5,96,128]{2,1,0:T(8,128)S(1)}, f32[5,96,128]{2,1,0:T(8,128)S(1)}) custom-call(f32[128,128]{1,0:T(8,128)S(1)} %bitcast.16, f32[4,96,128]{2,1,0:T(8,128)S(1)} %copy-done.6, f32[4,96,128]{2,1,0:T(8,128)S(1)} %copy-done.7), custom_call_target="tpu_custom_call" | custom-call | flops 10000000000 | bytes 2000000 | tf_op jit(solution)/shard_map/scatter/pallas_call | solution.py:326
  54.6 3.2 %collective-permute-start = (f32[5,96,128]{2,1,0:T(8,128)S(1)}, f32[5,96,128]{2,1,0:T(8,128)S(1)}, u32[]{:S(2)}, u32[]{:S(2)}) collective-permute-start(f32[5,96,128]{2,1,0:T(8,128)S(1)} %get-tuple-element.42), channel_id=1, source_target_pairs={{0,1},{1,2},{2,3},{3,4},{4,5},{5,6},{6,7},{7,8},{8,9},{9,10},{10,1... | collective-permute-start | bytes 737288 | tf_op jit(solution)/shard_map/ppermute | solution.py:758
  57.8 1.5 %collective-permute-start.1 = (f32[5,96,128]{2,1,0:T(8,128)S(1)}, f32[5,96,128]{2,1,0:T(8,128)S(1)}, u32[]{:S(2)}, u32[]{:S(2)}) collective-permute-start(f32[5,96,128]{2,1,0:T(8,128)S(1)} %get-tuple-element.43), channel_id=1, source_target_pairs={{1,0},{2,1},{3,2},{4,3},{5,4},{6,5},{7,6},{8,7},{9,8},{10,9},{11,1... | collective-permute-start | bytes 737288 | tf_op jit(solution)/shard_map/ppermute | solution.py:763
  59.3 7.2 %inner.2 = (f32[2,6,96,512]{3,2,1,0:T(8,128)S(1)}, f32[10,96,512]{2,1,0:T(8,128)S(1)}) custom-call(bf16[5,16,96,512]{3,2,1,0:T(8,128)(2,1)S(1)} %copy-done.5, f32[16,96,512]{2,1,0:T(8,128)S(1)} %get-tuple-element.45.refs_1_, bf16[192,192]{1,0:T(8,128)(2,1)S(1)} %get-tuple-element.46.refs_2_.weights, s32[4]{0:T(128)S(1)} %pad_add_fusion.refs_3_.place), custom_call_target="tpu_custom_call" | custom-call | flops 4000000000 | bytes 4000000 | tf_op jit(solution)/shard_map/inner/pallas_call | solution.py:510
  66.6 2.1 %strips.1 = (bf16[16,96,256]{2,1,0:T(8,128)(2,1)S(1)}, f32[16,96,256]{2,1,0:T(8,128)S(1)}, f32[3,3,96,256]{3,2,1,0:T(8,128)S(1)}, f32[3,3,96,256]{3,2,1,0:T(8,128)S(1)}) custom-call(bf16[16,96,256]{2,1,0:T(8,128)(2,1)S(1)} %copy-done.4, f32[16,96,256]{2,1,0:T(8,128)S(1)} %get-tuple-element.41.adjoint, f32[5,96,128]{2,1,0:T(8,128)S(1)} %collective-permute-done.left, ...), custom_call_target="tpu_custom_call" | custom-call | flops 1000000000 | bytes 4000000 | tf_op jit(solution)/shard_map/strips/pallas_call | solution.py:386
  68.7 4.7 %collective-permute-start.2 = (f32[3,3,96,256]{3,2,1,0:T(8,128)S(1)}, f32[3,3,96,256]{3,2,1,0:T(8,128)S(1)}, u32[]{:S(2)}, u32[]{:S(2)}) collective-permute-start(f32[3,3,96,256]{3,2,1,0:T(8,128)S(1)} %get-tuple-element.52), channel_id=1, source_target_pairs={{0,16},{16,32},{32,48},{48,64},{64,80},{80,96},{96,112},{1,17},{17... | collective-permute-start | bytes 2654216 | tf_op jit(solution)/shard_map/ppermute | solution.py:758
  73.4 1.9 %collective-permute-start.3 = (f32[3,3,96,256]{3,2,1,0:T(8,128)S(1)}, f32[3,3,96,256]{3,2,1,0:T(8,128)S(1)}, u32[]{:S(2)}, u32[]{:S(2)}) collective-permute-start(f32[3,3,96,256]{3,2,1,0:T(8,128)S(1)} %get-tuple-element.53), channel_id=1, source_target_pairs={{16,0},{32,16},{48,32},{64,48},{80,64},{96,80},{112,96},{17,1},{33... | collective-permute-start | bytes 2654216 | tf_op jit(solution)/shard_map/ppermute | solution.py:763
  75.4 10.4 %inner.3 = (f32[3,6,96,512]{3,2,1,0:T(8,128)S(1)}, f32[10,96,512]{2,1,0:T(8,128)S(1)}) custom-call(bf16[5,16,96,512]{3,2,1,0:T(8,128)(2,1)S(1)} %copy-done.5, f32[16,96,512]{2,1,0:T(8,128)S(1)} %get-tuple-element.45.refs_1_, bf16[192,192]{1,0:T(8,128)(2,1)S(1)} %get-tuple-element.46.refs_2_.weights, s32[4]{0:T(128)S(1)} %pad_add_fusion.refs_3_.place, ...), custom_call_target="tpu_custom_call" | custom-call | flops 6000000000 | bytes 6000000 | tf_op jit(solution)/shard_map/inner/pallas_call | solution.py:510
  85.8 2.0 %collective-permute-done.3.adj_b.halo_b = f32[3,3,96,256]{3,2,1,0:T(8,128)S(1)} collective-permute-done((f32[3,3,96,256]{3,2,1,0:T(8,128)S(1)}, f32[3,3,96,256]{3,2,1,0:T(8,128)S(1)}, u32[]{:S(2)}, u32[]{:S(2)}) %collective-permute-start.3) | collective-permute-done | bytes 884768 | tf_op jit(solution)/shard_map/ppermute | solution.py:763
  87.8 10.0 %outer.1.border = f32[6,96,512]{2,1,0:T(8,128)S(1)} custom-call(bf16[5,16,96,512]{3,2,1,0:T(8,128)(2,1)S(1)} %copy-done.5, f32[5,3,96,512]{3,2,1,0:T(8,128)S(1)} %collective-permute-done.4.halo_t, f32[5,3,96,512]{3,2,1,0:T(8,128)} %collective-permute-done.5.halo_b, f32[3,3,96,256]{3,2,1,0:T(8,128)S(1)} %collective-permute-done.2.adj_t.halo_t, ...), custom_call_target="tpu_custom_call" | custom-call | flops 10000000000 | bytes 30000000 | tf_op jit(solution)/shard_map/outer/pallas_call | solution.py:594
  97.8 5.0 %edge.1.field = f32[16,96,256]{2,1,0:T(8,128)S(1)} custom-call(bf16[16,96,256]{2,1,0:T(8,128)(2,1)S(1)} %get-tuple-element.50.strip, f32[16,96,256]{2,1,0:T(8,128)S(1)} %get-tuple-element.51.adj, f32[3,3,96,256]{3,2,1,0:T(8,128)S(1)} %collective-permute-done.2.adj_t.halo_t, f32[3,3,96,256]{3,2,1,0:T(8,128)S(1)} %collective-permute-done.3.adj_b.halo_b, ...), custom_call_target="tpu_custom_call" | custom-call | flops 4000000000 | bytes 8000000 | tf_op jit(solution)/shard_map/edge/pallas_call | solution.py:664
  102.8 11.9 %gather.1 = f32[128,128]{1,0:T(8,128)} custom-call(f32[16,96,256]{2,1,0:T(8,128)S(1)} %edge.1.field, f32[128,128]{1,0:T(8,128)S(1)} %bitcast.17), custom_call_target="tpu_custom_call" | custom-call | flops 10000000000 | bytes 2000000 | tf_op jit(solution)/shard_map/gather/pallas_call | solution.py:707
  114.7 10.8 %all-to-all-start.1 = ((f32[128,1,128]{2,1,0:T(1,128)}), f32[128,1,128]{2,1,0:T(1,128)S(1)}, u32[]{:S(2)}, u32[]{:S(2)}) async-start(f32[128,1,128]{2,1,0:T(1,128)} %bitcast.11), calls=%async_computation.1 | async-start | bytes 131072 | tf_op jit(solution)/shard_map/all_to_all | solution.py:796
  125.6 2.4 %restore.1 = f32[1440,256]{1,0:T(8,128)} custom-call(f32[16,96,256]{2,1,0:T(8,128)S(1)} %edge.1.field), custom_call_target="tpu_custom_call" | custom-call | flops 1000000000 | bytes 3000000 | tf_op jit(solution)/shard_map/restore/pallas_call | solution.py:744
  128.0 7.1 %all-to-all-done.1 = f32[128,1,128]{2,1,0:T(1,128)S(1)} async-done(((f32[128,1,128]{2,1,0:T(1,128)}), f32[128,1,128]{2,1,0:T(1,128)S(1)}, u32[]{:S(2)}, u32[]{:S(2)}) %all-to-all-start.1) | async-done | bytes 65568 | tf_op jit(solution)/shard_map/all_to_all | solution.py:796
  135.1 1.2 unpack.1
  (20 shorter events, 2.3 us)
Async XLA Ops:
  1.3 0.8 copy-start
  2.1 0.7 copy-start.1
  2.8 0.7 copy-start.2
  3.5 0.7 copy-start.3
  6.8 25.6 %all-to-all-start = ((f32[128,1,128]{2,1,0:T(1,128)}), f32[128,1,128]{2,1,0:T(1,128)S(1)}, u32[]{:S(2)}, u32[]{:S(2)}) async-start(f32[128,1,128]{2,1,0:T(1,128)} %bitcast.5), calls=%async_computation | async-start | bytes 131072 | tf_op jit(solution)/shard_map/all_to_all | solution.py:777
  32.4 55.4 %collective-permute-start.4 = (f32[5,3,96,512]{3,2,1,0:T(8,128)}, f32[5,3,96,512]{3,2,1,0:T(8,128)S(1)}, u32[]{:S(2)}, u32[]{:S(2)}) collective-permute-start(f32[5,3,96,512]{3,2,1,0:T(8,128)} %get-tuple-element.56), channel_id=1, source_target_pairs={{0,16},{16,32},{32,48},{48,64},{64,80},{80,96},{96,112},{1,17},{17... | collective-permute-start | bytes 8847368 | tf_op jit(solution)/shard_map/ppermute | solution.py:758
  36.1 51.8 %collective-permute-start.5 = (f32[5,3,96,512]{3,2,1,0:T(8,128)}, f32[5,3,96,512]{3,2,1,0:T(8,128)}, u32[]{:S(2)}, u32[]{:S(2)}) collective-permute-start(f32[5,3,96,512]{3,2,1,0:T(8,128)} %get-tuple-element.57), channel_id=1, source_target_pairs={{16,0},{32,16},{48,32},{64,48},{80,64},{96,80},{112,96},{17,1},{33... | collective-permute-start | bytes 8847368 | tf_op jit(solution)/shard_map/ppermute | solution.py:763
  38.1 0.9 copy-start.6
  39.0 0.9 copy-start.7
  39.9 19.4 %copy-start.5 = (bf16[5,16,96,512]{3,2,1,0:T(8,128)(2,1)S(1)}, bf16[5,16,96,512]{3,2,1,0:T(8,128)(2,1)}, u32[]{:S(2)}) copy-start(bf16[5,16,96,512]{3,2,1,0:T(8,128)(2,1)} %get-tuple-element.44.refs_0_.ens) | copy-start | bytes 23592964
  54.6 11.9 %collective-permute-start = (f32[5,96,128]{2,1,0:T(8,128)S(1)}, f32[5,96,128]{2,1,0:T(8,128)S(1)}, u32[]{:S(2)}, u32[]{:S(2)}) collective-permute-start(f32[5,96,128]{2,1,0:T(8,128)S(1)} %get-tuple-element.42), channel_id=1, source_target_pairs={{0,1},{1,2},{2,3},{3,4},{4,5},{5,6},{6,7},{7,8},{8,9},{9,10},{10,1... | collective-permute-start | bytes 737288 | tf_op jit(solution)/shard_map/ppermute | solution.py:758
  57.8 8.8 %collective-permute-start.1 = (f32[5,96,128]{2,1,0:T(8,128)S(1)}, f32[5,96,128]{2,1,0:T(8,128)S(1)}, u32[]{:S(2)}, u32[]{:S(2)}) collective-permute-start(f32[5,96,128]{2,1,0:T(8,128)S(1)} %get-tuple-element.43), channel_id=1, source_target_pairs={{1,0},{2,1},{3,2},{4,3},{5,4},{6,5},{7,6},{8,7},{9,8},{10,9},{11,1... | collective-permute-start | bytes 737288 | tf_op jit(solution)/shard_map/ppermute | solution.py:763
  59.3 7.3 %copy-start.4 = (bf16[16,96,256]{2,1,0:T(8,128)(2,1)S(1)}, bf16[16,96,256]{2,1,0:T(8,128)(2,1)}, u32[]{:S(2)}) copy-start(bf16[16,96,256]{2,1,0:T(8,128)(2,1)} %get-tuple-element.34.strip) | copy-start | bytes 2359300
  68.7 17.1 %collective-permute-start.2 = (f32[3,3,96,256]{3,2,1,0:T(8,128)S(1)}, f32[3,3,96,256]{3,2,1,0:T(8,128)S(1)}, u32[]{:S(2)}, u32[]{:S(2)}) collective-permute-start(f32[3,3,96,256]{3,2,1,0:T(8,128)S(1)} %get-tuple-element.52), channel_id=1, source_target_pairs={{0,16},{16,32},{32,48},{48,64},{64,80},{80,96},{96,112},{1,17},{17... | collective-permute-start | bytes 2654216 | tf_op jit(solution)/shard_map/ppermute | solution.py:758
  73.4 14.4 %collective-permute-start.3 = (f32[3,3,96,256]{3,2,1,0:T(8,128)S(1)}, f32[3,3,96,256]{3,2,1,0:T(8,128)S(1)}, u32[]{:S(2)}, u32[]{:S(2)}) collective-permute-start(f32[3,3,96,256]{3,2,1,0:T(8,128)S(1)} %get-tuple-element.53), channel_id=1, source_target_pairs={{16,0},{32,16},{48,32},{64,48},{80,64},{96,80},{112,96},{17,1},{33... | collective-permute-start | bytes 2654216 | tf_op jit(solution)/shard_map/ppermute | solution.py:763
  114.7 20.4 %all-to-all-start.1 = ((f32[128,1,128]{2,1,0:T(1,128)}), f32[128,1,128]{2,1,0:T(1,128)S(1)}, u32[]{:S(2)}, u32[]{:S(2)}) async-start(f32[128,1,128]{2,1,0:T(1,128)} %bitcast.11), calls=%async_computation.1 | async-start | bytes 131072 | tf_op jit(solution)/shard_map/all_to_all | solution.py:796

commit v4 on v3

--- a/solution.py
+++ b/solution.py
@@ -25,6 +25,7 @@
 SCALE = 0.24**3 / (MEM - 1)
 VMEM = 20 * 1024 * 1024
 MOST = 58 * 1024 * 1024
+ALL = 63 * 1024 * 1024
 
 
 def split(value, count):
@@ -61,7 +62,15 @@
     return pl.CostEstimate(flops=flops, bytes_accessed=moved, transcendentals=0)
 
 
-def pack_kernel(count, dual, col, lev, vertical, out, tgt_out, rank_out, weights, left_v, left_c, right_v, right_c):
+def pack_kernel(
+    count, dual_far, col_far, lev_far, vertical_far, out, tgt_out, rank_out, weights, left_v, left_c, right_v, right_c, dual, col, lev, vertical, sem
+):
+    pairs = ((col_far, col), (lev_far, lev), (dual_far, dual), (vertical_far, vertical))
+    copies = [pltpu.make_async_copy(a, b, sem.at[i]) for i, (a, b) in enumerate(pairs)]
+    for copy in copies:
+        copy.start()
+    for copy in copies:
+        copy.wait()
     wide = jnp.concatenate([vertical[...], jnp.zeros((LEV, PAD - LEV), F32)], axis=1)
     high, low = split(jnp.concatenate([wide, jnp.zeros((PAD - LEV, PAD), F32)], axis=0), 2)
     both = jnp.concatenate([low, jnp.zeros_like(low)], axis=1)
@@ -93,7 +102,7 @@
         values = dual[i : i + 1, :]
         for p, piece in enumerate(split(values, 3)):
             left_v[p * DEV : (p + 1) * DEV, at] = jnp.where(hit, piece.astype(F32), 0.0).astype(BF16)
-        cells = (lev[i : i + 1, :] << 12, (row & 15) << 8, y)
+        cells = (lev[i : i + 1, :] << 12, (row & 15) << 8, y + 1)
         for p, piece in enumerate(cells):
             left_c[p * DEV : (p + 1) * DEV, at] = jnp.where(hit, piece.astype(F32), 0.0).astype(BF16)
     a = dot_nt(left_v[...], right_v[...])
@@ -112,10 +121,13 @@
             jax.ShapeDtypeStruct((SLOTS // HALF, HALF), I32),
             jax.ShapeDtypeStruct((2 * PAD, 2 * PAD), BF16),
         ),
-        in_specs=[pl.BlockSpec(memory_space=pltpu.SMEM)] + [spec] * 4,
+        in_specs=[pl.BlockSpec(memory_space=pltpu.SMEM)] + [pl.BlockSpec(memory_space=pltpu.HBM)] * 4,
         out_specs=(spec,) * 4,
-        scratch_shapes=[pltpu.VMEM((3 * DEV, SLOTS), BF16)] * 2 + [pltpu.VMEM((DEV, SLOTS), BF16)] * 2,
-        compiler_params=params(),
+        scratch_shapes=[pltpu.VMEM((3 * DEV, SLOTS), BF16)] * 2
+        + [pltpu.VMEM((DEV, SLOTS), BF16)] * 2
+        + [pltpu.VMEM((SLOTS // HALF, HALF), kind) for kind in (F32, I32, I32)]
+        + [pltpu.VMEM((LEV, LEV), F32), pltpu.SemaphoreType.DMA((4,))],
+        compiler_params=params(ALL),
         cost_estimate=cost(10**9, 10**6),
     )(count, dual.reshape(-1, HALF), col.reshape(-1, HALF), lev.reshape(-1, HALF), vertical)
 
@@ -174,7 +186,7 @@
 
 
 def arrange_kernel(
-    ens, out, up, down, strip, side_l, side_r, taken, rows, turned_out, up_out, down_out, strip_acc, perm_y, perm_r, sem, sem_out
+    ens, out, up, down, strip, side_l, side_r, taken, rows, turned_out, up_out, down_out, strip_acc, perm_y, perm_r, sides_out, sem, sem_out
 ):
     def fetch(k):
         return pltpu.make_async_copy(ens.at[k], taken.at[k], sem.at[k])
@@ -234,14 +246,22 @@
     left, right = (c >= 3) & (c < 6), (c >= 12) & (c < 15)
     spot = jnp.where(left, 3 * member + c - 3, jnp.where(right, HALF + 3 * member + c - 12, -1000))
     places = [one_hot(iota((COLS, COLS), 1) == spot + 30 * j) for j in range(4)]
+    places = [one_hot(iota((COLS, COLS), 1) == spot + 30 * j) for j in range(4)]
     for group in range(4):
         sides = jnp.zeros((PAD, COLS), F32)
         for j in range(4):
             low = strip_acc[group * 4 + j].astype(BF16)
             strip[group * 4 + j] = low
             sides = sides + dot(low, places[j])
-        side_l[group] = sides[:, :HALF]
-        side_r[group] = sides[:, HALF:]
+        sides_out[0, group] = sides[:, :HALF]
+        sides_out[1, group] = sides[:, HALF:]
+    copies = [
+        pltpu.make_async_copy(sides_out.at[i], side.at[pl.ds(0, 4)], sem_out.at[0, i]) for i, side in enumerate((side_l, side_r))
+    ]
+    for copy in copies:
+        copy.start()
+    for copy in copies:
+        copy.wait()
 
 
 def arrange(ensemble):
@@ -254,11 +274,11 @@
             jax.ShapeDtypeStruct((DUOS, EDGE, PAD, DUO), F32),
             jax.ShapeDtypeStruct((DUOS, EDGE, PAD, DUO), F32),
             jax.ShapeDtypeStruct((ROWS, PAD, COLS), BF16),
-            jax.ShapeDtypeStruct((4, PAD, HALF), F32),
-            jax.ShapeDtypeStruct((4, PAD, HALF), F32),
+            jax.ShapeDtypeStruct((5, PAD, HALF), F32),
+            jax.ShapeDtypeStruct((5, PAD, HALF), F32),
         ),
         in_specs=[far],
-        out_specs=(far,) * 3 + (spec,) * 3,
+        out_specs=(far, far, far, spec, far, far),
         scratch_shapes=[
             pltpu.VMEM((MEM, LEV * ROWS, COLS), BF16),
             pltpu.VMEM((PAD * ROWS, DUO), BF16),
@@ -268,6 +288,7 @@
             pltpu.VMEM((ROWS, PAD, COLS), F32),
             pltpu.VMEM((DUO, DUO), BF16),
             pltpu.VMEM((256, 256), BF16),
+            pltpu.VMEM((2, 4, PAD, HALF), F32),
             pltpu.SemaphoreType.DMA((MEM,)),
             pltpu.SemaphoreType.DMA((3, 2)),
         ],
@@ -276,53 +297,94 @@
     )(ensemble.reshape(MEM, LEV * ROWS, COLS))
 
 
-KTILE = 1024
-
-
-def scatter_kernel(incoming, ens_l, ens_r, out, wide, side_l, side_r, turned, hot1, hot2, acc):
+CHUNKS = CAP // 2
+TILES = CHUNKS + ROWS
+SPACE = 48
+
+
+def scatter_kernel(
+    incoming, ens_l, ens_r, out, wide, side_l, side_r, level_out, column_out, pos_out, row_out,
+    turned, hot, left, right, rows_of, sorted_, sides_out, sem
+):
     turned[...] = incoming[...].T
-    acc[...] = jnp.zeros_like(acc)
-    rows1 = iota((4 * PAD, HALF), 0)
-    rows2 = iota((4 * COLS, HALF), 0)
-
-    @pl.loop(0, CAP // 8)
+    pairs = [[turned[pl.ds(first + i, CHUNKS, stride=2), :] for i in range(2)] for first in (0, CAP)]
+    values = jnp.concatenate(pairs[0], axis=1)
+    cells = jnp.concatenate(pairs[1], axis=1).astype(I32) - 1
+    full = cells >= 0
+    x = jnp.where(full, (cells >> 8) & 15, 99)
+
+    for c in range(CHUNKS):
+        hot[c * ROWS : (c + 1) * ROWS, :] = one_hot(iota((ROWS, COLS), 0) == x[c : c + 1, :])
+    size = CHUNKS * ROWS
+    lane = iota((COLS, COLS + HALF), 1)
+    both = dot(hot[...], one_hot((lane > iota((COLS, COLS + HALF), 0)) | (lane >= COLS)))
+    count = both[:, COLS:].astype(BF16)
+    here, there = iota((size, size), 0), iota((size, size), 1)
+    same = (here & 15) == (there & 15)
+    earlier = dot(one_hot(same & (there < here)), count)
+    needed = (dot(one_hot(same), count).astype(I32) + 255) >> 8
+    start = dot(one_hot(((there & 15) < (here & 15)) & (there < ROWS)), needed.astype(F32).astype(BF16))
+    base = start * 256.0 + earlier
+    place = both[:, :COLS] + jnp.concatenate([base, base], axis=1)
+    place = jnp.where(hot[...].astype(F32) > 0.5, place, 0.0)
+    pos = jnp.sum(place.reshape(CHUNKS, ROWS, COLS), axis=1).astype(I32)
+    pos = jnp.where(full, pos, -1)
+    pos_out[...] = pos
+    begun = jnp.where(start[:ROWS].astype(I32) <= iota((ROWS, HALF), 1), 1.0, 0.0)
+    row_out[...] = jnp.sum(begun, axis=0, keepdims=True).astype(I32) - 1
+    copy = pltpu.make_async_copy(row_out, rows_of, sem.at[0])
+    copy.start()
+
+    parts = [p.astype(F32) for p in split(values, 2)] + [(cells >> 12).astype(F32), (cells & 255).astype(F32)]
+    tile, spot = pos >> 8, pos & 255
+    for c in range(CHUNKS):
+        at = slice(c * COLS, (c + 1) * COLS)
+        hit = iota((SPACE, COLS), 0) == tile[c : c + 1, :]
+        for p, part in enumerate(parts):
+            left[p * SPACE : (p + 1) * SPACE, at] = jnp.where(hit, part[c : c + 1, :], 0.0).astype(BF16)
+        right[:, at] = one_hot(iota((COLS, COLS), 0) == spot[c : c + 1, :])
+    sorted_[...] = dot_nt(left[...], right[...])
+    level_out[...] = sorted_[2 * SPACE : 3 * SPACE, :]
+    column_out[...] = sorted_[3 * SPACE :, :]
+    out[...] = jnp.zeros_like(out)
+    copy.wait()
+
+    @pl.loop(0, TILES // 8)
     def _(j):
-        first = pl.multiple_of(j * 8, 8)
-        values = turned[pl.ds(first, 8), :]
-        cells = turned[pl.ds(CAP + first, 8), :].astype(I32)
-        for q in range(8):
-            at = slice(q * HALF, (q + 1) * HALF)
-            cell = cells[q : q + 1, :]
-            key1 = ((cell >> 10) & 3) * PAD + (cell >> 12)
-            hit = rows1 == key1
-            for p, piece in enumerate(split(values[q : q + 1, :], 2)):
-                hot1[p * 4 * PAD : (p + 1) * 4 * PAD, at] = jnp.where(hit, piece.astype(F32), 0.0).astype(BF16)
-            hot2[:, at] = one_hot(rows2 == (cell & 1023))
-        for n in range(4):
-            cols = slice(n * COLS, (n + 1) * COLS)
-            acc[:, cols] += dot_nt(hot1[...], hot2[cols, :])
+        high, low, level, column = (sorted_[pl.ds(pl.multiple_of(p * SPACE + j * 8, 8), 8), :] for p in range(4))
+        level, column = level.astype(I32), column.astype(I32)
+        for half in range(2):
+            results = []
+            for q in range(half * 4, half * 4 + 4):
+                at = slice(q, q + 1)
+                hit = iota((PAD, COLS), 0) == level[at, :]
+                lhs = jnp.concatenate([jnp.where(hit, high[at, :], 0.0), jnp.where(hit, low[at, :], 0.0)], axis=0)
+                both = dot_nt(lhs.astype(BF16), one_hot(iota((COLS, COLS), 0) == column[at, :]))
+                results.append(both[:PAD] + both[PAD:])
+            for i, result in enumerate(results):
+                out[rows_of[0, j * 8 + half * 4 + i]] += result
 
     y = natural(iota((COLS, COLS), 0))
     lane = iota((COLS, COLS), 1)
     place = jnp.where(y < 3, y, jnp.where(y >= 253, HALF + y - 253, -1000))
     packed = jnp.zeros((PAD, COLS), F32)
     for x in range(ROWS):
-        cols = slice(x % 4 * COLS, (x % 4 + 1) * COLS)
-        level = x // 4 * PAD
-        value = acc[level : level + PAD, cols] + acc[4 * PAD + level : 4 * PAD + level + PAD, cols]
-        out[x] = value
+        value = out[x]
         wide[x] = widen(value)
         select = one_hot(lane == place + 3 * x)
         for piece in split(value, 2):
             packed = packed + dot(piece, select)
-    side_l[:4] = ens_l[...]
-    side_r[:4] = ens_r[...]
-    side_l[4] = packed[:, :HALF]
-    side_r[4] = packed[:, HALF:]
+    sides_out[0] = packed[:, :HALF]
+    sides_out[1] = packed[:, HALF:]
+    copies = [pltpu.make_async_copy(sides_out.at[i], side.at[4], sem.at[i]) for i, side in enumerate((side_l, side_r))]
+    for copy in copies:
+        copy.start()
+    for copy in copies:
+        copy.wait()
 
 
 def scatter(incoming, ens_l, ens_r):
-    spec = pl.BlockSpec(memory_space=pltpu.VMEM)
+    spec, far = pl.BlockSpec(memory_space=pltpu.VMEM), pl.BlockSpec(memory_space=pltpu.HBM)
     return pl.pallas_call(
         scatter_kernel,
         name="scatter",
@@ -331,14 +393,23 @@
             jax.ShapeDtypeStruct((ROWS, PAD, DUO), F32),
             jax.ShapeDtypeStruct((5, PAD, HALF), F32),
             jax.ShapeDtypeStruct((5, PAD, HALF), F32),
+            jax.ShapeDtypeStruct((SPACE, COLS), F32),
+            jax.ShapeDtypeStruct((SPACE, COLS), F32),
+            jax.ShapeDtypeStruct((CHUNKS, COLS), I32),
+            jax.ShapeDtypeStruct((1, HALF), I32),
         ),
-        in_specs=[spec] * 3,
-        out_specs=(spec,) * 4,
+        in_specs=[spec, far, far],
+        out_specs=(spec, spec, far, far, spec, spec, spec, spec),
+        input_output_aliases={1: 2, 2: 3},
         scratch_shapes=[
             pltpu.VMEM((HALF, DEV), F32),
-            pltpu.VMEM((8 * PAD, KTILE), BF16),
-            pltpu.VMEM((4 * COLS, KTILE), BF16),
-            pltpu.VMEM((8 * PAD, 4 * COLS), F32),
+            pltpu.VMEM((CHUNKS * ROWS, COLS), BF16),
+            pltpu.VMEM((4 * SPACE, CHUNKS * COLS), BF16),
+            pltpu.VMEM((COLS, CHUNKS * COLS), BF16),
+            pltpu.SMEM((1, HALF), I32),
+            pltpu.VMEM((4 * SPACE, COLS), F32),
+            pltpu.VMEM((2, PAD, HALF), F32),
+            pltpu.SemaphoreType.DMA((2,)),
         ],
         compiler_params=params(),
         cost_estimate=cost(10**10, 2 * 10**6),
@@ -673,52 +744,49 @@
     )(strip, adj, halo_t, halo_b, weights, place, inside, border)
 
 
-def gather_kernel(field, incoming, out, turned, table, hot, picked):
-    turned[...] = incoming[...].T
+def gather_kernel(field, level, column, pos, rows_of, out, table, picked):
+    for x in range(ROWS):
+        table[x, :PAD, :], table[x, PAD:, :] = split(field[x], 2)
     picked[...] = jnp.zeros_like(picked)
-    for x in range(ROWS):
-        cols = slice(x % 4 * COLS, (x % 4 + 1) * COLS)
-        for p, piece in enumerate(split(field[x], 2)):
-            first = (p * 4 + x // 4) * PAD
-            table[first : first + PAD, cols] = piece
-    rows1 = iota((4 * PAD, COLS), 0)
-    rows2 = iota((4 * COLS, COLS), 0)
-
-    @pl.loop(0, CAP // 8)
+
+    @pl.loop(0, TILES // 8)
     def _(j):
         first = pl.multiple_of(j * 8, 8)
-        cells = turned[pl.ds(CAP + first, 8), :].astype(I32)
+        levels, columns = level[pl.ds(first, 8), :].astype(I32), column[pl.ds(first, 8), :].astype(I32)
         lines = []
-        for q in range(0, 8, 2):
-            cell = jnp.concatenate([cells[q : q + 1, :], cells[q + 1 : q + 2, :]], axis=1)
-            hot[...] = one_hot(rows2 == (cell & 1023))
-            found = dot(table[...], hot[...])
-            key1 = ((cell >> 10) & 3) * PAD + (cell >> 12)
-            found = jnp.where(rows1 == key1, found[: 4 * PAD] + found[4 * PAD :], 0.0)
-            found = jnp.sum(found, axis=0, keepdims=True)
-            lines += [found[:, :HALF], found[:, HALF:]]
+        for q in range(8):
+            at = slice(q, q + 1)
+            found = dot(table[rows_of[0, j * 8 + q]], one_hot(iota((COLS, COLS), 0) == columns[at, :]))
+            found = jnp.where(iota((PAD, COLS), 0) == levels[at, :], found[:PAD] + found[PAD:], 0.0)
+            lines.append(jnp.sum(found, axis=0, keepdims=True))
         picked[pl.ds(first, 8), :] = jnp.concatenate(lines, axis=0)
 
-    out[...] = picked[...].T
-
-
-def gather(field, incoming):
+    both = jnp.concatenate(split(picked[...], 2), axis=0)
+    tile, spot = pos[...] >> 8, pos[...] & 255
+    lines = []
+    for c in range(CHUNKS):
+        found = dot(both, one_hot(iota((COLS, COLS), 0) == spot[c : c + 1, :]))
+        found = jnp.where(iota((SPACE, COLS), 0) == tile[c : c + 1, :], found[:SPACE] + found[SPACE:], 0.0)
+        found = jnp.sum(found, axis=0, keepdims=True)
+        lines += [found[:, :HALF], found[:, HALF:]]
+    out[...] = jnp.concatenate(lines + [jnp.zeros((HALF - CAP, DEV), F32)], axis=0).T
+
+
+def gather(field, level, column, pos, rows_of):
     spec = pl.BlockSpec(memory_space=pltpu.VMEM)
     return pl.pallas_call(
         gather_kernel,
         name="gather",
         out_shape=jax.ShapeDtypeStruct((DEV, HALF), F32),
-        in_specs=[spec] * 2,
+        in_specs=[spec] * 4 + [pl.BlockSpec(memory_space=pltpu.SMEM)],
         out_specs=spec,
         scratch_shapes=[
-            pltpu.VMEM((HALF, DEV), F32),
-            pltpu.VMEM((8 * PAD, 4 * COLS), BF16),
-            pltpu.VMEM((4 * COLS, COLS), BF16),
-            pltpu.VMEM((HALF, DEV), F32),
+            pltpu.VMEM((ROWS, 2 * PAD, COLS), BF16),
+            pltpu.VMEM((SPACE, COLS), F32),
         ],
         compiler_params=params(),
         cost_estimate=cost(10**10, 2 * 10**6),
-    )(field, incoming)
+    )(field, level, column, pos, rows_of)
 
 
 def restore_kernel(field, out, rows):
@@ -780,7 +848,7 @@
     halo_t = forward(ens_down, "gx")
     halo_b = backward(ens_up, "gx")
 
-    adj, wide, side_l, side_r = scatter(incoming, ens_l, ens_r)
+    adj, wide, side_l, side_r, *slots = scatter(incoming, ens_l, ens_r)
     from_left = forward(side_r, "gy")
     from_right = backward(side_l, "gy")
     border0, inside = inner(ens, wide, weights, place, 0, FIRST)
@@ -792,7 +860,7 @@
 
     outside = outer(ens, halo_t, halo_b, top, bottom, border0, border1, weights)
     field = edge(strip, adj_strip, top, bottom, weights, place, inside, outside)
-    picked = gather(field, incoming)
+    picked = gather(field, *slots)
     back = lax.all_to_all(picked, ("gx", "gy"), split_axis=0, concat_axis=0, tiled=True)
     increment = restore(field)
     obs_product = unpack(back, target, rank)

time: 137 us -> 121 us (0.88)
  Pallas kernels: 81.6 us -> 67.5 us
  local copies, waits for them, and re-layouts: 4.75 us -> 0.02 us
  waiting for transfers between devices: 9.22 us -> 13.4 us
  starting transfers between devices: 39.2 us -> 37.6 us
    pallas_call x1, Pallas kernels: 11.9 us -> 4.29 us  [gather(): pl.pallas_call(gather_kernel, name='gather', out_shape=jax.ShapeDtypeStru...]
    pallas_call x1, Pallas kernels: 14.7 us -> 7.34 us  [scatter(): pl.pallas_call(scatter_kernel, name='scatter', out_shape=(jax.ShapeDtypeS...]
    unnamed x16 -> x10, local copies, waits for them, and re-layouts: 4.75 us -> 0.02 us
    ppermute x3, waiting for transfers between devices: 2.08 us -> 4.9 us  [backward(): return lax.ppermute(value, axis, [(i + 1, i) for i in range(size - 1)])]
    all_to_all x1, starting transfers between devices: 10.8 us -> 9.17 us  [body(): lax.all_to_all(picked, ('gx', 'gy'), split_axis=0, concat_axis=0, tiled=T...]
    ppermute x3, waiting for transfers between devices: 0.01 us -> 1.41 us  [forward(): return lax.ppermute(value, axis, [(i, i + 1) for i in range(size - 1)])]
  transfers between devices with their start and end apart: 8 -> 8, of which waited for: 3 -> 4; matrix products, arithmetic and copies ran while one was open for 0% -> 0% of each run, Pallas kernels for 37% -> 36%
where the time goes in v4:
time: 121 us; the launch traced here: 120 us
  Pallas kernels  67.5 us (56%)
  starting transfers between devices  37.6 us (31%)
  waiting for transfers between devices  13.4 us (11%)
  between operations  1.46 us (1%)
    pallas_call x2, Pallas kernels, inner(): pl.pallas_call(lambda *refs: inner_kernel(start, count, *refs), name='inn...  17 us
    pallas_call x1, Pallas kernels, arrange(): pl.pallas_call(arrange_kernel, name='arrange', out_shape=(jax.ShapeDtypeS...  14.9 us
    ppermute x3, starting transfers between devices, forward(): return lax.ppermute(value, axis, [(i, i + 1) for i in range(size - 1)])  11.6 us
    all_to_all x1, starting transfers between devices, body(): lax.all_to_all(outgoing, ('gx', 'gy'), split_axis=0, concat_axis=0, tiled...  11.5 us
    pallas_call x1, Pallas kernels, outer(): pl.pallas_call(outer_kernel, name='outer', out_shape=jax.ShapeDtypeStruct...  9.84 us
    all_to_all x1, starting transfers between devices, body(): lax.all_to_all(picked, ('gx', 'gy'), split_axis=0, concat_axis=0, tiled=T...  9.17 us
    pallas_call x1, Pallas kernels, scatter(): pl.pallas_call(scatter_kernel, name='scatter', out_shape=(jax.ShapeDtypeS...  7.34 us
    all_to_all x1, waiting for transfers between devices, body(): lax.all_to_all(picked, ('gx', 'gy'), split_axis=0, concat_axis=0, tiled=T...  7.11 us
  transfers between devices with their start and end apart: 8, of which 4 were waited for; matrix products, arithmetic and copies ran while one was open for 0% of the time, Pallas kernels for 36%

profile of v4, /device:TPU:1, one launch (start us, length us, event | category | flops | bytes accessed | tf_op | source)
XLA Modules:
  0.0 120.1 jit_solution(1285895050095298009)
XLA Ops:
  1.3 3.5 %pack.1 = (f32[128,128]{1,0:T(8,128)}, s32[16,128]{1,0:T(8,128)}, s32[16,128]{1,0:T(8,128)}, bf16[192,192]{1,0:T(8,128)(2,1)}) custom-call(s32[1]{0:T(128)S(6)} %copy.14.count, f32[16,128]{1,0:T(8,128)} %bitcast.20, s32[16,128]{1,0:T(8,128)} %bitcast.21, s32[16,128]{1,0:T(8,128)} %bitcast.22, f32[90,90]{1,0:T(8,128)} %vertical_far.1), custom_call_target="tpu_custom_call" | custom-call | flops 1000000000 | bytes 1000000 | tf_op jit(solution)/shard_map/pack/pallas_call | solution.py:115
  4.8 11.5 %all-to-all-start = ((f32[128,1,128]{2,1,0:T(1,128)}), f32[128,1,128]{2,1,0:T(1,128)S(1)}, u32[]{:S(2)}, u32[]{:S(2)}) async-start(f32[128,1,128]{2,1,0:T(1,128)} %bitcast.18), calls=%async_computation | async-start | bytes 131072 | tf_op jit(solution)/shard_map/all_to_all | solution.py:845
  16.3 14.9 %arrange.1 = (bf16[5,16,96,512]{3,2,1,0:T(8,128)(2,1)}, f32[5,3,96,512]{3,2,1,0:T(8,128)}, f32[5,3,96,512]{3,2,1,0:T(8,128)}, bf16[16,96,256]{2,1,0:T(8,128)(2,1...) custom-call(bf16[10,1440,256]{2,1,0:T(8,128)(2,1)} %bitcast.19), custom_call_target="tpu_custom_call" | custom-call | flops 10000000000 | bytes 25000000 | tf_op jit(solution)/shard_map/arrange/pallas_call | solution.py:269
  31.3 3.7 %collective-permute-start.4 = (f32[5,3,96,512]{3,2,1,0:T(8,128)}, f32[5,3,96,512]{3,2,1,0:T(8,128)S(1)}, u32[]{:S(2)}, u32[]{:S(2)}) collective-permute-start(f32[5,3,96,512]{3,2,1,0:T(8,128)} %get-tuple-element.60), channel_id=1, source_target_pairs={{0,16},{16,32},{32,48},{48,64},{64,80},{80,96},{96,112},{1,17},{17... | collective-permute-start | bytes 8847368 | tf_op jit(solution)/shard_map/ppermute | solution.py:826
  34.9 1.9 %collective-permute-start.5 = (f32[5,3,96,512]{3,2,1,0:T(8,128)}, f32[5,3,96,512]{3,2,1,0:T(8,128)}, u32[]{:S(2)}, u32[]{:S(2)}) collective-permute-start(f32[5,3,96,512]{3,2,1,0:T(8,128)} %get-tuple-element.61), channel_id=1, source_target_pairs={{16,0},{32,16},{48,32},{64,48},{80,64},{96,80},{112,96},{17,1},{33... | collective-permute-start | bytes 8847368 | tf_op jit(solution)/shard_map/ppermute | solution.py:831
  36.8 0.1 pad_add_fusion.refs_3_.place
  36.9 7.3 %scatter.1 = (f32[16,96,256]{2,1,0:T(8,128)S(1)}, f32[16,96,512]{2,1,0:T(8,128)S(1)}, f32[5,96,128]{2,1,0:T(8,128)}, f32[5,96,128]{2,1,0:T(8,128)}, f32[48,256]{...) custom-call(f32[128,128]{1,0:T(8,128)S(1)} %bitcast.16, ...), custom_call_target="tpu_custom_call", output_to_operand_aliasing={{2}: (1, {}), {3}: (2, {})} | custom-call | flops 10000000000 | bytes 2000000 | tf_op jit(solution)/shard_map/scatter/pallas_call | solution.py:388
  44.3 3.2 %collective-permute-start = (f32[5,96,128]{2,1,0:T(8,128)}, f32[5,96,128]{2,1,0:T(8,128)S(1)}, u32[]{:S(2)}, u32[]{:S(2)}) collective-permute-start(f32[5,96,128]{2,1,0:T(8,128)} %get-tuple-element.46), channel_id=1, source_target_pairs={{0,1},{1,2},{2,3},{3,4},{4,5},{5,6},{6,7},{7,8},{8,9},{9,10},{10,1... | collective-permute-start | bytes 737288 | tf_op jit(solution)/shard_map/ppermute | solution.py:826
  47.5 1.5 %collective-permute-start.1 = (f32[5,96,128]{2,1,0:T(8,128)}, f32[5,96,128]{2,1,0:T(8,128)S(1)}, u32[]{:S(2)}, u32[]{:S(2)}) collective-permute-start(f32[5,96,128]{2,1,0:T(8,128)} %get-tuple-element.47), channel_id=1, source_target_pairs={{1,0},{2,1},{3,2},{4,3},{5,4},{6,5},{7,6},{8,7},{9,8},{10,9},{11,1... | collective-permute-start | bytes 737288 | tf_op jit(solution)/shard_map/ppermute | solution.py:831
  49.0 6.9 %inner.2 = (f32[2,6,96,512]{3,2,1,0:T(8,128)S(1)}, f32[10,96,512]{2,1,0:T(8,128)S(1)}) custom-call(bf16[5,16,96,512]{3,2,1,0:T(8,128)(2,1)S(1)} %copy-done.1, f32[16,96,512]{2,1,0:T(8,128)S(1)} %get-tuple-element.49.refs_1_, bf16[192,192]{1,0:T(8,128)(2,1)S(1)} %copy-done.4, s32[4]{0:T(128)S(1)} %pad_add_fusion.refs_3_.place), custom_call_target="tpu_custom_call" | custom-call | flops 4000000000 | bytes 4000000 | tf_op jit(solution)/shard_map/inner/pallas_call | solution.py:581
  55.9 0.5 collective-permute-done.1.right
  56.4 2.1 %strips.1 = (bf16[16,96,256]{2,1,0:T(8,128)(2,1)S(1)}, f32[16,96,256]{2,1,0:T(8,128)S(1)}, f32[3,3,96,256]{3,2,1,0:T(8,128)S(1)}, f32[3,3,96,256]{3,2,1,0:T(8,128)S(1)}) custom-call(bf16[16,96,256]{2,1,0:T(8,128)(2,1)S(1)} %copy-done, f32[16,96,256]{2,1,0:T(8,128)S(1)} %get-tuple-element.45.adjoint, f32[5,96,128]{2,1,0:T(8,128)S(1)} %collective-permute-done.left, ...), custom_call_target="tpu_custom_call" | custom-call | flops 1000000000 | bytes 4000000 | tf_op jit(solution)/shard_map/strips/pallas_call | solution.py:457
  58.5 4.8 %collective-permute-start.2 = (f32[3,3,96,256]{3,2,1,0:T(8,128)S(1)}, f32[3,3,96,256]{3,2,1,0:T(8,128)S(1)}, u32[]{:S(2)}, u32[]{:S(2)}) collective-permute-start(f32[3,3,96,256]{3,2,1,0:T(8,128)S(1)} %get-tuple-element.56), channel_id=1, source_target_pairs={{0,16},{16,32},{32,48},{48,64},{64,80},{80,96},{96,112},{1,17},{17... | collective-permute-start | bytes 2654216 | tf_op jit(solution)/shard_map/ppermute | solution.py:826
  63.3 1.9 %collective-permute-start.3 = (f32[3,3,96,256]{3,2,1,0:T(8,128)S(1)}, f32[3,3,96,256]{3,2,1,0:T(8,128)S(1)}, u32[]{:S(2)}, u32[]{:S(2)}) collective-permute-start(f32[3,3,96,256]{3,2,1,0:T(8,128)S(1)} %get-tuple-element.57), channel_id=1, source_target_pairs={{16,0},{32,16},{48,32},{64,48},{80,64},{96,80},{112,96},{17,1},{33... | collective-permute-start | bytes 2654216 | tf_op jit(solution)/shard_map/ppermute | solution.py:831
  65.2 10.1 %inner.3 = (f32[3,6,96,512]{3,2,1,0:T(8,128)S(1)}, f32[10,96,512]{2,1,0:T(8,128)S(1)}) custom-call(bf16[5,16,96,512]{3,2,1,0:T(8,128)(2,1)S(1)} %copy-done.1, f32[16,96,512]{2,1,0:T(8,128)S(1)} %get-tuple-element.49.refs_1_, bf16[192,192]{1,0:T(8,128)(2,1)S(1)} %copy-done.4, s32[4]{0:T(128)S(1)} %pad_add_fusion.refs_3_.place, ...), custom_call_target="tpu_custom_call" | custom-call | flops 6000000000 | bytes 6000000 | tf_op jit(solution)/shard_map/inner/pallas_call | solution.py:581
  75.3 1.4 %collective-permute-done.2.adj_t.halo_t = f32[3,3,96,256]{3,2,1,0:T(8,128)S(1)} collective-permute-done((f32[3,3,96,256]{3,2,1,0:T(8,128)S(1)}, f32[3,3,96,256]{3,2,1,0:T(8,128)S(1)}, u32[]{:S(2)}, u32[]{:S(2)}) %collective-permute-start.2) | collective-permute-done | bytes 884768 | tf_op jit(solution)/shard_map/ppermute | solution.py:826
  76.7 4.4 %collective-permute-done.3.adj_b.halo_b = f32[3,3,96,256]{3,2,1,0:T(8,128)S(1)} collective-permute-done((f32[3,3,96,256]{3,2,1,0:T(8,128)S(1)}, f32[3,3,96,256]{3,2,1,0:T(8,128)S(1)}, u32[]{:S(2)}, u32[]{:S(2)}) %collective-permute-start.3) | collective-permute-done | bytes 884768 | tf_op jit(solution)/shard_map/ppermute | solution.py:831
  81.1 9.8 %outer.1.border = f32[6,96,512]{2,1,0:T(8,128)S(1)} custom-call(bf16[5,16,96,512]{3,2,1,0:T(8,128)(2,1)S(1)} %copy-done.1, f32[5,3,96,512]{3,2,1,0:T(8,128)S(1)} %collective-permute-done.4.halo_t, f32[5,3,96,512]{3,2,1,0:T(8,128)} %collective-permute-done.5.halo_b, f32[3,3,96,256]{3,2,1,0:T(8,128)S(1)} %collective-permute-done.2.adj_t.halo_t, ...), custom_call_target="tpu_custom_call" | custom-call | flops 10000000000 | bytes 30000000 | tf_op jit(solution)/shard_map/outer/pallas_call | solution.py:665
  90.9 4.9 %edge.1.field = f32[16,96,256]{2,1,0:T(8,128)S(1)} custom-call(bf16[16,96,256]{2,1,0:T(8,128)(2,1)S(1)} %get-tuple-element.54.strip, f32[16,96,256]{2,1,0:T(8,128)S(1)} %get-tuple-element.55.adj, f32[3,3,96,256]{3,2,1,0:T(8,128)S(1)} %collective-permute-done.2.adj_t.halo_t, f32[3,3,96,256]{3,2,1,0:T(8,128)S(1)} %collective-permute-done.3.adj_b.halo_b, ...), custom_call_target="tpu_custom_call" | custom-call | flops 4000000000 | bytes 8000000 | tf_op jit(solution)/shard_map/edge/pallas_call | solution.py:735
  95.9 4.3 %gather.1 = f32[128,128]{1,0:T(8,128)} custom-call(f32[16,96,256]{2,1,0:T(8,128)S(1)} %edge.1.field, f32[48,256]{1,0:T(8,128)S(1)} %get-tuple-element.64.level, f32[48,256]{1,0:T(8,128)S(1)} %get-tuple-element.65.column, s32[24,256]{1,0:T(8,128)S(1)} %get-tuple-element.66.pos, s32[1,128]{1,0:T(1,128)S(1)} %get-tuple-element.67.rows_of), custom_call_target="tpu_custom_call" | custom-call | flops 10000000000 | bytes 2000000 | tf_op jit(solution)/shard_map/gather/pallas_call | solution.py:777
  100.2 9.2 %all-to-all-start.1 = ((f32[128,1,128]{2,1,0:T(1,128)}), f32[128,1,128]{2,1,0:T(1,128)S(1)}, u32[]{:S(2)}, u32[]{:S(2)}) async-start(f32[128,1,128]{2,1,0:T(1,128)} %bitcast.11), calls=%async_computation.1 | async-start | bytes 131072 | tf_op jit(solution)/shard_map/all_to_all | solution.py:864
  109.4 2.5 %restore.1 = f32[1440,256]{1,0:T(8,128)} custom-call(f32[16,96,256]{2,1,0:T(8,128)S(1)} %edge.1.field), custom_call_target="tpu_custom_call" | custom-call | flops 1000000000 | bytes 3000000 | tf_op jit(solution)/shard_map/restore/pallas_call | solution.py:812
  111.8 7.1 %all-to-all-done.1 = f32[128,1,128]{2,1,0:T(1,128)S(1)} async-done(((f32[128,1,128]{2,1,0:T(1,128)}), f32[128,1,128]{2,1,0:T(1,128)S(1)}, u32[]{:S(2)}, u32[]{:S(2)}) %all-to-all-start.1) | async-done | bytes 65568 | tf_op jit(solution)/shard_map/all_to_all | solution.py:864
  118.9 1.2 unpack.1
  (14 shorter events, 0.0 us)
Async XLA Ops:
  4.8 26.5 %all-to-all-start = ((f32[128,1,128]{2,1,0:T(1,128)}), f32[128,1,128]{2,1,0:T(1,128)S(1)}, u32[]{:S(2)}, u32[]{:S(2)}) async-start(f32[128,1,128]{2,1,0:T(1,128)} %bitcast.18), calls=%async_computation | async-start | bytes 131072 | tf_op jit(solution)/shard_map/all_to_all | solution.py:845
  31.3 49.8 %collective-permute-start.4 = (f32[5,3,96,512]{3,2,1,0:T(8,128)}, f32[5,3,96,512]{3,2,1,0:T(8,128)S(1)}, u32[]{:S(2)}, u32[]{:S(2)}) collective-permute-start(f32[5,3,96,512]{3,2,1,0:T(8,128)} %get-tuple-element.60), channel_id=1, source_target_pairs={{0,16},{16,32},{32,48},{48,64},{64,80},{80,96},{96,112},{1,17},{17... | collective-permute-start | bytes 8847368 | tf_op jit(solution)/shard_map/ppermute | solution.py:826
  34.9 46.2 %collective-permute-start.5 = (f32[5,3,96,512]{3,2,1,0:T(8,128)}, f32[5,3,96,512]{3,2,1,0:T(8,128)}, u32[]{:S(2)}, u32[]{:S(2)}) collective-permute-start(f32[5,3,96,512]{3,2,1,0:T(8,128)} %get-tuple-element.61), channel_id=1, source_target_pairs={{16,0},{32,16},{48,32},{64,48},{80,64},{96,80},{112,96},{17,1},{33... | collective-permute-start | bytes 8847368 | tf_op jit(solution)/shard_map/ppermute | solution.py:831
  36.9 12.0 %copy-start.1 = (bf16[5,16,96,512]{3,2,1,0:T(8,128)(2,1)S(1)}, bf16[5,16,96,512]{3,2,1,0:T(8,128)(2,1)}, u32[]{:S(2)}) copy-start(bf16[5,16,96,512]{3,2,1,0:T(8,128)(2,1)} %get-tuple-element.48.refs_0_.ens) | copy-start | bytes 23592964
  36.9 12.0 %copy-start.4 = (bf16[192,192]{1,0:T(8,128)(2,1)S(1)}, bf16[192,192]{1,0:T(8,128)(2,1)}, u32[]{:S(2)}) copy-start(bf16[192,192]{1,0:T(8,128)(2,1)} %get-tuple-element.50.refs_2_.weights) | copy-start | bytes 221188
  44.3 11.6 %collective-permute-start = (f32[5,96,128]{2,1,0:T(8,128)}, f32[5,96,128]{2,1,0:T(8,128)S(1)}, u32[]{:S(2)}, u32[]{:S(2)}) collective-permute-start(f32[5,96,128]{2,1,0:T(8,128)} %get-tuple-element.46), channel_id=1, source_target_pairs={{0,1},{1,2},{2,3},{3,4},{4,5},{5,6},{6,7},{7,8},{8,9},{9,10},{10,1... | collective-permute-start | bytes 737288 | tf_op jit(solution)/shard_map/ppermute | solution.py:826
  47.5 9.0 %collective-permute-start.1 = (f32[5,96,128]{2,1,0:T(8,128)}, f32[5,96,128]{2,1,0:T(8,128)S(1)}, u32[]{:S(2)}, u32[]{:S(2)}) collective-permute-start(f32[5,96,128]{2,1,0:T(8,128)} %get-tuple-element.47), channel_id=1, source_target_pairs={{1,0},{2,1},{3,2},{4,3},{5,4},{6,5},{7,6},{8,7},{9,8},{10,9},{11,1... | collective-permute-start | bytes 737288 | tf_op jit(solution)/shard_map/ppermute | solution.py:831
  49.0 7.5 %copy-start = (bf16[16,96,256]{2,1,0:T(8,128)(2,1)S(1)}, bf16[16,96,256]{2,1,0:T(8,128)(2,1)}, u32[]{:S(2)}) copy-start(bf16[16,96,256]{2,1,0:T(8,128)(2,1)} %get-tuple-element.38.strip) | copy-start | bytes 2359300
  58.5 18.2 %collective-permute-start.2 = (f32[3,3,96,256]{3,2,1,0:T(8,128)S(1)}, f32[3,3,96,256]{3,2,1,0:T(8,128)S(1)}, u32[]{:S(2)}, u32[]{:S(2)}) collective-permute-start(f32[3,3,96,256]{3,2,1,0:T(8,128)S(1)} %get-tuple-element.56), channel_id=1, source_target_pairs={{0,16},{16,32},{32,48},{48,64},{64,80},{80,96},{96,112},{1,17},{17... | collective-permute-start | bytes 2654216 | tf_op jit(solution)/shard_map/ppermute | solution.py:826
  63.3 17.8 %collective-permute-start.3 = (f32[3,3,96,256]{3,2,1,0:T(8,128)S(1)}, f32[3,3,96,256]{3,2,1,0:T(8,128)S(1)}, u32[]{:S(2)}, u32[]{:S(2)}) collective-permute-start(f32[3,3,96,256]{3,2,1,0:T(8,128)S(1)} %get-tuple-element.57), channel_id=1, source_target_pairs={{16,0},{32,16},{48,32},{64,48},{80,64},{96,80},{112,96},{17,1},{33... | collective-permute-start | bytes 2654216 | tf_op jit(solution)/shard_map/ppermute | solution.py:831
  100.2 18.8 %copy-start.2 = (s32[16,128]{1,0:T(8,128)S(1)}, s32[16,128]{1,0:T(8,128)}, u32[]{:S(2)}) copy-start(s32[16,128]{1,0:T(8,128)} %get-tuple-element.68.tgt) | copy-start | bytes 24580
  100.2 18.8 %copy-start.3 = (s32[16,128]{1,0:T(8,128)S(1)}, s32[16,128]{1,0:T(8,128)}, u32[]{:S(2)}) copy-start(s32[16,128]{1,0:T(8,128)} %get-tuple-element.69.rank) | copy-start | bytes 24580
  100.2 18.7 %all-to-all-start.1 = ((f32[128,1,128]{2,1,0:T(1,128)}), f32[128,1,128]{2,1,0:T(1,128)S(1)}, u32[]{:S(2)}, u32[]{:S(2)}) async-start(f32[128,1,128]{2,1,0:T(1,128)} %bitcast.11), calls=%async_computation.1 | async-start | bytes 131072 | tf_op jit(solution)/shard_map/all_to_all | solution.py:864

commit v5 on v4

--- a/solution.py
+++ b/solution.py
@@ -154,9 +154,9 @@
     )(back, tgt, rank).reshape(SLOTS)
 
 
-def strip_place(lane):
+def strip_place(lane, members=MEM):
     j = lane % HALF
-    return j // PAIRS, jnp.where(j < MEM * PAIRS, j % PAIRS * 2 + lane // HALF, -1)
+    return j // PAIRS, jnp.where(j < members * PAIRS, j % PAIRS * 2 + lane // HALF, -1)
 
 
 def natural(place):
@@ -417,24 +417,22 @@
 
 
 def strips_kernel(strip, adjoint, left, right, ens_out, out, up, down):
-    member, member_c = strip_place(iota((COLS, COLS), 1))
+    lane = iota((COLS, COLS), 1)
+    member, member_c = strip_place(lane, MEM + 1)
     y = natural(iota((COLS, COLS), 0))
     own = one_hot(member_c == jnp.where(y < 6, 3 + y, jnp.where(y >= 250, y - 241, -2)))
     from_lane = iota((HALF, COLS), 0)
     member_c, member = member_c[:HALF], member[:HALF]
     pieces = [split(side[4], 2) for side in (left, right)]
+    ens_lanes = iota((PAD, COLS), 1) % HALF < MEM * PAIRS
     for x in range(ROWS):
-        value = strip[x].astype(F32)
+        ens_value = strip[x].astype(F32)
         first = x % 4 * 30 + 3 * member
         for side, shift in ((left, 0), (right, 15)):
-            inside = (member_c >= shift) & (member_c < shift + 3)
+            inside = (member_c >= shift) & (member_c < shift + 3) & (member < MEM)
             spot = one_hot(inside & (from_lane == first + member_c - shift))
-            value = value + dot(side[x // 4].astype(BF16), spot)
-        ens_out[x] = value.astype(BF16)
-        if x < EDGE:
-            up[2, x] = value
-        if x >= ROWS - EDGE:
-            down[2, x - (ROWS - EDGE)] = value
+            ens_value = ens_value + dot(side[x // 4].astype(BF16), spot)
+        ens_out[x] = ens_value.astype(BF16)
         value = jnp.zeros((PAD, COLS), F32)
         for piece in split(adjoint[x], 2):
             value = value + dot(piece, own)
@@ -444,12 +442,10 @@
             for piece in side:
                 value = value + dot(piece, spot)
         out[x] = value
-        if x < EDGE:
-            up[0, x] = adjoint[x]
-            up[1, x] = value
-        if x >= ROWS - EDGE:
-            down[0, x - (ROWS - EDGE)] = adjoint[x]
-            down[1, x - (ROWS - EDGE)] = value
+        for target, start in ((up, 0), (down, ROWS - EDGE)):
+            if start <= x < start + EDGE:
+                target[0, x - start] = adjoint[x]
+                target[1, x - start] = jnp.where(ens_lanes, ens_value, value)
 
 
 def strips(strip, adjoint, left, right):
@@ -460,8 +456,8 @@
         out_shape=(
             jax.ShapeDtypeStruct((ROWS, PAD, COLS), BF16),
             jax.ShapeDtypeStruct((ROWS, PAD, COLS), F32),
-            jax.ShapeDtypeStruct((3, EDGE, PAD, COLS), F32),
-            jax.ShapeDtypeStruct((3, EDGE, PAD, COLS), F32),
+            jax.ShapeDtypeStruct((2, EDGE, PAD, COLS), F32),
+            jax.ShapeDtypeStruct((2, EDGE, PAD, COLS), F32),
         ),
         in_specs=[spec] * 4,
         out_specs=(spec,) * 4,
@@ -633,7 +629,7 @@
             for copy in fetch(duo):
                 copy.wait()
 
-            @pl.loop(0, PAD // 16)
+            @pl.loop(0, PAD // 16, unroll=True)
             def _(group):
                 at = pl.ds(pl.multiple_of(group * 16, 16), 16)
 
@@ -681,11 +677,18 @@
     )(ens, halo_t, halo_b, adj_t, adj_b, border0, border1, weights)
 
 
-def edge_kernel(strip, adj, halo_t, halo_b, weights, place, inside, border, out, field):
+def edge_kernel(strip, adj, halo_t, halo_b, weights, place, inside, border, out, field, halo_adj):
     top_open = jnp.where(place[0] == 0, 0.0, 1.0)
     bottom_open = jnp.where(place[0] == place[2], 0.0, 1.0)
     left_open = jnp.where(place[1] == 0, 0.0, 1.0)
     right_open = jnp.where(place[1] == place[3], 0.0, 1.0)
+    member, source = strip_place(iota((COLS, COLS), 0), MEM + 1)
+    target = strip_place(iota((COLS, COLS), 1))[1]
+    repeat = one_hot((member == MEM) & (source == target))
+    for i, halo in enumerate((halo_t, halo_b)):
+        for x in range(EDGE):
+            high, low = split(halo[1, x], 2)
+            halo_adj[i * EDGE + x] = dot(high, repeat) + dot(low, repeat)
 
     @pl.loop(0, PAD // 16)
     def _(group):
@@ -703,9 +706,9 @@
 
         def get(x):
             if x < 0:
-                return halo_t[2, x + EDGE, at, :] * halo_t[1, x + EDGE, at, :]
+                return halo_t[1, x + EDGE, at, :] * halo_adj[x + EDGE, at, :]
             if x >= ROWS:
-                return halo_b[2, x - ROWS, at, :] * halo_b[1, x - ROWS, at, :]
+                return halo_b[1, x - ROWS, at, :] * halo_adj[x - ROWS + EDGE, at, :]
             return strip[x, at, :].astype(F32) * adj[x, at, :]
 
         def emit(x, value):
@@ -738,7 +741,7 @@
         out_shape=jax.ShapeDtypeStruct((ROWS, PAD, COLS), F32),
         in_specs=[spec] * 5 + [pl.BlockSpec(memory_space=pltpu.SMEM)] + [spec] * 2,
         out_specs=spec,
-        scratch_shapes=[pltpu.VMEM((ROWS, 2 * PAD, COLS), BF16)],
+        scratch_shapes=[pltpu.VMEM((ROWS, 2 * PAD, COLS), BF16), pltpu.VMEM((2 * EDGE, PAD, COLS), F32)],
         compiler_params=params(),
         cost_estimate=cost(4 * 10**9, 8 * 10**6),
     )(strip, adj, halo_t, halo_b, weights, place, inside, border)

time: 121 us -> 115 us (0.950)
  waiting for transfers between devices: 13.4 us -> 10.2 us
  Pallas kernels: 67.5 us -> 65.1 us
    pallas_call x1, Pallas kernels: 9.84 us -> 7.04 us  [outer(): pl.pallas_call(outer_kernel, name='outer', out_shape=jax.ShapeDtypeStruct...]
    ppermute x3, waiting for transfers between devices: 4.9 us -> 3.11 us  [backward(): return lax.ppermute(value, axis, [(i + 1, i) for i in range(size - 1)])]
    ppermute x3, waiting for transfers between devices: 1.41 us -> 0.01 us  [forward(): return lax.ppermute(value, axis, [(i, i + 1) for i in range(size - 1)])]
  transfers between devices with their start and end apart: 8 -> 8, of which waited for: 4 -> 3; matrix products, arithmetic and copies ran while one was open for 0% -> 0% of each run, Pallas kernels for 36% -> 38%
where the time goes in v5:
time: 115 us; the launch traced here: 114 us
  Pallas kernels  65.1 us (57%)
  starting transfers between devices  37.6 us (33%)
  waiting for transfers between devices  10.2 us (9%)
  between operations  1.46 us (1%)
    pallas_call x2, Pallas kernels, inner(): pl.pallas_call(lambda *refs: inner_kernel(start, count, *refs), name='inn...  17 us
    pallas_call x1, Pallas kernels, arrange(): pl.pallas_call(arrange_kernel, name='arrange', out_shape=(jax.ShapeDtypeS...  14.9 us
    ppermute x3, starting transfers between devices, forward(): return lax.ppermute(value, axis, [(i, i + 1) for i in range(size - 1)])  11.6 us
    all_to_all x1, starting transfers between devices, body(): lax.all_to_all(outgoing, ('gx', 'gy'), split_axis=0, concat_axis=0, tiled...  11.5 us
    all_to_all x1, starting transfers between devices, body(): lax.all_to_all(picked, ('gx', 'gy'), split_axis=0, concat_axis=0, tiled=T...  9.17 us
    pallas_call x1, Pallas kernels, scatter(): pl.pallas_call(scatter_kernel, name='scatter', out_shape=(jax.ShapeDtypeS...  7.34 us
    all_to_all x1, waiting for transfers between devices, body(): lax.all_to_all(picked, ('gx', 'gy'), split_axis=0, concat_axis=0, tiled=T...  7.11 us
    pallas_call x1, Pallas kernels, outer(): pl.pallas_call(outer_kernel, name='outer', out_shape=jax.ShapeDtypeStruct...  7.04 us
  transfers between devices with their start and end apart: 8, of which 3 were waited for; matrix products, arithmetic and copies ran while one was open for 0% of the time, Pallas kernels for 38%

profile of v5, /device:TPU:1, one launch (start us, length us, event | category | flops | bytes accessed | tf_op | source)
XLA Modules:
  0.0 114.5 jit_solution(8939776851629610649)
XLA Ops:
  1.3 3.5 %pack.1 = (f32[128,128]{1,0:T(8,128)}, s32[16,128]{1,0:T(8,128)}, s32[16,128]{1,0:T(8,128)}, bf16[192,192]{1,0:T(8,128)(2,1)}) custom-call(s32[1]{0:T(128)S(6)} %copy.14.count, f32[16,128]{1,0:T(8,128)} %bitcast.20, s32[16,128]{1,0:T(8,128)} %bitcast.21, s32[16,128]{1,0:T(8,128)} %bitcast.22, f32[90,90]{1,0:T(8,128)} %vertical_far.1), custom_call_target="tpu_custom_call" | custom-call | flops 1000000000 | bytes 1000000 | tf_op jit(solution)/shard_map/pack/pallas_call | solution.py:115
  4.8 11.5 %all-to-all-start = ((f32[128,1,128]{2,1,0:T(1,128)}), f32[128,1,128]{2,1,0:T(1,128)S(1)}, u32[]{:S(2)}, u32[]{:S(2)}) async-start(f32[128,1,128]{2,1,0:T(1,128)} %bitcast.18), calls=%async_computation | async-start | bytes 131072 | tf_op jit(solution)/shard_map/all_to_all | solution.py:848
  16.3 14.9 %arrange.1 = (bf16[5,16,96,512]{3,2,1,0:T(8,128)(2,1)}, f32[5,3,96,512]{3,2,1,0:T(8,128)}, f32[5,3,96,512]{3,2,1,0:T(8,128)}, bf16[16,96,256]{2,1,0:T(8,128)(2,1...) custom-call(bf16[10,1440,256]{2,1,0:T(8,128)(2,1)} %bitcast.19), custom_call_target="tpu_custom_call" | custom-call | flops 10000000000 | bytes 25000000 | tf_op jit(solution)/shard_map/arrange/pallas_call | solution.py:269
  31.3 3.7 %collective-permute-start.4 = (f32[5,3,96,512]{3,2,1,0:T(8,128)}, f32[5,3,96,512]{3,2,1,0:T(8,128)S(1)}, u32[]{:S(2)}, u32[]{:S(2)}) collective-permute-start(f32[5,3,96,512]{3,2,1,0:T(8,128)} %get-tuple-element.60), channel_id=1, source_target_pairs={{0,16},{16,32},{32,48},{48,64},{64,80},{80,96},{96,112},{1,17},{17... | collective-permute-start | bytes 8847368 | tf_op jit(solution)/shard_map/ppermute | solution.py:829
  34.9 1.9 %collective-permute-start.5 = (f32[5,3,96,512]{3,2,1,0:T(8,128)}, f32[5,3,96,512]{3,2,1,0:T(8,128)}, u32[]{:S(2)}, u32[]{:S(2)}) collective-permute-start(f32[5,3,96,512]{3,2,1,0:T(8,128)} %get-tuple-element.61), channel_id=1, source_target_pairs={{16,0},{32,16},{48,32},{64,48},{80,64},{96,80},{112,96},{17,1},{33... | collective-permute-start | bytes 8847368 | tf_op jit(solution)/shard_map/ppermute | solution.py:834
  36.8 0.1 pad_add_fusion.refs_3_.place
  36.9 7.3 %scatter.1 = (f32[16,96,256]{2,1,0:T(8,128)S(1)}, f32[16,96,512]{2,1,0:T(8,128)S(1)}, f32[5,96,128]{2,1,0:T(8,128)}, f32[5,96,128]{2,1,0:T(8,128)}, f32[48,256]{...) custom-call(f32[128,128]{1,0:T(8,128)S(1)} %bitcast.16, ...), custom_call_target="tpu_custom_call", output_to_operand_aliasing={{2}: (1, {}), {3}: (2, {})} | custom-call | flops 10000000000 | bytes 2000000 | tf_op jit(solution)/shard_map/scatter/pallas_call | solution.py:388
  44.3 3.2 %collective-permute-start = (f32[5,96,128]{2,1,0:T(8,128)}, f32[5,96,128]{2,1,0:T(8,128)S(1)}, u32[]{:S(2)}, u32[]{:S(2)}) collective-permute-start(f32[5,96,128]{2,1,0:T(8,128)} %get-tuple-element.46), channel_id=1, source_target_pairs={{0,1},{1,2},{2,3},{3,4},{4,5},{5,6},{6,7},{7,8},{8,9},{9,10},{10,1... | collective-permute-start | bytes 737288 | tf_op jit(solution)/shard_map/ppermute | solution.py:829
  47.5 1.5 %collective-permute-start.1 = (f32[5,96,128]{2,1,0:T(8,128)}, f32[5,96,128]{2,1,0:T(8,128)S(1)}, u32[]{:S(2)}, u32[]{:S(2)}) collective-permute-start(f32[5,96,128]{2,1,0:T(8,128)} %get-tuple-element.47), channel_id=1, source_target_pairs={{1,0},{2,1},{3,2},{4,3},{5,4},{6,5},{7,6},{8,7},{9,8},{10,9},{11,1... | collective-permute-start | bytes 737288 | tf_op jit(solution)/shard_map/ppermute | solution.py:834
  49.0 0.0 copy-start
  49.0 6.9 %inner.2 = (f32[2,6,96,512]{3,2,1,0:T(8,128)S(1)}, f32[10,96,512]{2,1,0:T(8,128)S(1)}) custom-call(bf16[5,16,96,512]{3,2,1,0:T(8,128)(2,1)S(1)} %copy-done.1, f32[16,96,512]{2,1,0:T(8,128)S(1)} %get-tuple-element.49.refs_1_, bf16[192,192]{1,0:T(8,128)(2,1)S(1)} %copy-done.4, s32[4]{0:T(128)S(1)} %pad_add_fusion.refs_3_.place), custom_call_target="tpu_custom_call" | custom-call | flops 4000000000 | bytes 4000000 | tf_op jit(solution)/shard_map/inner/pallas_call | solution.py:577
  55.9 0.5 collective-permute-done.1.right
  56.4 2.1 %strips.1 = (bf16[16,96,256]{2,1,0:T(8,128)(2,1)S(1)}, f32[16,96,256]{2,1,0:T(8,128)S(1)}, f32[2,3,96,256]{3,2,1,0:T(8,128)S(1)}, f32[2,3,96,256]{3,2,1,0:T(8,128)S(1)}) custom-call(bf16[16,96,256]{2,1,0:T(8,128)(2,1)S(1)} %copy-done, f32[16,96,256]{2,1,0:T(8,128)S(1)} %get-tuple-element.45.adjoint, f32[5,96,128]{2,1,0:T(8,128)S(1)} %collective-permute-done.left, ...), custom_call_target="tpu_custom_call" | custom-call | flops 1000000000 | bytes 4000000 | tf_op jit(solution)/shard_map/strips/pallas_call | solution.py:453
  58.5 4.8 %collective-permute-start.2 = (f32[2,3,96,256]{3,2,1,0:T(8,128)S(1)}, f32[2,3,96,256]{3,2,1,0:T(8,128)S(1)}, u32[]{:S(2)}, u32[]{:S(2)}) collective-permute-start(f32[2,3,96,256]{3,2,1,0:T(8,128)S(1)} %get-tuple-element.56), channel_id=1, source_target_pairs={{0,16},{16,32},{32,48},{48,64},{64,80},{80,96},{96,112},{1,17},{17... | collective-permute-start | bytes 1769480 | tf_op jit(solution)/shard_map/ppermute | solution.py:829
  63.3 1.9 %collective-permute-start.3 = (f32[2,3,96,256]{3,2,1,0:T(8,128)S(1)}, f32[2,3,96,256]{3,2,1,0:T(8,128)S(1)}, u32[]{:S(2)}, u32[]{:S(2)}) collective-permute-start(f32[2,3,96,256]{3,2,1,0:T(8,128)S(1)} %get-tuple-element.57), channel_id=1, source_target_pairs={{16,0},{32,16},{48,32},{64,48},{80,64},{96,80},{112,96},{17,1},{33... | collective-permute-start | bytes 1769480 | tf_op jit(solution)/shard_map/ppermute | solution.py:834
  65.2 10.1 %inner.3 = (f32[3,6,96,512]{3,2,1,0:T(8,128)S(1)}, f32[10,96,512]{2,1,0:T(8,128)S(1)}) custom-call(bf16[5,16,96,512]{3,2,1,0:T(8,128)(2,1)S(1)} %copy-done.1, f32[16,96,512]{2,1,0:T(8,128)S(1)} %get-tuple-element.49.refs_1_, bf16[192,192]{1,0:T(8,128)(2,1)S(1)} %copy-done.4, s32[4]{0:T(128)S(1)} %pad_add_fusion.refs_3_.place, ...), custom_call_target="tpu_custom_call" | custom-call | flops 6000000000 | bytes 6000000 | tf_op jit(solution)/shard_map/inner/pallas_call | solution.py:577
  75.3 2.6 %collective-permute-done.3.adj_b.halo_b = f32[2,3,96,256]{3,2,1,0:T(8,128)S(1)} collective-permute-done((f32[2,3,96,256]{3,2,1,0:T(8,128)S(1)}, f32[2,3,96,256]{3,2,1,0:T(8,128)S(1)}, u32[]{:S(2)}, u32[]{:S(2)}) %collective-permute-start.3) | collective-permute-done | bytes 589856 | tf_op jit(solution)/shard_map/ppermute | solution.py:834
  77.9 7.0 %outer.1.border = f32[6,96,512]{2,1,0:T(8,128)S(1)} custom-call(bf16[5,16,96,512]{3,2,1,0:T(8,128)(2,1)S(1)} %copy-done.1, f32[5,3,96,512]{3,2,1,0:T(8,128)S(1)} %collective-permute-done.4.halo_t, f32[5,3,96,512]{3,2,1,0:T(8,128)} %collective-permute-done.5.halo_b, f32[2,3,96,256]{3,2,1,0:T(8,128)S(1)} %collective-permute-done.2.adj_t.halo_t, ...), custom_call_target="tpu_custom_call" | custom-call | flops 10000000000 | bytes 30000000 | tf_op jit(solution)/shard_map/outer/pallas_call | solution.py:661
  85.0 5.3 %edge.1.field = f32[16,96,256]{2,1,0:T(8,128)S(1)} custom-call(bf16[16,96,256]{2,1,0:T(8,128)(2,1)S(1)} %get-tuple-element.54.strip, f32[16,96,256]{2,1,0:T(8,128)S(1)} %get-tuple-element.55.adj, f32[2,3,96,256]{3,2,1,0:T(8,128)S(1)} %collective-permute-done.2.adj_t.halo_t, f32[2,3,96,256]{3,2,1,0:T(8,128)S(1)} %collective-permute-done.3.adj_b.halo_b, ...), custom_call_target="tpu_custom_call" | custom-call | flops 4000000000 | bytes 8000000 | tf_op jit(solution)/shard_map/edge/pallas_call | solution.py:738
  90.3 4.3 %gather.1 = f32[128,128]{1,0:T(8,128)} custom-call(f32[16,96,256]{2,1,0:T(8,128)S(1)} %edge.1.field, f32[48,256]{1,0:T(8,128)S(1)} %get-tuple-element.64.level, f32[48,256]{1,0:T(8,128)S(1)} %get-tuple-element.65.column, s32[24,256]{1,0:T(8,128)S(1)} %get-tuple-element.66.pos, s32[1,128]{1,0:T(1,128)S(1)} %get-tuple-element.67.rows_of), custom_call_target="tpu_custom_call" | custom-call | flops 10000000000 | bytes 2000000 | tf_op jit(solution)/shard_map/gather/pallas_call | solution.py:780
  94.6 9.2 %all-to-all-start.1 = ((f32[128,1,128]{2,1,0:T(1,128)}), f32[128,1,128]{2,1,0:T(1,128)S(1)}, u32[]{:S(2)}, u32[]{:S(2)}) async-start(f32[128,1,128]{2,1,0:T(1,128)} %bitcast.11), calls=%async_computation.1 | async-start | bytes 131072 | tf_op jit(solution)/shard_map/all_to_all | solution.py:867
  103.7 2.5 %restore.1 = f32[1440,256]{1,0:T(8,128)} custom-call(f32[16,96,256]{2,1,0:T(8,128)S(1)} %edge.1.field), custom_call_target="tpu_custom_call" | custom-call | flops 1000000000 | bytes 3000000 | tf_op jit(solution)/shard_map/restore/pallas_call | solution.py:815
  106.2 7.1 %all-to-all-done.1 = f32[128,1,128]{2,1,0:T(1,128)S(1)} async-done(((f32[128,1,128]{2,1,0:T(1,128)}), f32[128,1,128]{2,1,0:T(1,128)S(1)}, u32[]{:S(2)}, u32[]{:S(2)}) %all-to-all-start.1) | async-done | bytes 65568 | tf_op jit(solution)/shard_map/all_to_all | solution.py:867
  113.3 1.2 %unpack.1 = f32[16,128]{1,0:T(8,128)} custom-call(f32[128,128]{1,0:T(8,128)S(1)} %bitcast.17, s32[16,128]{1,0:T(8,128)S(1)} %copy-done.2, s32[16,128]{1,0:T(8,128)S(1)} %copy-done.3), custom_call_target="tpu_custom_call" | custom-call | flops 100000000 | bytes 100000 | tf_op jit(solution)/shard_map/unpack/pallas_call | solution.py:146
  (14 shorter events, 0.0 us)
Async XLA Ops:
  4.8 26.5 %all-to-all-start = ((f32[128,1,128]{2,1,0:T(1,128)}), f32[128,1,128]{2,1,0:T(1,128)S(1)}, u32[]{:S(2)}, u32[]{:S(2)}) async-start(f32[128,1,128]{2,1,0:T(1,128)} %bitcast.18), calls=%async_computation | async-start | bytes 131072 | tf_op jit(solution)/shard_map/all_to_all | solution.py:848
  31.3 46.7 %collective-permute-start.4 = (f32[5,3,96,512]{3,2,1,0:T(8,128)}, f32[5,3,96,512]{3,2,1,0:T(8,128)S(1)}, u32[]{:S(2)}, u32[]{:S(2)}) collective-permute-start(f32[5,3,96,512]{3,2,1,0:T(8,128)} %get-tuple-element.60), channel_id=1, source_target_pairs={{0,16},{16,32},{32,48},{48,64},{64,80},{80,96},{96,112},{1,17},{17... | collective-permute-start | bytes 8847368 | tf_op jit(solution)/shard_map/ppermute | solution.py:829
  34.9 43.0 %collective-permute-start.5 = (f32[5,3,96,512]{3,2,1,0:T(8,128)}, f32[5,3,96,512]{3,2,1,0:T(8,128)}, u32[]{:S(2)}, u32[]{:S(2)}) collective-permute-start(f32[5,3,96,512]{3,2,1,0:T(8,128)} %get-tuple-element.61), channel_id=1, source_target_pairs={{16,0},{32,16},{48,32},{64,48},{80,64},{96,80},{112,96},{17,1},{33... | collective-permute-start | bytes 8847368 | tf_op jit(solution)/shard_map/ppermute | solution.py:834
  36.9 12.0 %copy-start.1 = (bf16[5,16,96,512]{3,2,1,0:T(8,128)(2,1)S(1)}, bf16[5,16,96,512]{3,2,1,0:T(8,128)(2,1)}, u32[]{:S(2)}) copy-start(bf16[5,16,96,512]{3,2,1,0:T(8,128)(2,1)} %get-tuple-element.48.refs_0_.ens) | copy-start | bytes 23592964
  36.9 12.0 %copy-start.4 = (bf16[192,192]{1,0:T(8,128)(2,1)S(1)}, bf16[192,192]{1,0:T(8,128)(2,1)}, u32[]{:S(2)}) copy-start(bf16[192,192]{1,0:T(8,128)(2,1)} %get-tuple-element.50.refs_2_.weights) | copy-start | bytes 221188
  44.3 11.6 %collective-permute-start = (f32[5,96,128]{2,1,0:T(8,128)}, f32[5,96,128]{2,1,0:T(8,128)S(1)}, u32[]{:S(2)}, u32[]{:S(2)}) collective-permute-start(f32[5,96,128]{2,1,0:T(8,128)} %get-tuple-element.46), channel_id=1, source_target_pairs={{0,1},{1,2},{2,3},{3,4},{4,5},{5,6},{6,7},{7,8},{8,9},{9,10},{10,1... | collective-permute-start | bytes 737288 | tf_op jit(solution)/shard_map/ppermute | solution.py:829
  47.5 9.0 %collective-permute-start.1 = (f32[5,96,128]{2,1,0:T(8,128)}, f32[5,96,128]{2,1,0:T(8,128)S(1)}, u32[]{:S(2)}, u32[]{:S(2)}) collective-permute-start(f32[5,96,128]{2,1,0:T(8,128)} %get-tuple-element.47), channel_id=1, source_target_pairs={{1,0},{2,1},{3,2},{4,3},{5,4},{6,5},{7,6},{8,7},{9,8},{10,9},{11,1... | collective-permute-start | bytes 737288 | tf_op jit(solution)/shard_map/ppermute | solution.py:834
  49.0 7.5 %copy-start = (bf16[16,96,256]{2,1,0:T(8,128)(2,1)S(1)}, bf16[16,96,256]{2,1,0:T(8,128)(2,1)}, u32[]{:S(2)}) copy-start(bf16[16,96,256]{2,1,0:T(8,128)(2,1)} %get-tuple-element.38.strip) | copy-start | bytes 2359300
  58.5 16.8 %collective-permute-start.2 = (f32[2,3,96,256]{3,2,1,0:T(8,128)S(1)}, f32[2,3,96,256]{3,2,1,0:T(8,128)S(1)}, u32[]{:S(2)}, u32[]{:S(2)}) collective-permute-start(f32[2,3,96,256]{3,2,1,0:T(8,128)S(1)} %get-tuple-element.56), channel_id=1, source_target_pairs={{0,16},{16,32},{32,48},{48,64},{64,80},{80,96},{96,112},{1,17},{17... | collective-permute-start | bytes 1769480 | tf_op jit(solution)/shard_map/ppermute | solution.py:829
  63.3 14.6 %collective-permute-start.3 = (f32[2,3,96,256]{3,2,1,0:T(8,128)S(1)}, f32[2,3,96,256]{3,2,1,0:T(8,128)S(1)}, u32[]{:S(2)}, u32[]{:S(2)}) collective-permute-start(f32[2,3,96,256]{3,2,1,0:T(8,128)S(1)} %get-tuple-element.57), channel_id=1, source_target_pairs={{16,0},{32,16},{48,32},{64,48},{80,64},{96,80},{112,96},{17,1},{33... | collective-permute-start | bytes 1769480 | tf_op jit(solution)/shard_map/ppermute | solution.py:834
  94.6 18.8 %copy-start.2 = (s32[16,128]{1,0:T(8,128)S(1)}, s32[16,128]{1,0:T(8,128)}, u32[]{:S(2)}) copy-start(s32[16,128]{1,0:T(8,128)} %get-tuple-element.68.tgt) | copy-start | bytes 24580
  94.6 18.8 %copy-start.3 = (s32[16,128]{1,0:T(8,128)S(1)}, s32[16,128]{1,0:T(8,128)}, u32[]{:S(2)}) copy-start(s32[16,128]{1,0:T(8,128)} %get-tuple-element.69.rank) | copy-start | bytes 24580
  94.6 18.7 %all-to-all-start.1 = ((f32[128,1,128]{2,1,0:T(1,128)}), f32[128,1,128]{2,1,0:T(1,128)S(1)}, u32[]{:S(2)}, u32[]{:S(2)}) async-start(f32[128,1,128]{2,1,0:T(1,128)} %bitcast.11), calls=%async_computation.1 | async-start | bytes 131072 | tf_op jit(solution)/shard_map/all_to_all | solution.py:867

commit v6 on v5

--- a/solution.py
+++ b/solution.py
@@ -218,10 +218,13 @@
         fetch(2 * duo).wait()
         fetch(2 * duo + 1).wait()
         here, there, slot = 2 * duo, 2 * duo + 1, duo % 2
-        y, which = duo_place(iota((DUO, COLS), 0))
+        lane = iota((COLS, COLS), 0)
+        y, which = jnp.where(lane % HALF < QUARTER, lane % HALF, lane % HALF + HALF), lane // HALF
         member, c = strip_place(iota((1, COLS), 1))
         want = jnp.where(y < 6, 3 + y, jnp.where(y >= 250, y - 241, -2))
         select = one_hot((member == 2 * duo + which) & (c == want))
+        outside = iota((LEV * ROWS, HALF), 1) < QUARTER
+        ends = [jnp.where(outside, taken[k, :, :HALF], taken[k, :, HALF:]) for k in (here, there)]
         block = jnp.concatenate([taken[here], taken[there]], axis=1)
         rows[: LEV * ROWS, :] = dot(block, perm_y[...]).astype(BF16)
         for b in range(6):
@@ -236,30 +239,30 @@
                     down_out[slot, x - (ROWS - EDGE), at, :] = part
         for copy in send(duo):
             copy.start()
+        strip_acc[: LEV * ROWS, :] += dot(jnp.concatenate(ends, axis=1), select)
+
+    member, c = strip_place(iota((COLS, COLS), 0))
+    for b in range(6):
+        turned = dot(perm_r[...], strip_acc[b * 256 : (b + 1) * 256, :].astype(BF16)).astype(BF16)
         for x in range(ROWS):
-            strip_acc[x] += dot(turned_out[slot, x], select)
-
-    for duo in (DUOS - 2, DUOS - 1):
-        for copy in send(duo):
-            copy.wait()
-    member, c = strip_place(iota((COLS, COLS), 0))
+            strip[x, b * 16 : (b + 1) * 16, :] = turned[x * 16 : (x + 1) * 16, :]
     left, right = (c >= 3) & (c < 6), (c >= 12) & (c < 15)
     spot = jnp.where(left, 3 * member + c - 3, jnp.where(right, HALF + 3 * member + c - 12, -1000))
-    places = [one_hot(iota((COLS, COLS), 1) == spot + 30 * j) for j in range(4)]
     places = [one_hot(iota((COLS, COLS), 1) == spot + 30 * j) for j in range(4)]
     for group in range(4):
         sides = jnp.zeros((PAD, COLS), F32)
         for j in range(4):
-            low = strip_acc[group * 4 + j].astype(BF16)
-            strip[group * 4 + j] = low
-            sides = sides + dot(low, places[j])
+            sides = sides + dot(strip[group * 4 + j], places[j])
         sides_out[0, group] = sides[:, :HALF]
         sides_out[1, group] = sides[:, HALF:]
     copies = [
-        pltpu.make_async_copy(sides_out.at[i], side.at[pl.ds(0, 4)], sem_out.at[0, i]) for i, side in enumerate((side_l, side_r))
+        pltpu.make_async_copy(sides_out.at[i], side.at[pl.ds(0, 4)], sem_out.at[3, i]) for i, side in enumerate((side_l, side_r))
     ]
     for copy in copies:
         copy.start()
+    for duo in (DUOS - 2, DUOS - 1):
+        for copy in send(duo):
+            copy.wait()
     for copy in copies:
         copy.wait()
 
@@ -285,12 +288,12 @@
             pltpu.VMEM((2, ROWS, PAD, DUO), BF16),
             pltpu.VMEM((2, EDGE, PAD, DUO), F32),
             pltpu.VMEM((2, EDGE, PAD, DUO), F32),
-            pltpu.VMEM((ROWS, PAD, COLS), F32),
+            pltpu.VMEM((ROWS * PAD, COLS), F32),
             pltpu.VMEM((DUO, DUO), BF16),
             pltpu.VMEM((256, 256), BF16),
             pltpu.VMEM((2, 4, PAD, HALF), F32),
             pltpu.SemaphoreType.DMA((MEM,)),
-            pltpu.SemaphoreType.DMA((3, 2)),
+            pltpu.SemaphoreType.DMA((4, 2)),
         ],
         compiler_params=params(MOST),
         cost_estimate=cost(10**10, 25 * 10**6),
@@ -369,16 +372,16 @@
     place = jnp.where(y < 3, y, jnp.where(y >= 253, HALF + y - 253, -1000))
     packed = jnp.zeros((PAD, COLS), F32)
     for x in range(ROWS):
-        value = out[x]
-        wide[x] = widen(value)
         select = one_hot(lane == place + 3 * x)
-        for piece in split(value, 2):
+        for piece in split(out[x], 2):
             packed = packed + dot(piece, select)
     sides_out[0] = packed[:, :HALF]
     sides_out[1] = packed[:, HALF:]
     copies = [pltpu.make_async_copy(sides_out.at[i], side.at[4], sem.at[i]) for i, side in enumerate((side_l, side_r))]
     for copy in copies:
         copy.start()
+    for x in range(ROWS):
+        wide[x] = widen(out[x])
     for copy in copies:
         copy.wait()
 

time: 115 us -> 112 us (0.974)
  Pallas kernels: 65.1 us -> 61.9 us
    pallas_call x1, Pallas kernels: 14.9 us -> 11.7 us  [arrange(): pl.pallas_call(arrange_kernel, name='arrange', out_shape=(jax.ShapeDtypeS...]
  transfers between devices with their start and end apart: 8 -> 8, of which waited for: 3 -> 3; matrix products, arithmetic and copies ran while one was open for 0% -> 0% of each run, Pallas kernels for 38% -> 37%
where the time goes in v6:
time: 112 us; the launch traced here: 111 us
  Pallas kernels  61.9 us (55%)
  starting transfers between devices  37.6 us (34%)
  waiting for transfers between devices  10.2 us (9%)
  between operations  1.46 us (1%)
    pallas_call x2, Pallas kernels, inner(): pl.pallas_call(lambda *refs: inner_kernel(start, count, *refs), name='inn...  17 us
    pallas_call x1, Pallas kernels, arrange(): pl.pallas_call(arrange_kernel, name='arrange', out_shape=(jax.ShapeDtypeS...  11.7 us
    ppermute x3, starting transfers between devices, forward(): return lax.ppermute(value, axis, [(i, i + 1) for i in range(size - 1)])  11.6 us
    all_to_all x1, starting transfers between devices, body(): lax.all_to_all(outgoing, ('gx', 'gy'), split_axis=0, concat_axis=0, tiled...  11.5 us
    all_to_all x1, starting transfers between devices, body(): lax.all_to_all(picked, ('gx', 'gy'), split_axis=0, concat_axis=0, tiled=T...  9.15 us
    pallas_call x1, Pallas kernels, scatter(): pl.pallas_call(scatter_kernel, name='scatter', out_shape=(jax.ShapeDtypeS...  7.35 us
    all_to_all x1, waiting for transfers between devices, body(): lax.all_to_all(picked, ('gx', 'gy'), split_axis=0, concat_axis=0, tiled=T...  7.11 us
    pallas_call x1, Pallas kernels, outer(): pl.pallas_call(outer_kernel, name='outer', out_shape=jax.ShapeDtypeStruct...  7.02 us
  transfers between devices with their start and end apart: 8, of which 3 were waited for; matrix products, arithmetic and copies ran while one was open for 0% of the time, Pallas kernels for 37%

profile of v6, /device:TPU:1, one launch (start us, length us, event | category | flops | bytes accessed | tf_op | source)
XLA Modules:
  0.0 111.3 jit_solution(5568807465852787195)
XLA Ops:
  1.3 3.5 %pack.1 = (f32[128,128]{1,0:T(8,128)}, s32[16,128]{1,0:T(8,128)}, s32[16,128]{1,0:T(8,128)}, bf16[192,192]{1,0:T(8,128)(2,1)}) custom-call(s32[1]{0:T(128)S(6)} %copy.14.count, f32[16,128]{1,0:T(8,128)} %bitcast.20, s32[16,128]{1,0:T(8,128)} %bitcast.21, s32[16,128]{1,0:T(8,128)} %bitcast.22, f32[90,90]{1,0:T(8,128)} %vertical_far.1), custom_call_target="tpu_custom_call" | custom-call | flops 1000000000 | bytes 1000000 | tf_op jit(solution)/shard_map/pack/pallas_call | solution.py:115
  4.8 11.5 %all-to-all-start = ((f32[128,1,128]{2,1,0:T(1,128)}), f32[128,1,128]{2,1,0:T(1,128)S(1)}, u32[]{:S(2)}, u32[]{:S(2)}) async-start(f32[128,1,128]{2,1,0:T(1,128)} %bitcast.18), calls=%async_computation | async-start | bytes 131072 | tf_op jit(solution)/shard_map/all_to_all | solution.py:851
  16.3 11.7 %arrange.1 = (bf16[5,16,96,512]{3,2,1,0:T(8,128)(2,1)}, f32[5,3,96,512]{3,2,1,0:T(8,128)}, f32[5,3,96,512]{3,2,1,0:T(8,128)}, bf16[16,96,256]{2,1,0:T(8,128)(2,1...) custom-call(bf16[10,1440,256]{2,1,0:T(8,128)(2,1)} %bitcast.19), custom_call_target="tpu_custom_call" | custom-call | flops 10000000000 | bytes 25000000 | tf_op jit(solution)/shard_map/arrange/pallas_call | solution.py:272
  28.1 3.7 %collective-permute-start.4 = (f32[5,3,96,512]{3,2,1,0:T(8,128)}, f32[5,3,96,512]{3,2,1,0:T(8,128)S(1)}, u32[]{:S(2)}, u32[]{:S(2)}) collective-permute-start(f32[5,3,96,512]{3,2,1,0:T(8,128)} %get-tuple-element.60), channel_id=1, source_target_pairs={{0,16},{16,32},{32,48},{48,64},{64,80},{80,96},{96,112},{1,17},{17... | collective-permute-start | bytes 8847368 | tf_op jit(solution)/shard_map/ppermute | solution.py:832
  31.7 1.9 %collective-permute-start.5 = (f32[5,3,96,512]{3,2,1,0:T(8,128)}, f32[5,3,96,512]{3,2,1,0:T(8,128)}, u32[]{:S(2)}, u32[]{:S(2)}) collective-permute-start(f32[5,3,96,512]{3,2,1,0:T(8,128)} %get-tuple-element.61), channel_id=1, source_target_pairs={{16,0},{32,16},{48,32},{64,48},{80,64},{96,80},{112,96},{17,1},{33... | collective-permute-start | bytes 8847368 | tf_op jit(solution)/shard_map/ppermute | solution.py:837
  33.7 0.1 pad_add_fusion.refs_3_.place
  33.8 7.3 %scatter.1 = (f32[16,96,256]{2,1,0:T(8,128)S(1)}, f32[16,96,512]{2,1,0:T(8,128)S(1)}, f32[5,96,128]{2,1,0:T(8,128)}, f32[5,96,128]{2,1,0:T(8,128)}, f32[48,256]{...) custom-call(f32[128,128]{1,0:T(8,128)S(1)} %bitcast.16, ...), custom_call_target="tpu_custom_call", output_to_operand_aliasing={{2}: (1, {}), {3}: (2, {})} | custom-call | flops 10000000000 | bytes 2000000 | tf_op jit(solution)/shard_map/scatter/pallas_call | solution.py:391
  41.1 3.2 %collective-permute-start = (f32[5,96,128]{2,1,0:T(8,128)}, f32[5,96,128]{2,1,0:T(8,128)S(1)}, u32[]{:S(2)}, u32[]{:S(2)}) collective-permute-start(f32[5,96,128]{2,1,0:T(8,128)} %get-tuple-element.46), channel_id=1, source_target_pairs={{0,1},{1,2},{2,3},{3,4},{4,5},{5,6},{6,7},{7,8},{8,9},{9,10},{10,1... | collective-permute-start | bytes 737288 | tf_op jit(solution)/shard_map/ppermute | solution.py:832
  44.3 1.5 %collective-permute-start.1 = (f32[5,96,128]{2,1,0:T(8,128)}, f32[5,96,128]{2,1,0:T(8,128)S(1)}, u32[]{:S(2)}, u32[]{:S(2)}) collective-permute-start(f32[5,96,128]{2,1,0:T(8,128)} %get-tuple-element.47), channel_id=1, source_target_pairs={{1,0},{2,1},{3,2},{4,3},{5,4},{6,5},{7,6},{8,7},{9,8},{10,9},{11,1... | collective-permute-start | bytes 737288 | tf_op jit(solution)/shard_map/ppermute | solution.py:837
  45.8 0.0 copy-start
  45.8 6.9 %inner.2 = (f32[2,6,96,512]{3,2,1,0:T(8,128)S(1)}, f32[10,96,512]{2,1,0:T(8,128)S(1)}) custom-call(bf16[5,16,96,512]{3,2,1,0:T(8,128)(2,1)S(1)} %copy-done.1, f32[16,96,512]{2,1,0:T(8,128)S(1)} %get-tuple-element.49.refs_1_, bf16[192,192]{1,0:T(8,128)(2,1)S(1)} %copy-done.4, s32[4]{0:T(128)S(1)} %pad_add_fusion.refs_3_.place), custom_call_target="tpu_custom_call" | custom-call | flops 4000000000 | bytes 4000000 | tf_op jit(solution)/shard_map/inner/pallas_call | solution.py:580
  52.7 0.5 collective-permute-done.1.right
  53.3 2.1 %strips.1 = (bf16[16,96,256]{2,1,0:T(8,128)(2,1)S(1)}, f32[16,96,256]{2,1,0:T(8,128)S(1)}, f32[2,3,96,256]{3,2,1,0:T(8,128)S(1)}, f32[2,3,96,256]{3,2,1,0:T(8,128)S(1)}) custom-call(bf16[16,96,256]{2,1,0:T(8,128)(2,1)S(1)} %copy-done, f32[16,96,256]{2,1,0:T(8,128)S(1)} %get-tuple-element.45.adjoint, f32[5,96,128]{2,1,0:T(8,128)S(1)} %collective-permute-done.left, ...), custom_call_target="tpu_custom_call" | custom-call | flops 1000000000 | bytes 4000000 | tf_op jit(solution)/shard_map/strips/pallas_call | solution.py:456
  55.4 4.8 %collective-permute-start.2 = (f32[2,3,96,256]{3,2,1,0:T(8,128)S(1)}, f32[2,3,96,256]{3,2,1,0:T(8,128)S(1)}, u32[]{:S(2)}, u32[]{:S(2)}) collective-permute-start(f32[2,3,96,256]{3,2,1,0:T(8,128)S(1)} %get-tuple-element.56), channel_id=1, source_target_pairs={{0,16},{16,32},{32,48},{48,64},{64,80},{80,96},{96,112},{1,17},{17... | collective-permute-start | bytes 1769480 | tf_op jit(solution)/shard_map/ppermute | solution.py:832
  60.2 1.9 %collective-permute-start.3 = (f32[2,3,96,256]{3,2,1,0:T(8,128)S(1)}, f32[2,3,96,256]{3,2,1,0:T(8,128)S(1)}, u32[]{:S(2)}, u32[]{:S(2)}) collective-permute-start(f32[2,3,96,256]{3,2,1,0:T(8,128)S(1)} %get-tuple-element.57), channel_id=1, source_target_pairs={{16,0},{32,16},{48,32},{64,48},{80,64},{96,80},{112,96},{17,1},{33... | collective-permute-start | bytes 1769480 | tf_op jit(solution)/shard_map/ppermute | solution.py:837
  62.1 10.0 %inner.3 = (f32[3,6,96,512]{3,2,1,0:T(8,128)S(1)}, f32[10,96,512]{2,1,0:T(8,128)S(1)}) custom-call(bf16[5,16,96,512]{3,2,1,0:T(8,128)(2,1)S(1)} %copy-done.1, f32[16,96,512]{2,1,0:T(8,128)S(1)} %get-tuple-element.49.refs_1_, bf16[192,192]{1,0:T(8,128)(2,1)S(1)} %copy-done.4, s32[4]{0:T(128)S(1)} %pad_add_fusion.refs_3_.place, ...), custom_call_target="tpu_custom_call" | custom-call | flops 6000000000 | bytes 6000000 | tf_op jit(solution)/shard_map/inner/pallas_call | solution.py:580
  72.2 2.6 %collective-permute-done.3.adj_b.halo_b = f32[2,3,96,256]{3,2,1,0:T(8,128)S(1)} collective-permute-done((f32[2,3,96,256]{3,2,1,0:T(8,128)S(1)}, f32[2,3,96,256]{3,2,1,0:T(8,128)S(1)}, u32[]{:S(2)}, u32[]{:S(2)}) %collective-permute-start.3) | collective-permute-done | bytes 589856 | tf_op jit(solution)/shard_map/ppermute | solution.py:837
  74.8 7.0 %outer.1.border = f32[6,96,512]{2,1,0:T(8,128)S(1)} custom-call(bf16[5,16,96,512]{3,2,1,0:T(8,128)(2,1)S(1)} %copy-done.1, f32[5,3,96,512]{3,2,1,0:T(8,128)S(1)} %collective-permute-done.4.halo_t, f32[5,3,96,512]{3,2,1,0:T(8,128)} %collective-permute-done.5.halo_b, f32[2,3,96,256]{3,2,1,0:T(8,128)S(1)} %collective-permute-done.2.adj_t.halo_t, ...), custom_call_target="tpu_custom_call" | custom-call | flops 10000000000 | bytes 30000000 | tf_op jit(solution)/shard_map/outer/pallas_call | solution.py:664
  81.8 5.3 %edge.1.field = f32[16,96,256]{2,1,0:T(8,128)S(1)} custom-call(bf16[16,96,256]{2,1,0:T(8,128)(2,1)S(1)} %get-tuple-element.54.strip, f32[16,96,256]{2,1,0:T(8,128)S(1)} %get-tuple-element.55.adj, f32[2,3,96,256]{3,2,1,0:T(8,128)S(1)} %collective-permute-done.2.adj_t.halo_t, f32[2,3,96,256]{3,2,1,0:T(8,128)S(1)} %collective-permute-done.3.adj_b.halo_b, ...), custom_call_target="tpu_custom_call" | custom-call | flops 4000000000 | bytes 8000000 | tf_op jit(solution)/shard_map/edge/pallas_call | solution.py:741
  87.1 4.3 %gather.1 = f32[128,128]{1,0:T(8,128)} custom-call(f32[16,96,256]{2,1,0:T(8,128)S(1)} %edge.1.field, f32[48,256]{1,0:T(8,128)S(1)} %get-tuple-element.64.level, f32[48,256]{1,0:T(8,128)S(1)} %get-tuple-element.65.column, s32[24,256]{1,0:T(8,128)S(1)} %get-tuple-element.66.pos, s32[1,128]{1,0:T(1,128)S(1)} %get-tuple-element.67.rows_of), custom_call_target="tpu_custom_call" | custom-call | flops 10000000000 | bytes 2000000 | tf_op jit(solution)/shard_map/gather/pallas_call | solution.py:783
  91.4 9.1 %all-to-all-start.1 = ((f32[128,1,128]{2,1,0:T(1,128)}), f32[128,1,128]{2,1,0:T(1,128)S(1)}, u32[]{:S(2)}, u32[]{:S(2)}) async-start(f32[128,1,128]{2,1,0:T(1,128)} %bitcast.11), calls=%async_computation.1 | async-start | bytes 131072 | tf_op jit(solution)/shard_map/all_to_all | solution.py:870
  100.5 2.5 %restore.1 = f32[1440,256]{1,0:T(8,128)} custom-call(f32[16,96,256]{2,1,0:T(8,128)S(1)} %edge.1.field), custom_call_target="tpu_custom_call" | custom-call | flops 1000000000 | bytes 3000000 | tf_op jit(solution)/shard_map/restore/pallas_call | solution.py:818
  103.0 7.1 %all-to-all-done.1 = f32[128,1,128]{2,1,0:T(1,128)S(1)} async-done(((f32[128,1,128]{2,1,0:T(1,128)}), f32[128,1,128]{2,1,0:T(1,128)S(1)}, u32[]{:S(2)}, u32[]{:S(2)}) %all-to-all-start.1) | async-done | bytes 65568 | tf_op jit(solution)/shard_map/all_to_all | solution.py:870
  110.1 1.2 %unpack.1 = f32[16,128]{1,0:T(8,128)} custom-call(f32[128,128]{1,0:T(8,128)S(1)} %bitcast.17, s32[16,128]{1,0:T(8,128)S(1)} %copy-done.2, s32[16,128]{1,0:T(8,128)S(1)} %copy-done.3), custom_call_target="tpu_custom_call" | custom-call | flops 100000000 | bytes 100000 | tf_op jit(solution)/shard_map/unpack/pallas_call | solution.py:146
  (14 shorter events, 0.0 us)
Async XLA Ops:
  4.8 23.3 %all-to-all-start = ((f32[128,1,128]{2,1,0:T(1,128)}), f32[128,1,128]{2,1,0:T(1,128)S(1)}, u32[]{:S(2)}, u32[]{:S(2)}) async-start(f32[128,1,128]{2,1,0:T(1,128)} %bitcast.18), calls=%async_computation | async-start | bytes 131072 | tf_op jit(solution)/shard_map/all_to_all | solution.py:851
  28.1 46.7 %collective-permute-start.4 = (f32[5,3,96,512]{3,2,1,0:T(8,128)}, f32[5,3,96,512]{3,2,1,0:T(8,128)S(1)}, u32[]{:S(2)}, u32[]{:S(2)}) collective-permute-start(f32[5,3,96,512]{3,2,1,0:T(8,128)} %get-tuple-element.60), channel_id=1, source_target_pairs={{0,16},{16,32},{32,48},{48,64},{64,80},{80,96},{96,112},{1,17},{17... | collective-permute-start | bytes 8847368 | tf_op jit(solution)/shard_map/ppermute | solution.py:832
  31.7 43.0 %collective-permute-start.5 = (f32[5,3,96,512]{3,2,1,0:T(8,128)}, f32[5,3,96,512]{3,2,1,0:T(8,128)}, u32[]{:S(2)}, u32[]{:S(2)}) collective-permute-start(f32[5,3,96,512]{3,2,1,0:T(8,128)} %get-tuple-element.61), channel_id=1, source_target_pairs={{16,0},{32,16},{48,32},{64,48},{80,64},{96,80},{112,96},{17,1},{33... | collective-permute-start | bytes 8847368 | tf_op jit(solution)/shard_map/ppermute | solution.py:837
  33.7 12.0 %copy-start.1 = (bf16[5,16,96,512]{3,2,1,0:T(8,128)(2,1)S(1)}, bf16[5,16,96,512]{3,2,1,0:T(8,128)(2,1)}, u32[]{:S(2)}) copy-start(bf16[5,16,96,512]{3,2,1,0:T(8,128)(2,1)} %get-tuple-element.48.refs_0_.ens) | copy-start | bytes 23592964
  33.8 12.0 %copy-start.4 = (bf16[192,192]{1,0:T(8,128)(2,1)S(1)}, bf16[192,192]{1,0:T(8,128)(2,1)}, u32[]{:S(2)}) copy-start(bf16[192,192]{1,0:T(8,128)(2,1)} %get-tuple-element.50.refs_2_.weights) | copy-start | bytes 221188
  41.1 11.6 %collective-permute-start = (f32[5,96,128]{2,1,0:T(8,128)}, f32[5,96,128]{2,1,0:T(8,128)S(1)}, u32[]{:S(2)}, u32[]{:S(2)}) collective-permute-start(f32[5,96,128]{2,1,0:T(8,128)} %get-tuple-element.46), channel_id=1, source_target_pairs={{0,1},{1,2},{2,3},{3,4},{4,5},{5,6},{6,7},{7,8},{8,9},{9,10},{10,1... | collective-permute-start | bytes 737288 | tf_op jit(solution)/shard_map/ppermute | solution.py:832
  44.3 9.0 %collective-permute-start.1 = (f32[5,96,128]{2,1,0:T(8,128)}, f32[5,96,128]{2,1,0:T(8,128)S(1)}, u32[]{:S(2)}, u32[]{:S(2)}) collective-permute-start(f32[5,96,128]{2,1,0:T(8,128)} %get-tuple-element.47), channel_id=1, source_target_pairs={{1,0},{2,1},{3,2},{4,3},{5,4},{6,5},{7,6},{8,7},{9,8},{10,9},{11,1... | collective-permute-start | bytes 737288 | tf_op jit(solution)/shard_map/ppermute | solution.py:837
  45.8 7.5 %copy-start = (bf16[16,96,256]{2,1,0:T(8,128)(2,1)S(1)}, bf16[16,96,256]{2,1,0:T(8,128)(2,1)}, u32[]{:S(2)}) copy-start(bf16[16,96,256]{2,1,0:T(8,128)(2,1)} %get-tuple-element.38.strip) | copy-start | bytes 2359300
  55.4 16.8 %collective-permute-start.2 = (f32[2,3,96,256]{3,2,1,0:T(8,128)S(1)}, f32[2,3,96,256]{3,2,1,0:T(8,128)S(1)}, u32[]{:S(2)}, u32[]{:S(2)}) collective-permute-start(f32[2,3,96,256]{3,2,1,0:T(8,128)S(1)} %get-tuple-element.56), channel_id=1, source_target_pairs={{0,16},{16,32},{32,48},{48,64},{64,80},{80,96},{96,112},{1,17},{17... | collective-permute-start | bytes 1769480 | tf_op jit(solution)/shard_map/ppermute | solution.py:832
  60.2 14.6 %collective-permute-start.3 = (f32[2,3,96,256]{3,2,1,0:T(8,128)S(1)}, f32[2,3,96,256]{3,2,1,0:T(8,128)S(1)}, u32[]{:S(2)}, u32[]{:S(2)}) collective-permute-start(f32[2,3,96,256]{3,2,1,0:T(8,128)S(1)} %get-tuple-element.57), channel_id=1, source_target_pairs={{16,0},{32,16},{48,32},{64,48},{80,64},{96,80},{112,96},{17,1},{33... | collective-permute-start | bytes 1769480 | tf_op jit(solution)/shard_map/ppermute | solution.py:837
  91.4 18.7 %copy-start.2 = (s32[16,128]{1,0:T(8,128)S(1)}, s32[16,128]{1,0:T(8,128)}, u32[]{:S(2)}) copy-start(s32[16,128]{1,0:T(8,128)} %get-tuple-element.68.tgt) | copy-start | bytes 24580
  91.4 18.7 %copy-start.3 = (s32[16,128]{1,0:T(8,128)S(1)}, s32[16,128]{1,0:T(8,128)}, u32[]{:S(2)}) copy-start(s32[16,128]{1,0:T(8,128)} %get-tuple-element.69.rank) | copy-start | bytes 24580
  91.4 18.7 %all-to-all-start.1 = ((f32[128,1,128]{2,1,0:T(1,128)}), f32[128,1,128]{2,1,0:T(1,128)S(1)}, u32[]{:S(2)}, u32[]{:S(2)}) async-start(f32[128,1,128]{2,1,0:T(1,128)} %bitcast.11), calls=%async_computation.1 | async-start | bytes 131072 | tf_op jit(solution)/shard_map/all_to_all | solution.py:870

commit v7 on v6

--- a/solution.py
+++ b/solution.py
@@ -318,19 +318,22 @@
 
     for c in range(CHUNKS):
         hot[c * ROWS : (c + 1) * ROWS, :] = one_hot(iota((ROWS, COLS), 0) == x[c : c + 1, :])
-    size = CHUNKS * ROWS
     lane = iota((COLS, COLS + HALF), 1)
     both = dot(hot[...], one_hot((lane > iota((COLS, COLS + HALF), 0)) | (lane >= COLS)))
-    count = both[:, COLS:].astype(BF16)
-    here, there = iota((size, size), 0), iota((size, size), 1)
-    same = (here & 15) == (there & 15)
-    earlier = dot(one_hot(same & (there < here)), count)
-    needed = (dot(one_hot(same), count).astype(I32) + 255) >> 8
-    start = dot(one_hot(((there & 15) < (here & 15)) & (there < ROWS)), needed.astype(F32).astype(BF16))
-    base = start * 256.0 + earlier
-    place = both[:, :COLS] + jnp.concatenate([base, base], axis=1)
-    place = jnp.where(hot[...].astype(F32) > 0.5, place, 0.0)
-    pos = jnp.sum(place.reshape(CHUNKS, ROWS, COLS), axis=1).astype(I32)
+    before = jnp.zeros((ROWS, HALF), F32)
+    earlier = []
+    for c in range(CHUNKS):
+        earlier.append(before)
+        before = before + both[c * ROWS : (c + 1) * ROWS, COLS:]
+    needed = ((before.astype(I32) + 255) >> 8).astype(F32).astype(BF16)
+    start = dot(one_hot(iota((ROWS, ROWS), 1) < iota((ROWS, ROWS), 0)), needed)
+    lines = []
+    for c in range(CHUNKS):
+        base = start * 256.0 + earlier[c]
+        spots = both[c * ROWS : (c + 1) * ROWS, :COLS] + jnp.concatenate([base, base], axis=1)
+        spots = jnp.where(iota((ROWS, COLS), 0) == x[c : c + 1, :], spots, 0.0)
+        lines.append(jnp.sum(spots, axis=0, keepdims=True))
+    pos = jnp.concatenate(lines, axis=0).astype(I32)
     pos = jnp.where(full, pos, -1)
     pos_out[...] = pos
     begun = jnp.where(start[:ROWS].astype(I32) <= iota((ROWS, HALF), 1), 1.0, 0.0)

time: 112 us -> 112 us (level)
  transfers between devices with their start and end apart: 8 -> 8, of which waited for: 3 -> 3; matrix products, arithmetic and copies ran while one was open for 0% -> 0% of each run, Pallas kernels for 37% -> 36%
where the time goes in v7:
time: 112 us; the launch traced here: 111 us
  Pallas kernels  61.4 us (55%)
  starting transfers between devices  37.6 us (34%)
  waiting for transfers between devices  10.7 us (10%)
  between operations  1.46 us (1%)
    pallas_call x2, Pallas kernels, inner(): pl.pallas_call(lambda *refs: inner_kernel(start, count, *refs), name='inn...  17 us
    pallas_call x1, Pallas kernels, arrange(): pl.pallas_call(arrange_kernel, name='arrange', out_shape=(jax.ShapeDtypeS...  11.7 us
    ppermute x3, starting transfers between devices, forward(): return lax.ppermute(value, axis, [(i, i + 1) for i in range(size - 1)])  11.6 us
    all_to_all x1, starting transfers between devices, body(): lax.all_to_all(outgoing, ('gx', 'gy'), split_axis=0, concat_axis=0, tiled...  11.5 us
    all_to_all x1, starting transfers between devices, body(): lax.all_to_all(picked, ('gx', 'gy'), split_axis=0, concat_axis=0, tiled=T...  9.15 us
    all_to_all x1, waiting for transfers between devices, body(): lax.all_to_all(picked, ('gx', 'gy'), split_axis=0, concat_axis=0, tiled=T...  7.11 us
    pallas_call x1, Pallas kernels, outer(): pl.pallas_call(outer_kernel, name='outer', out_shape=jax.ShapeDtypeStruct...  7.02 us
    pallas_call x1, Pallas kernels, scatter(): pl.pallas_call(scatter_kernel, name='scatter', out_shape=(jax.ShapeDtypeS...  6.88 us
  transfers between devices with their start and end apart: 8, of which 3 were waited for; matrix products, arithmetic and copies ran while one was open for 0% of the time, Pallas kernels for 36%

profile of v7, /device:TPU:1, one launch (start us, length us, event | category | flops | bytes accessed | tf_op | source)
XLA Modules:
  0.0 111.3 jit_solution(165866964350888659)
XLA Ops:
  1.3 3.5 %pack.1 = (f32[128,128]{1,0:T(8,128)}, s32[16,128]{1,0:T(8,128)}, s32[16,128]{1,0:T(8,128)}, bf16[192,192]{1,0:T(8,128)(2,1)}) custom-call(s32[1]{0:T(128)S(6)} %copy.14.count, f32[16,128]{1,0:T(8,128)} %bitcast.20, s32[16,128]{1,0:T(8,128)} %bitcast.21, s32[16,128]{1,0:T(8,128)} %bitcast.22, f32[90,90]{1,0:T(8,128)} %vertical_far.1), custom_call_target="tpu_custom_call" | custom-call | flops 1000000000 | bytes 1000000 | tf_op jit(solution)/shard_map/pack/pallas_call | solution.py:115
  4.8 11.5 %all-to-all-start = ((f32[128,1,128]{2,1,0:T(1,128)}), f32[128,1,128]{2,1,0:T(1,128)S(1)}, u32[]{:S(2)}, u32[]{:S(2)}) async-start(f32[128,1,128]{2,1,0:T(1,128)} %bitcast.18), calls=%async_computation | async-start | bytes 131072 | tf_op jit(solution)/shard_map/all_to_all | solution.py:854
  16.3 11.7 %arrange.1 = (bf16[5,16,96,512]{3,2,1,0:T(8,128)(2,1)}, f32[5,3,96,512]{3,2,1,0:T(8,128)}, f32[5,3,96,512]{3,2,1,0:T(8,128)}, bf16[16,96,256]{2,1,0:T(8,128)(2,1...) custom-call(bf16[10,1440,256]{2,1,0:T(8,128)(2,1)} %bitcast.19), custom_call_target="tpu_custom_call" | custom-call | flops 10000000000 | bytes 25000000 | tf_op jit(solution)/shard_map/arrange/pallas_call | solution.py:272
  28.1 3.7 %collective-permute-start.4 = (f32[5,3,96,512]{3,2,1,0:T(8,128)}, f32[5,3,96,512]{3,2,1,0:T(8,128)S(1)}, u32[]{:S(2)}, u32[]{:S(2)}) collective-permute-start(f32[5,3,96,512]{3,2,1,0:T(8,128)} %get-tuple-element.60), channel_id=1, source_target_pairs={{0,16},{16,32},{32,48},{48,64},{64,80},{80,96},{96,112},{1,17},{17... | collective-permute-start | bytes 8847368 | tf_op jit(solution)/shard_map/ppermute | solution.py:835
  31.7 1.9 %collective-permute-start.5 = (f32[5,3,96,512]{3,2,1,0:T(8,128)}, f32[5,3,96,512]{3,2,1,0:T(8,128)}, u32[]{:S(2)}, u32[]{:S(2)}) collective-permute-start(f32[5,3,96,512]{3,2,1,0:T(8,128)} %get-tuple-element.61), channel_id=1, source_target_pairs={{16,0},{32,16},{48,32},{64,48},{80,64},{96,80},{112,96},{17,1},{33... | collective-permute-start | bytes 8847368 | tf_op jit(solution)/shard_map/ppermute | solution.py:840
  33.7 0.1 pad_add_fusion.refs_3_.place
  33.8 6.9 %scatter.1 = (f32[16,96,256]{2,1,0:T(8,128)S(1)}, f32[16,96,512]{2,1,0:T(8,128)S(1)}, f32[5,96,128]{2,1,0:T(8,128)}, f32[5,96,128]{2,1,0:T(8,128)}, f32[48,256]{...) custom-call(f32[128,128]{1,0:T(8,128)S(1)} %bitcast.16, ...), custom_call_target="tpu_custom_call", output_to_operand_aliasing={{2}: (1, {}), {3}: (2, {})} | custom-call | flops 10000000000 | bytes 2000000 | tf_op jit(solution)/shard_map/scatter/pallas_call | solution.py:394
  40.6 3.2 %collective-permute-start = (f32[5,96,128]{2,1,0:T(8,128)}, f32[5,96,128]{2,1,0:T(8,128)S(1)}, u32[]{:S(2)}, u32[]{:S(2)}) collective-permute-start(f32[5,96,128]{2,1,0:T(8,128)} %get-tuple-element.46), channel_id=1, source_target_pairs={{0,1},{1,2},{2,3},{3,4},{4,5},{5,6},{6,7},{7,8},{8,9},{9,10},{10,1... | collective-permute-start | bytes 737288 | tf_op jit(solution)/shard_map/ppermute | solution.py:835
  43.8 1.3 %collective-permute-start.1 = (f32[5,96,128]{2,1,0:T(8,128)}, f32[5,96,128]{2,1,0:T(8,128)S(1)}, u32[]{:S(2)}, u32[]{:S(2)}) collective-permute-start(f32[5,96,128]{2,1,0:T(8,128)} %get-tuple-element.47), channel_id=1, source_target_pairs={{1,0},{2,1},{3,2},{4,3},{5,4},{6,5},{7,6},{8,7},{9,8},{10,9},{11,1... | collective-permute-start | bytes 737288 | tf_op jit(solution)/shard_map/ppermute | solution.py:840
  45.1 0.0 copy-start
  45.1 6.9 %inner.2 = (f32[2,6,96,512]{3,2,1,0:T(8,128)S(1)}, f32[10,96,512]{2,1,0:T(8,128)S(1)}) custom-call(bf16[5,16,96,512]{3,2,1,0:T(8,128)(2,1)S(1)} %copy-done.1, f32[16,96,512]{2,1,0:T(8,128)S(1)} %get-tuple-element.49.refs_1_, bf16[192,192]{1,0:T(8,128)(2,1)S(1)} %copy-done.4, s32[4]{0:T(128)S(1)} %pad_add_fusion.refs_3_.place), custom_call_target="tpu_custom_call" | custom-call | flops 4000000000 | bytes 4000000 | tf_op jit(solution)/shard_map/inner/pallas_call | solution.py:583
  52.1 0.7 collective-permute-done.1.right
  52.8 2.1 %strips.1 = (bf16[16,96,256]{2,1,0:T(8,128)(2,1)S(1)}, f32[16,96,256]{2,1,0:T(8,128)S(1)}, f32[2,3,96,256]{3,2,1,0:T(8,128)S(1)}, f32[2,3,96,256]{3,2,1,0:T(8,128)S(1)}) custom-call(bf16[16,96,256]{2,1,0:T(8,128)(2,1)S(1)} %copy-done, f32[16,96,256]{2,1,0:T(8,128)S(1)} %get-tuple-element.45.adjoint, f32[5,96,128]{2,1,0:T(8,128)S(1)} %collective-permute-done.left, ...), custom_call_target="tpu_custom_call" | custom-call | flops 1000000000 | bytes 4000000 | tf_op jit(solution)/shard_map/strips/pallas_call | solution.py:459
  54.9 4.8 %collective-permute-start.2 = (f32[2,3,96,256]{3,2,1,0:T(8,128)S(1)}, f32[2,3,96,256]{3,2,1,0:T(8,128)S(1)}, u32[]{:S(2)}, u32[]{:S(2)}) collective-permute-start(f32[2,3,96,256]{3,2,1,0:T(8,128)S(1)} %get-tuple-element.56), channel_id=1, source_target_pairs={{0,16},{16,32},{32,48},{48,64},{64,80},{80,96},{96,112},{1,17},{17... | collective-permute-start | bytes 1769480 | tf_op jit(solution)/shard_map/ppermute | solution.py:835
  59.7 2.1 %collective-permute-start.3 = (f32[2,3,96,256]{3,2,1,0:T(8,128)S(1)}, f32[2,3,96,256]{3,2,1,0:T(8,128)S(1)}, u32[]{:S(2)}, u32[]{:S(2)}) collective-permute-start(f32[2,3,96,256]{3,2,1,0:T(8,128)S(1)} %get-tuple-element.57), channel_id=1, source_target_pairs={{16,0},{32,16},{48,32},{64,48},{80,64},{96,80},{112,96},{17,1},{33... | collective-permute-start | bytes 1769480 | tf_op jit(solution)/shard_map/ppermute | solution.py:840
  61.8 10.1 %inner.3 = (f32[3,6,96,512]{3,2,1,0:T(8,128)S(1)}, f32[10,96,512]{2,1,0:T(8,128)S(1)}) custom-call(bf16[5,16,96,512]{3,2,1,0:T(8,128)(2,1)S(1)} %copy-done.1, f32[16,96,512]{2,1,0:T(8,128)S(1)} %get-tuple-element.49.refs_1_, bf16[192,192]{1,0:T(8,128)(2,1)S(1)} %copy-done.4, s32[4]{0:T(128)S(1)} %pad_add_fusion.refs_3_.place, ...), custom_call_target="tpu_custom_call" | custom-call | flops 6000000000 | bytes 6000000 | tf_op jit(solution)/shard_map/inner/pallas_call | solution.py:583
  71.9 2.9 %collective-permute-done.3.adj_b.halo_b = f32[2,3,96,256]{3,2,1,0:T(8,128)S(1)} collective-permute-done((f32[2,3,96,256]{3,2,1,0:T(8,128)S(1)}, f32[2,3,96,256]{3,2,1,0:T(8,128)S(1)}, u32[]{:S(2)}, u32[]{:S(2)}) %collective-permute-start.3) | collective-permute-done | bytes 589856 | tf_op jit(solution)/shard_map/ppermute | solution.py:840
  74.8 7.0 %outer.1.border = f32[6,96,512]{2,1,0:T(8,128)S(1)} custom-call(bf16[5,16,96,512]{3,2,1,0:T(8,128)(2,1)S(1)} %copy-done.1, f32[5,3,96,512]{3,2,1,0:T(8,128)S(1)} %collective-permute-done.4.halo_t, f32[5,3,96,512]{3,2,1,0:T(8,128)} %collective-permute-done.5.halo_b, f32[2,3,96,256]{3,2,1,0:T(8,128)S(1)} %collective-permute-done.2.adj_t.halo_t, ...), custom_call_target="tpu_custom_call" | custom-call | flops 10000000000 | bytes 30000000 | tf_op jit(solution)/shard_map/outer/pallas_call | solution.py:667
  81.8 5.3 %edge.1.field = f32[16,96,256]{2,1,0:T(8,128)S(1)} custom-call(bf16[16,96,256]{2,1,0:T(8,128)(2,1)S(1)} %get-tuple-element.54.strip, f32[16,96,256]{2,1,0:T(8,128)S(1)} %get-tuple-element.55.adj, f32[2,3,96,256]{3,2,1,0:T(8,128)S(1)} %collective-permute-done.2.adj_t.halo_t, f32[2,3,96,256]{3,2,1,0:T(8,128)S(1)} %collective-permute-done.3.adj_b.halo_b, ...), custom_call_target="tpu_custom_call" | custom-call | flops 4000000000 | bytes 8000000 | tf_op jit(solution)/shard_map/edge/pallas_call | solution.py:744
  87.1 4.3 %gather.1 = f32[128,128]{1,0:T(8,128)} custom-call(f32[16,96,256]{2,1,0:T(8,128)S(1)} %edge.1.field, f32[48,256]{1,0:T(8,128)S(1)} %get-tuple-element.64.level, f32[48,256]{1,0:T(8,128)S(1)} %get-tuple-element.65.column, s32[24,256]{1,0:T(8,128)S(1)} %get-tuple-element.66.pos, s32[1,128]{1,0:T(1,128)S(1)} %get-tuple-element.67.rows_of), custom_call_target="tpu_custom_call" | custom-call | flops 10000000000 | bytes 2000000 | tf_op jit(solution)/shard_map/gather/pallas_call | solution.py:786
  91.4 9.1 %all-to-all-start.1 = ((f32[128,1,128]{2,1,0:T(1,128)}), f32[128,1,128]{2,1,0:T(1,128)S(1)}, u32[]{:S(2)}, u32[]{:S(2)}) async-start(f32[128,1,128]{2,1,0:T(1,128)} %bitcast.11), calls=%async_computation.1 | async-start | bytes 131072 | tf_op jit(solution)/shard_map/all_to_all | solution.py:873
  100.5 2.5 %restore.1 = f32[1440,256]{1,0:T(8,128)} custom-call(f32[16,96,256]{2,1,0:T(8,128)S(1)} %edge.1.field), custom_call_target="tpu_custom_call" | custom-call | flops 1000000000 | bytes 3000000 | tf_op jit(solution)/shard_map/restore/pallas_call | solution.py:821
  103.0 7.1 %all-to-all-done.1 = f32[128,1,128]{2,1,0:T(1,128)S(1)} async-done(((f32[128,1,128]{2,1,0:T(1,128)}), f32[128,1,128]{2,1,0:T(1,128)S(1)}, u32[]{:S(2)}, u32[]{:S(2)}) %all-to-all-start.1) | async-done | bytes 65568 | tf_op jit(solution)/shard_map/all_to_all | solution.py:873
  110.1 1.2 %unpack.1 = f32[16,128]{1,0:T(8,128)} custom-call(f32[128,128]{1,0:T(8,128)S(1)} %bitcast.17, s32[16,128]{1,0:T(8,128)S(1)} %copy-done.2, s32[16,128]{1,0:T(8,128)S(1)} %copy-done.3), custom_call_target="tpu_custom_call" | custom-call | flops 100000000 | bytes 100000 | tf_op jit(solution)/shard_map/unpack/pallas_call | solution.py:146
  (14 shorter events, 0.0 us)
Async XLA Ops:
  4.8 23.3 %all-to-all-start = ((f32[128,1,128]{2,1,0:T(1,128)}), f32[128,1,128]{2,1,0:T(1,128)S(1)}, u32[]{:S(2)}, u32[]{:S(2)}) async-start(f32[128,1,128]{2,1,0:T(1,128)} %bitcast.18), calls=%async_computation | async-start | bytes 131072 | tf_op jit(solution)/shard_map/all_to_all | solution.py:854
  28.1 46.7 %collective-permute-start.4 = (f32[5,3,96,512]{3,2,1,0:T(8,128)}, f32[5,3,96,512]{3,2,1,0:T(8,128)S(1)}, u32[]{:S(2)}, u32[]{:S(2)}) collective-permute-start(f32[5,3,96,512]{3,2,1,0:T(8,128)} %get-tuple-element.60), channel_id=1, source_target_pairs={{0,16},{16,32},{32,48},{48,64},{64,80},{80,96},{96,112},{1,17},{17... | collective-permute-start | bytes 8847368 | tf_op jit(solution)/shard_map/ppermute | solution.py:835
  31.7 43.0 %collective-permute-start.5 = (f32[5,3,96,512]{3,2,1,0:T(8,128)}, f32[5,3,96,512]{3,2,1,0:T(8,128)}, u32[]{:S(2)}, u32[]{:S(2)}) collective-permute-start(f32[5,3,96,512]{3,2,1,0:T(8,128)} %get-tuple-element.61), channel_id=1, source_target_pairs={{16,0},{32,16},{48,32},{64,48},{80,64},{96,80},{112,96},{17,1},{33... | collective-permute-start | bytes 8847368 | tf_op jit(solution)/shard_map/ppermute | solution.py:840
  33.7 11.4 %copy-start.1 = (bf16[5,16,96,512]{3,2,1,0:T(8,128)(2,1)S(1)}, bf16[5,16,96,512]{3,2,1,0:T(8,128)(2,1)}, u32[]{:S(2)}) copy-start(bf16[5,16,96,512]{3,2,1,0:T(8,128)(2,1)} %get-tuple-element.48.refs_0_.ens) | copy-start | bytes 23592964
  33.8 11.4 %copy-start.4 = (bf16[192,192]{1,0:T(8,128)(2,1)S(1)}, bf16[192,192]{1,0:T(8,128)(2,1)}, u32[]{:S(2)}) copy-start(bf16[192,192]{1,0:T(8,128)(2,1)} %get-tuple-element.50.refs_2_.weights) | copy-start | bytes 221188
  40.6 11.4 %collective-permute-start = (f32[5,96,128]{2,1,0:T(8,128)}, f32[5,96,128]{2,1,0:T(8,128)S(1)}, u32[]{:S(2)}, u32[]{:S(2)}) collective-permute-start(f32[5,96,128]{2,1,0:T(8,128)} %get-tuple-element.46), channel_id=1, source_target_pairs={{0,1},{1,2},{2,3},{3,4},{4,5},{5,6},{6,7},{7,8},{8,9},{9,10},{10,1... | collective-permute-start | bytes 737288 | tf_op jit(solution)/shard_map/ppermute | solution.py:835
  43.8 9.0 %collective-permute-start.1 = (f32[5,96,128]{2,1,0:T(8,128)}, f32[5,96,128]{2,1,0:T(8,128)S(1)}, u32[]{:S(2)}, u32[]{:S(2)}) collective-permute-start(f32[5,96,128]{2,1,0:T(8,128)} %get-tuple-element.47), channel_id=1, source_target_pairs={{1,0},{2,1},{3,2},{4,3},{5,4},{6,5},{7,6},{8,7},{9,8},{10,9},{11,1... | collective-permute-start | bytes 737288 | tf_op jit(solution)/shard_map/ppermute | solution.py:840
  45.1 7.7 %copy-start = (bf16[16,96,256]{2,1,0:T(8,128)(2,1)S(1)}, bf16[16,96,256]{2,1,0:T(8,128)(2,1)}, u32[]{:S(2)}) copy-start(bf16[16,96,256]{2,1,0:T(8,128)(2,1)} %get-tuple-element.38.strip) | copy-start | bytes 2359300
  54.9 17.0 %collective-permute-start.2 = (f32[2,3,96,256]{3,2,1,0:T(8,128)S(1)}, f32[2,3,96,256]{3,2,1,0:T(8,128)S(1)}, u32[]{:S(2)}, u32[]{:S(2)}) collective-permute-start(f32[2,3,96,256]{3,2,1,0:T(8,128)S(1)} %get-tuple-element.56), channel_id=1, source_target_pairs={{0,16},{16,32},{32,48},{48,64},{64,80},{80,96},{96,112},{1,17},{17... | collective-permute-start | bytes 1769480 | tf_op jit(solution)/shard_map/ppermute | solution.py:835
  59.7 15.0 %collective-permute-start.3 = (f32[2,3,96,256]{3,2,1,0:T(8,128)S(1)}, f32[2,3,96,256]{3,2,1,0:T(8,128)S(1)}, u32[]{:S(2)}, u32[]{:S(2)}) collective-permute-start(f32[2,3,96,256]{3,2,1,0:T(8,128)S(1)} %get-tuple-element.57), channel_id=1, source_target_pairs={{16,0},{32,16},{48,32},{64,48},{80,64},{96,80},{112,96},{17,1},{33... | collective-permute-start | bytes 1769480 | tf_op jit(solution)/shard_map/ppermute | solution.py:840
  91.4 18.7 %copy-start.2 = (s32[16,128]{1,0:T(8,128)S(1)}, s32[16,128]{1,0:T(8,128)}, u32[]{:S(2)}) copy-start(s32[16,128]{1,0:T(8,128)} %get-tuple-element.68.tgt) | copy-start | bytes 24580
  91.4 18.7 %copy-start.3 = (s32[16,128]{1,0:T(8,128)S(1)}, s32[16,128]{1,0:T(8,128)}, u32[]{:S(2)}) copy-start(s32[16,128]{1,0:T(8,128)} %get-tuple-element.69.rank) | copy-start | bytes 24580
  91.4 18.7 %all-to-all-start.1 = ((f32[128,1,128]{2,1,0:T(1,128)}), f32[128,1,128]{2,1,0:T(1,128)S(1)}, u32[]{:S(2)}, u32[]{:S(2)}) async-start(f32[128,1,128]{2,1,0:T(1,128)} %bitcast.11), calls=%async_computation.1 | async-start | bytes 131072 | tf_op jit(solution)/shard_map/all_to_all | solution.py:873

commit v8 on v7

--- a/solution.py
+++ b/solution.py
@@ -63,7 +63,7 @@
 
 
 def pack_kernel(
-    count, dual_far, col_far, lev_far, vertical_far, out, tgt_out, rank_out, weights, left_v, left_c, right_v, right_c, dual, col, lev, vertical, sem
+    count, dual_far, col_far, lev_far, vertical_far, out, tgt_out, rank_out, weights, left, right, dual, col, lev, vertical, sem
 ):
     pairs = ((col_far, col), (lev_far, lev), (dual_far, dual), (vertical_far, vertical))
     copies = [pltpu.make_async_copy(a, b, sem.at[i]) for i, (a, b) in enumerate(pairs)]
@@ -97,17 +97,16 @@
         tgt_out[i : i + 1, :] = target
         rank = rank.astype(I32)
         rank_out[i : i + 1, :] = rank
-        right_v[:, at] = one_hot(rows == rank)
-        right_c[:, at] = one_hot(rows == rank + CAP)
+        right[:, at] = one_hot(rows == rank)
         values = dual[i : i + 1, :]
         for p, piece in enumerate(split(values, 3)):
-            left_v[p * DEV : (p + 1) * DEV, at] = jnp.where(hit, piece.astype(F32), 0.0).astype(BF16)
+            left[p * DEV : (p + 1) * DEV, at] = jnp.where(hit, piece.astype(F32), 0.0).astype(BF16)
         cells = (lev[i : i + 1, :] << 12, (row & 15) << 8, y + 1)
         for p, piece in enumerate(cells):
-            left_c[p * DEV : (p + 1) * DEV, at] = jnp.where(hit, piece.astype(F32), 0.0).astype(BF16)
-    a = dot_nt(left_v[...], right_v[...])
-    b = dot_nt(left_c[...], right_c[...])
-    out[...] = ((a[:DEV] + a[DEV : 2 * DEV]) + a[2 * DEV :]) + ((b[:DEV] + b[DEV : 2 * DEV]) + b[2 * DEV :])
+            left[(p + 3) * DEV : (p + 4) * DEV, at] = jnp.where(hit, piece.astype(F32), 0.0).astype(BF16)
+    both = dot_nt(left[...], right[...])
+    part = [both[p * DEV : (p + 1) * DEV] for p in range(6)]
+    out[...] = ((part[0] + part[1]) + part[2]) + pltpu.roll((part[3] + part[4]) + part[5], CAP, 1)
 
 
 def pack(count, dual, col, lev, vertical):
@@ -123,8 +122,7 @@
         ),
         in_specs=[pl.BlockSpec(memory_space=pltpu.SMEM)] + [pl.BlockSpec(memory_space=pltpu.HBM)] * 4,
         out_specs=(spec,) * 4,
-        scratch_shapes=[pltpu.VMEM((3 * DEV, SLOTS), BF16)] * 2
-        + [pltpu.VMEM((DEV, SLOTS), BF16)] * 2
+        scratch_shapes=[pltpu.VMEM((6 * DEV, SLOTS), BF16), pltpu.VMEM((DEV, SLOTS), BF16)]
         + [pltpu.VMEM((SLOTS // HALF, HALF), kind) for kind in (F32, I32, I32)]
         + [pltpu.VMEM((LEV, LEV), F32), pltpu.SemaphoreType.DMA((4,))],
         compiler_params=params(ALL),

time: 112 us -> 112 us (level)
  no operation moved by 1% of the time
where the time goes in v8:
time: 112 us; the launch traced here: 111 us
  Pallas kernels  61.5 us (55%)
  starting transfers between devices  37.5 us (33%)
  waiting for transfers between devices  10.8 us (10%)
  between operations  1.46 us (1%)
    pallas_call x2, Pallas kernels, inner(): pl.pallas_call(lambda *refs: inner_kernel(start, count, *refs), name='inn...  17 us
    pallas_call x1, Pallas kernels, arrange(): pl.pallas_call(arrange_kernel, name='arrange', out_shape=(jax.ShapeDtypeS...  11.7 us
    ppermute x3, starting transfers between devices, forward(): return lax.ppermute(value, axis, [(i, i + 1) for i in range(size - 1)])  11.6 us
    all_to_all x1, starting transfers between devices, body(): lax.all_to_all(outgoing, ('gx', 'gy'), split_axis=0, concat_axis=0, tiled...  11.5 us
    all_to_all x1, starting transfers between devices, body(): lax.all_to_all(picked, ('gx', 'gy'), split_axis=0, concat_axis=0, tiled=T...  9.17 us
    all_to_all x1, waiting for transfers between devices, body(): lax.all_to_all(picked, ('gx', 'gy'), split_axis=0, concat_axis=0, tiled=T...  7.11 us
    pallas_call x1, Pallas kernels, outer(): pl.pallas_call(outer_kernel, name='outer', out_shape=jax.ShapeDtypeStruct...  7.02 us
    pallas_call x1, Pallas kernels, scatter(): pl.pallas_call(scatter_kernel, name='scatter', out_shape=(jax.ShapeDtypeS...  6.88 us
  transfers between devices with their start and end apart: 8, of which 3 were waited for; matrix products, arithmetic and copies ran while one was open for 0% of the time, Pallas kernels for 36%

profile of v8, /device:TPU:1, one launch (start us, length us, event | category | flops | bytes accessed | tf_op | source)
XLA Modules:
  0.0 111.4 jit_solution(11696433031214939084)
XLA Ops:
  1.3 3.6 %pack.1 = (f32[128,128]{1,0:T(8,128)}, s32[16,128]{1,0:T(8,128)}, s32[16,128]{1,0:T(8,128)}, bf16[192,192]{1,0:T(8,128)(2,1)}) custom-call(s32[1]{0:T(128)S(6)} %copy.14.count, f32[16,128]{1,0:T(8,128)} %bitcast.20, s32[16,128]{1,0:T(8,128)} %bitcast.21, s32[16,128]{1,0:T(8,128)} %bitcast.22, f32[90,90]{1,0:T(8,128)} %vertical_far.1), custom_call_target="tpu_custom_call" | custom-call | flops 1000000000 | bytes 1000000 | tf_op jit(solution)/shard_map/pack/pallas_call | solution.py:114
  4.9 11.5 %all-to-all-start = ((f32[128,1,128]{2,1,0:T(1,128)}), f32[128,1,128]{2,1,0:T(1,128)S(1)}, u32[]{:S(2)}, u32[]{:S(2)}) async-start(f32[128,1,128]{2,1,0:T(1,128)} %bitcast.18), calls=%async_computation | async-start | bytes 131072 | tf_op jit(solution)/shard_map/all_to_all | solution.py:852
  16.4 11.7 %arrange.1 = (bf16[5,16,96,512]{3,2,1,0:T(8,128)(2,1)}, f32[5,3,96,512]{3,2,1,0:T(8,128)}, f32[5,3,96,512]{3,2,1,0:T(8,128)}, bf16[16,96,256]{2,1,0:T(8,128)(2,1...) custom-call(bf16[10,1440,256]{2,1,0:T(8,128)(2,1)} %bitcast.19), custom_call_target="tpu_custom_call" | custom-call | flops 10000000000 | bytes 25000000 | tf_op jit(solution)/shard_map/arrange/pallas_call | solution.py:270
  28.1 3.7 %collective-permute-start.4 = (f32[5,3,96,512]{3,2,1,0:T(8,128)}, f32[5,3,96,512]{3,2,1,0:T(8,128)S(1)}, u32[]{:S(2)}, u32[]{:S(2)}) collective-permute-start(f32[5,3,96,512]{3,2,1,0:T(8,128)} %get-tuple-element.60), channel_id=1, source_target_pairs={{0,16},{16,32},{32,48},{48,64},{64,80},{80,96},{96,112},{1,17},{17... | collective-permute-start | bytes 8847368 | tf_op jit(solution)/shard_map/ppermute | solution.py:833
  31.8 1.9 %collective-permute-start.5 = (f32[5,3,96,512]{3,2,1,0:T(8,128)}, f32[5,3,96,512]{3,2,1,0:T(8,128)}, u32[]{:S(2)}, u32[]{:S(2)}) collective-permute-start(f32[5,3,96,512]{3,2,1,0:T(8,128)} %get-tuple-element.61), channel_id=1, source_target_pairs={{16,0},{32,16},{48,32},{64,48},{80,64},{96,80},{112,96},{17,1},{33... | collective-permute-start | bytes 8847368 | tf_op jit(solution)/shard_map/ppermute | solution.py:838
  33.8 0.1 pad_add_fusion.refs_3_.place
  33.9 6.9 %scatter.1 = (f32[16,96,256]{2,1,0:T(8,128)S(1)}, f32[16,96,512]{2,1,0:T(8,128)S(1)}, f32[5,96,128]{2,1,0:T(8,128)}, f32[5,96,128]{2,1,0:T(8,128)}, f32[48,256]{...) custom-call(f32[128,128]{1,0:T(8,128)S(1)} %bitcast.16, ...), custom_call_target="tpu_custom_call", output_to_operand_aliasing={{2}: (1, {}), {3}: (2, {})} | custom-call | flops 10000000000 | bytes 2000000 | tf_op jit(solution)/shard_map/scatter/pallas_call | solution.py:392
  40.7 3.2 %collective-permute-start = (f32[5,96,128]{2,1,0:T(8,128)}, f32[5,96,128]{2,1,0:T(8,128)S(1)}, u32[]{:S(2)}, u32[]{:S(2)}) collective-permute-start(f32[5,96,128]{2,1,0:T(8,128)} %get-tuple-element.46), channel_id=1, source_target_pairs={{0,1},{1,2},{2,3},{3,4},{4,5},{5,6},{6,7},{7,8},{8,9},{9,10},{10,1... | collective-permute-start | bytes 737288 | tf_op jit(solution)/shard_map/ppermute | solution.py:833
  43.9 1.3 %collective-permute-start.1 = (f32[5,96,128]{2,1,0:T(8,128)}, f32[5,96,128]{2,1,0:T(8,128)S(1)}, u32[]{:S(2)}, u32[]{:S(2)}) collective-permute-start(f32[5,96,128]{2,1,0:T(8,128)} %get-tuple-element.47), channel_id=1, source_target_pairs={{1,0},{2,1},{3,2},{4,3},{5,4},{6,5},{7,6},{8,7},{9,8},{10,9},{11,1... | collective-permute-start | bytes 737288 | tf_op jit(solution)/shard_map/ppermute | solution.py:838
  45.2 0.0 copy-start
  45.3 6.9 %inner.2 = (f32[2,6,96,512]{3,2,1,0:T(8,128)S(1)}, f32[10,96,512]{2,1,0:T(8,128)S(1)}) custom-call(bf16[5,16,96,512]{3,2,1,0:T(8,128)(2,1)S(1)} %copy-done.1, f32[16,96,512]{2,1,0:T(8,128)S(1)} %get-tuple-element.49.refs_1_, bf16[192,192]{1,0:T(8,128)(2,1)S(1)} %copy-done.4, s32[4]{0:T(128)S(1)} %pad_add_fusion.refs_3_.place), custom_call_target="tpu_custom_call" | custom-call | flops 4000000000 | bytes 4000000 | tf_op jit(solution)/shard_map/inner/pallas_call | solution.py:581
  52.2 0.7 collective-permute-done.1.right
  52.9 2.1 %strips.1 = (bf16[16,96,256]{2,1,0:T(8,128)(2,1)S(1)}, f32[16,96,256]{2,1,0:T(8,128)S(1)}, f32[2,3,96,256]{3,2,1,0:T(8,128)S(1)}, f32[2,3,96,256]{3,2,1,0:T(8,128)S(1)}) custom-call(bf16[16,96,256]{2,1,0:T(8,128)(2,1)S(1)} %copy-done, f32[16,96,256]{2,1,0:T(8,128)S(1)} %get-tuple-element.45.adjoint, f32[5,96,128]{2,1,0:T(8,128)S(1)} %collective-permute-done.left, ...), custom_call_target="tpu_custom_call" | custom-call | flops 1000000000 | bytes 4000000 | tf_op jit(solution)/shard_map/strips/pallas_call | solution.py:457
  55.0 4.7 %collective-permute-start.2 = (f32[2,3,96,256]{3,2,1,0:T(8,128)S(1)}, f32[2,3,96,256]{3,2,1,0:T(8,128)S(1)}, u32[]{:S(2)}, u32[]{:S(2)}) collective-permute-start(f32[2,3,96,256]{3,2,1,0:T(8,128)S(1)} %get-tuple-element.56), channel_id=1, source_target_pairs={{0,16},{16,32},{32,48},{48,64},{64,80},{80,96},{96,112},{1,17},{17... | collective-permute-start | bytes 1769480 | tf_op jit(solution)/shard_map/ppermute | solution.py:833
  59.7 2.1 %collective-permute-start.3 = (f32[2,3,96,256]{3,2,1,0:T(8,128)S(1)}, f32[2,3,96,256]{3,2,1,0:T(8,128)S(1)}, u32[]{:S(2)}, u32[]{:S(2)}) collective-permute-start(f32[2,3,96,256]{3,2,1,0:T(8,128)S(1)} %get-tuple-element.57), channel_id=1, source_target_pairs={{16,0},{32,16},{48,32},{64,48},{80,64},{96,80},{112,96},{17,1},{33... | collective-permute-start | bytes 1769480 | tf_op jit(solution)/shard_map/ppermute | solution.py:838
  61.8 10.1 %inner.3 = (f32[3,6,96,512]{3,2,1,0:T(8,128)S(1)}, f32[10,96,512]{2,1,0:T(8,128)S(1)}) custom-call(bf16[5,16,96,512]{3,2,1,0:T(8,128)(2,1)S(1)} %copy-done.1, f32[16,96,512]{2,1,0:T(8,128)S(1)} %get-tuple-element.49.refs_1_, bf16[192,192]{1,0:T(8,128)(2,1)S(1)} %copy-done.4, s32[4]{0:T(128)S(1)} %pad_add_fusion.refs_3_.place, ...), custom_call_target="tpu_custom_call" | custom-call | flops 6000000000 | bytes 6000000 | tf_op jit(solution)/shard_map/inner/pallas_call | solution.py:581
  71.9 3.0 %collective-permute-done.3.adj_b.halo_b = f32[2,3,96,256]{3,2,1,0:T(8,128)S(1)} collective-permute-done((f32[2,3,96,256]{3,2,1,0:T(8,128)S(1)}, f32[2,3,96,256]{3,2,1,0:T(8,128)S(1)}, u32[]{:S(2)}, u32[]{:S(2)}) %collective-permute-start.3) | collective-permute-done | bytes 589856 | tf_op jit(solution)/shard_map/ppermute | solution.py:838
  74.9 7.0 %outer.1.border = f32[6,96,512]{2,1,0:T(8,128)S(1)} custom-call(bf16[5,16,96,512]{3,2,1,0:T(8,128)(2,1)S(1)} %copy-done.1, f32[5,3,96,512]{3,2,1,0:T(8,128)S(1)} %collective-permute-done.4.halo_t, f32[5,3,96,512]{3,2,1,0:T(8,128)} %collective-permute-done.5.halo_b, f32[2,3,96,256]{3,2,1,0:T(8,128)S(1)} %collective-permute-done.2.adj_t.halo_t, ...), custom_call_target="tpu_custom_call" | custom-call | flops 10000000000 | bytes 30000000 | tf_op jit(solution)/shard_map/outer/pallas_call | solution.py:665
  81.9 5.3 %edge.1.field = f32[16,96,256]{2,1,0:T(8,128)S(1)} custom-call(bf16[16,96,256]{2,1,0:T(8,128)(2,1)S(1)} %get-tuple-element.54.strip, f32[16,96,256]{2,1,0:T(8,128)S(1)} %get-tuple-element.55.adj, f32[2,3,96,256]{3,2,1,0:T(8,128)S(1)} %collective-permute-done.2.adj_t.halo_t, f32[2,3,96,256]{3,2,1,0:T(8,128)S(1)} %collective-permute-done.3.adj_b.halo_b, ...), custom_call_target="tpu_custom_call" | custom-call | flops 4000000000 | bytes 8000000 | tf_op jit(solution)/shard_map/edge/pallas_call | solution.py:742
  87.2 4.3 %gather.1 = f32[128,128]{1,0:T(8,128)} custom-call(f32[16,96,256]{2,1,0:T(8,128)S(1)} %edge.1.field, f32[48,256]{1,0:T(8,128)S(1)} %get-tuple-element.64.level, f32[48,256]{1,0:T(8,128)S(1)} %get-tuple-element.65.column, s32[24,256]{1,0:T(8,128)S(1)} %get-tuple-element.66.pos, s32[1,128]{1,0:T(1,128)S(1)} %get-tuple-element.67.rows_of), custom_call_target="tpu_custom_call" | custom-call | flops 10000000000 | bytes 2000000 | tf_op jit(solution)/shard_map/gather/pallas_call | solution.py:784
  91.5 9.2 %all-to-all-start.1 = ((f32[128,1,128]{2,1,0:T(1,128)}), f32[128,1,128]{2,1,0:T(1,128)S(1)}, u32[]{:S(2)}, u32[]{:S(2)}) async-start(f32[128,1,128]{2,1,0:T(1,128)} %bitcast.11), calls=%async_computation.1 | async-start | bytes 131072 | tf_op jit(solution)/shard_map/all_to_all | solution.py:871
  100.6 2.5 %restore.1 = f32[1440,256]{1,0:T(8,128)} custom-call(f32[16,96,256]{2,1,0:T(8,128)S(1)} %edge.1.field), custom_call_target="tpu_custom_call" | custom-call | flops 1000000000 | bytes 3000000 | tf_op jit(solution)/shard_map/restore/pallas_call | solution.py:819
  103.1 7.1 %all-to-all-done.1 = f32[128,1,128]{2,1,0:T(1,128)S(1)} async-done(((f32[128,1,128]{2,1,0:T(1,128)}), f32[128,1,128]{2,1,0:T(1,128)S(1)}, u32[]{:S(2)}, u32[]{:S(2)}) %all-to-all-start.1) | async-done | bytes 65568 | tf_op jit(solution)/shard_map/all_to_all | solution.py:871
  110.2 1.2 %unpack.1 = f32[16,128]{1,0:T(8,128)} custom-call(f32[128,128]{1,0:T(8,128)S(1)} %bitcast.17, s32[16,128]{1,0:T(8,128)S(1)} %copy-done.2, s32[16,128]{1,0:T(8,128)S(1)} %copy-done.3), custom_call_target="tpu_custom_call" | custom-call | flops 100000000 | bytes 100000 | tf_op jit(solution)/shard_map/unpack/pallas_call | solution.py:144
  (14 shorter events, 0.0 us)
Async XLA Ops:
  4.9 23.3 %all-to-all-start = ((f32[128,1,128]{2,1,0:T(1,128)}), f32[128,1,128]{2,1,0:T(1,128)S(1)}, u32[]{:S(2)}, u32[]{:S(2)}) async-start(f32[128,1,128]{2,1,0:T(1,128)} %bitcast.18), calls=%async_computation | async-start | bytes 131072 | tf_op jit(solution)/shard_map/all_to_all | solution.py:852
  28.1 46.7 %collective-permute-start.4 = (f32[5,3,96,512]{3,2,1,0:T(8,128)}, f32[5,3,96,512]{3,2,1,0:T(8,128)S(1)}, u32[]{:S(2)}, u32[]{:S(2)}) collective-permute-start(f32[5,3,96,512]{3,2,1,0:T(8,128)} %get-tuple-element.60), channel_id=1, source_target_pairs={{0,16},{16,32},{32,48},{48,64},{64,80},{80,96},{96,112},{1,17},{17... | collective-permute-start | bytes 8847368 | tf_op jit(solution)/shard_map/ppermute | solution.py:833
  31.8 43.0 %collective-permute-start.5 = (f32[5,3,96,512]{3,2,1,0:T(8,128)}, f32[5,3,96,512]{3,2,1,0:T(8,128)}, u32[]{:S(2)}, u32[]{:S(2)}) collective-permute-start(f32[5,3,96,512]{3,2,1,0:T(8,128)} %get-tuple-element.61), channel_id=1, source_target_pairs={{16,0},{32,16},{48,32},{64,48},{80,64},{96,80},{112,96},{17,1},{33... | collective-permute-start | bytes 8847368 | tf_op jit(solution)/shard_map/ppermute | solution.py:838
  33.8 11.4 %copy-start.1 = (bf16[5,16,96,512]{3,2,1,0:T(8,128)(2,1)S(1)}, bf16[5,16,96,512]{3,2,1,0:T(8,128)(2,1)}, u32[]{:S(2)}) copy-start(bf16[5,16,96,512]{3,2,1,0:T(8,128)(2,1)} %get-tuple-element.48.refs_0_.ens) | copy-start | bytes 23592964
  33.8 11.4 %copy-start.4 = (bf16[192,192]{1,0:T(8,128)(2,1)S(1)}, bf16[192,192]{1,0:T(8,128)(2,1)}, u32[]{:S(2)}) copy-start(bf16[192,192]{1,0:T(8,128)(2,1)} %get-tuple-element.50.refs_2_.weights) | copy-start | bytes 221188
  40.7 11.5 %collective-permute-start = (f32[5,96,128]{2,1,0:T(8,128)}, f32[5,96,128]{2,1,0:T(8,128)S(1)}, u32[]{:S(2)}, u32[]{:S(2)}) collective-permute-start(f32[5,96,128]{2,1,0:T(8,128)} %get-tuple-element.46), channel_id=1, source_target_pairs={{0,1},{1,2},{2,3},{3,4},{4,5},{5,6},{6,7},{7,8},{8,9},{9,10},{10,1... | collective-permute-start | bytes 737288 | tf_op jit(solution)/shard_map/ppermute | solution.py:833
  43.9 9.0 %collective-permute-start.1 = (f32[5,96,128]{2,1,0:T(8,128)}, f32[5,96,128]{2,1,0:T(8,128)S(1)}, u32[]{:S(2)}, u32[]{:S(2)}) collective-permute-start(f32[5,96,128]{2,1,0:T(8,128)} %get-tuple-element.47), channel_id=1, source_target_pairs={{1,0},{2,1},{3,2},{4,3},{5,4},{6,5},{7,6},{8,7},{9,8},{10,9},{11,1... | collective-permute-start | bytes 737288 | tf_op jit(solution)/shard_map/ppermute | solution.py:838
  45.2 7.6 %copy-start = (bf16[16,96,256]{2,1,0:T(8,128)(2,1)S(1)}, bf16[16,96,256]{2,1,0:T(8,128)(2,1)}, u32[]{:S(2)}) copy-start(bf16[16,96,256]{2,1,0:T(8,128)(2,1)} %get-tuple-element.38.strip) | copy-start | bytes 2359300
  55.0 16.9 %collective-permute-start.2 = (f32[2,3,96,256]{3,2,1,0:T(8,128)S(1)}, f32[2,3,96,256]{3,2,1,0:T(8,128)S(1)}, u32[]{:S(2)}, u32[]{:S(2)}) collective-permute-start(f32[2,3,96,256]{3,2,1,0:T(8,128)S(1)} %get-tuple-element.56), channel_id=1, source_target_pairs={{0,16},{16,32},{32,48},{48,64},{64,80},{80,96},{96,112},{1,17},{17... | collective-permute-start | bytes 1769480 | tf_op jit(solution)/shard_map/ppermute | solution.py:833
  59.7 15.1 %collective-permute-start.3 = (f32[2,3,96,256]{3,2,1,0:T(8,128)S(1)}, f32[2,3,96,256]{3,2,1,0:T(8,128)S(1)}, u32[]{:S(2)}, u32[]{:S(2)}) collective-permute-start(f32[2,3,96,256]{3,2,1,0:T(8,128)S(1)} %get-tuple-element.57), channel_id=1, source_target_pairs={{16,0},{32,16},{48,32},{64,48},{80,64},{96,80},{112,96},{17,1},{33... | collective-permute-start | bytes 1769480 | tf_op jit(solution)/shard_map/ppermute | solution.py:838
  91.5 18.8 %copy-start.2 = (s32[16,128]{1,0:T(8,128)S(1)}, s32[16,128]{1,0:T(8,128)}, u32[]{:S(2)}) copy-start(s32[16,128]{1,0:T(8,128)} %get-tuple-element.68.tgt) | copy-start | bytes 24580
  91.5 18.8 %copy-start.3 = (s32[16,128]{1,0:T(8,128)S(1)}, s32[16,128]{1,0:T(8,128)}, u32[]{:S(2)}) copy-start(s32[16,128]{1,0:T(8,128)} %get-tuple-element.69.rank) | copy-start | bytes 24580
  91.5 18.7 %all-to-all-start.1 = ((f32[128,1,128]{2,1,0:T(1,128)}), f32[128,1,128]{2,1,0:T(1,128)S(1)}, u32[]{:S(2)}, u32[]{:S(2)}) async-start(f32[128,1,128]{2,1,0:T(1,128)} %bitcast.11), calls=%async_computation.1 | async-start | bytes 131072 | tf_op jit(solution)/shard_map/all_to_all | solution.py:871
